TPU v7x, 32 devices: a whole 2x2x4 slice. The times are simulated.
32 devices in a mesh: dp: 4 (over y, core), expert: 8 (over z, x).
Axes of the slice: x: 2, y: 2, z: 4, core: 2. Of those that a mesh axis runs over, the one named last changes fastest.
Arguments:
- tokens: bfloat16 [4096, 4096], P(('dp', 'expert')), may hold values from -6 to 6
- out_grad: bfloat16 [4096, 4096], P(('dp', 'expert')), may hold values from -0.29882812 to 0.29882812
- probs: bfloat16 [4096, 8], P(('dp', 'expert')), may hold values from 0.049804688 to 0.5
- routes: int32 [4096, 8], P(('dp', 'expert')), may hold values from 0 to 31, as said below
- saved_gate: bfloat16 [16384, 768], P(('dp', 'expert')), may hold values from -6 to 6
- saved_up: bfloat16 [16384, 768], P(('dp', 'expert')), may hold values from -6 to 6
- down_weight: bfloat16 [8, 768, 4096], P('expert'), may hold values from -0.21875 to 0.21875
Outputs:
- grad_down: float32 [8, 768, 4096], P('expert', 'dp')
- grad_up: bfloat16 [8, 4096, 768], P('expert', 'dp')
- prob_grad: float32 [4096, 8], P(('dp', 'expert'))
Inputs may be any that keep to these rules, and one draw needn't show every extreme that they name: `routes`: each row names 8 different experts. In every aligned block of 128 rows at least half of the rows name one common expert whose number is a multiple of 4; which one is drawn from the seed.
All inputs are finite; a program needn't handle non-finite values.
Results may differ from a plain program's by a relative error of at most 0.014.
Values may be sent and summed in bfloat16 or wider, within the bound.
No kernel may reach another device: no remote copies, remote signals or barrier semaphores. Data moves between devices by JAX's collectives and lax.ppermute only.
A program may use at most 192 MiB of HBM per device.

v0:
```python
import jax
import jax.numpy as jnp
from jax import lax
from jax.sharding import PartitionSpec as P

EXP_DEV = 4


def per_device(tokens, out_grad, probs, routes, saved_gate, saved_up, down_weight):
    owners = lax.axis_size("expert")
    groups = lax.axis_size("dp")
    tok_count = tokens.shape[0]
    model_width = tokens.shape[1]
    slot_rows = saved_gate.shape[0]
    capacity = slot_rows // owners
    hidden_width = saved_gate.shape[1]
    in_window = routes % EXP_DEV == 0
    target = routes // EXP_DEV
    owner_ids = jnp.arange(owners, dtype=jnp.int32)
    routed = jnp.sum(
        ((target[:, :, None] == owner_ids[None, None, :]) & in_window[:, :, None]).astype(
            jnp.int32
        ),
        axis=1,
    )
    before = jnp.cumsum(routed, axis=0) - routed
    position = jnp.take_along_axis(before, target, axis=1)
    retained = in_window & (position < capacity)
    slot_index = jnp.where(retained, target * capacity + position, slot_rows)
    flat_index = slot_index.reshape(-1)
    token_ids = jnp.broadcast_to(jnp.arange(tok_count, dtype=jnp.int32)[:, None], routes.shape)
    holders = (
        jnp.full((slot_rows,), -1, jnp.int32).at[flat_index].set(token_ids.reshape(-1), mode="drop")
    )
    weight_slot = (
        jnp.zeros((slot_rows,), jnp.bfloat16).at[flat_index].set(probs.reshape(-1), mode="drop")
    )
    filled = holders >= 0
    safe_rows = jnp.maximum(holders, 0)
    send_x = jnp.where(filled[:, None], tokens[safe_rows], jnp.zeros((), jnp.bfloat16)).reshape(
        owners, capacity, model_width
    )
    send_dy = jnp.where(filled[:, None], out_grad[safe_rows], jnp.zeros((), jnp.bfloat16)).reshape(
        owners, capacity, model_width
    )
    send_weight = weight_slot.reshape(owners, capacity)
    recv_x, recv_dy, recv_weight = (
        lax.all_to_all(send_x, "expert", split_axis=0, concat_axis=0, tiled=True),
        lax.all_to_all(send_dy, "expert", split_axis=0, concat_axis=0, tiled=True),
        lax.all_to_all(send_weight, "expert", split_axis=0, concat_axis=0, tiled=True),
    )
    recv_x = recv_x.reshape(slot_rows, model_width)
    recv_dy = recv_dy.reshape(slot_rows, model_width)
    weights = recv_weight.reshape(slot_rows).astype(jnp.float32)
    gate_act = jax.nn.silu(saved_gate.astype(jnp.float32))
    hidden = (gate_act * saved_up.astype(jnp.float32)).astype(jnp.bfloat16)
    matrix = down_weight[0]
    back_grad = lax.dot_general(
        recv_dy, matrix, (((1,), (1,)), ((), ())), preferred_element_type=jnp.float32
    )
    projected = jnp.dot(hidden, matrix, preferred_element_type=jnp.float32)
    slot_grad = jnp.sum(recv_dy.astype(jnp.float32) * projected, axis=1)
    returned = lax.all_to_all(
        slot_grad.reshape(owners, capacity), "expert", split_axis=0, concat_axis=0, tiled=True
    )
    gathered_grad = returned.reshape(-1)[jnp.minimum(slot_index, slot_rows - 1)]
    prob_grad = jnp.where(retained, gathered_grad, jnp.zeros((), jnp.float32))
    scaled = (weights[:, None] * recv_dy.astype(jnp.float32)).astype(jnp.bfloat16)
    grad_pre = (weights[:, None] * back_grad * gate_act).astype(jnp.bfloat16)
    column_block = hidden
    down_share = lax.psum_scatter(
        lax.dot_general(
            column_block, scaled, (((0,), (0,)), ((), ())), preferred_element_type=jnp.float32
        ),
        "dp",
        scatter_dimension=0,
        tiled=True,
    )
    column_block = recv_x
    product = lax.dot_general(
        column_block, grad_pre, (((0,), (0,)), ((), ())), preferred_element_type=jnp.float32
    )
    up_share = lax.psum_scatter(
        lax.optimization_barrier(product.astype(jnp.bfloat16))
        .astype(jnp.float32)
        .astype(jnp.bfloat16),
        "dp",
        scatter_dimension=0,
        tiled=True,
    )
    return (
        down_share.reshape(1, hidden_width // groups, model_width),
        up_share.reshape(1, model_width // groups, hidden_width),
        prob_grad,
    )


def solution(mesh):
    in_specs = (
        P(("dp", "expert"), None),
        P(("dp", "expert"), None),
        P(("dp", "expert"), None),
        P(("dp", "expert"), None),
        P(("dp", "expert"), None),
        P(("dp", "expert"), None),
        P("expert", None, None),
    )
    out_specs = (P("expert", "dp", None), P("expert", "dp", None), P(("dp", "expert"), None))
    return jax.shard_map(
        per_device, mesh=mesh, in_specs=in_specs, out_specs=out_specs, check_vma=False
    )
```

profile of v0, /device:TPU:0, one launch (start us, length us, event | category | flops | bytes accessed | tf_op | source)
XLA Modules:
  0.0 422.5 jit_solution(4936992754845990598)
XLA Ops:
  7.2 0.0 copy-start
  7.2 0.9 copy.25
  8.1 0.1 bitcast_or_fusion
  8.2 0.8 copy.33
  9.0 0.1 reshape.145
  9.1 0.1 copy.30
  9.1 0.1 reshape.135
  9.3 0.1 copy.31
  9.4 0.2 reduce_window_sum.11
  9.6 7.1 %gather_fusion.3 = s32[1024]{0:T(1024)S(1)} fusion(s32[128,8]{1,0:T(8,128)S(1)} %sub.10, s32[1024]{0:T(1024)S(1)} %reshape.135), kind=kCustom, calls=%fused_computation.3 | custom fusion | bytes 16384 | tf_op jit(solution)/shard_map/jit(take_along_axis)/gather | solution.py:27
  16.7 0.1 reshape.138
  16.8 0.1 compare_select_fusion
  16.9 0.1 reshape.102
  17.0 7.6 %scatter_custom_fusion = bf16[512]{0:T(512)(128)(2,1)S(1)} fusion(s32[1024]{0:T(1024)S(1)} %bitcast.28, bf16[1024]{0:T(1024)(128)(2,1)S(1)} %reshape.145, bf16[]{:T(256)} %constant.39.clone.1), kind=kCustom, calls=%fused_computation.52 | custom fusion | bytes 1026 | tf_op jit(solution)/shard_map/scatter | solution.py:36
  24.6 0.7 all_to_all.24
  25.2 7.3 %all-to-all-start = ((bf16[8,1,64]{2,1,0:T(2,128)(2,1)}), bf16[8,1,64]{2,1,0:T(2,128)(2,1)S(1)}, u32[]{:S(2)}, u32[]{:S(2)}) async-start(bf16[8,1,64]{2,1,0:T(2,128)(2,1)} %all_to_all.24), calls=%async_computation | async-start | bytes 8192 | tf_op jit(solution)/shard_map/all_to_all | solution.py:50
  32.5 0.1 reshape.153
  32.6 4.3 %scatter_custom_fusion.1 = s32[512]{0:T(512)S(1)} fusion(s32[1024]{0:T(1024)S(1)} %bitcast.29, s32[1024]{0:T(1024)S(1)} %reshape.153, s32[]{:T(128)} %constant.61.clone.1), kind=kCustom, calls=%fused_computation.50 | custom fusion | bytes 2052 | tf_op jit(solution)/shard_map/scatter | solution.py:33
  36.9 0.1 broadcast_in_dim.63
  37.0 0.0 copy-done
  37.0 0.0 copy-start.1
  37.0 4.4 %gather_fusion.1 = bf16[512,4096]{1,0:T(8,128)(2,1)} fusion(bf16[128,4096]{1,0:T(8,128)(2,1)S(1)} %copy-done, s32[1024]{0:T(1024)S(1)} %pad_clamp_fusion), kind=kCustom, calls=%fused_computation.1 | custom fusion | bytes 8390656 | tf_op jit(solution)/shard_map/gather | solution.py:40
  41.4 0.0 copy-done.1
  41.4 4.4 %gather_fusion = bf16[512,4096]{1,0:T(8,128)(2,1)} fusion(bf16[128,4096]{1,0:T(8,128)(2,1)S(1)} %copy-done.1, s32[1024]{0:T(1024)S(1)} %pad_clamp_fusion), kind=kCustom, calls=%fused_computation | custom fusion | bytes 8390656 | tf_op jit(solution)/shard_map/gather | solution.py:43
  45.8 5.8 %broadcast_select_fusion = (bf16[8,64,4096]{2,1,0:T(8,128)(2,1)}, bf16[8,64,4096]{2,1,0:T(8,128)(2,1)}) fusion(bf16[8,64,4096]{2,1,0:T(8,128)(2,1)} %bitcast.26, pred[8,64]{1,0:T(8,128)(4,1)S(1)} %broadcast_in_dim.63, bf16[8,64,4096]{2,1,0:T(8,128)(2,1)} %bitcast.27), kind=kLoop, calls=%fused_computation.16 | loop fusion | flops 4194304 | bytes 16777728 | tf_op jit(solution)/shard_map/jit(_where)/select_n | solution.py:40
  51.6 0.0 all-to-all-done
  51.6 98.9 %all_to_all.29 = bf16[8,64,4096]{2,1,0:T(8,128)(2,1)} all-to-all(bf16[8,64,4096]{2,1,0:T(8,128)(2,1)} %get-tuple-element.17), channel_id=1, replica_groups=mesh['dp'=4,'expert'=8] {'expert'}, dimensions={0} | all-to-all | bytes 8388608 | tf_op jit(solution)/shard_map/all_to_all | solution.py:49
  150.5 0.0 copy-start.2
  150.5 4.7 %all-to-all-start.2 = ((bf16[8,64,4096]{2,1,0:T(8,128)(2,1)}), bf16[8,64,4096]{2,1,0:T(8,128)(2,1)}, u32[]{:S(2)}, u32[]{:S(2)}) async-start(bf16[8,64,4096]{2,1,0:T(8,128)(2,1)} %get-tuple-element.16), calls=%async_computation.3 | async-start | bytes 8388608 | tf_op jit(solution)/shard_map/all_to_all | solution.py:48
  155.2 0.2 reduce-scatter.5.cloned.1.call-start
  155.5 0.1 reshape.110
  155.5 0.0 copy-done.2
  155.5 7.7 %multiply_convert_fusion = bf16[512,768]{1,0:T(8,128)(2,1)S(1)} fusion(bf16[512,4096]{1,0:T(8,128)(2,1)} %bitcast.23, bf16[1,768,4096]{2,1,0:T(8,128)(2,1)} %param.13, f32[512]{0:T(512)S(1)} %reshape.110, bf16[512,768]{1,0:T(8,128)(2,1)S(1)} %copy-done.2), kind=kOutput, calls=%fused_computation.23 | convolution fusion | flops 3224371200 | bytes 12060672 | tf_op jit(solution)/shard_map/dot_general | solution.py:58
  163.2 84.1 %all-to-all-done.2 = bf16[8,64,4096]{2,1,0:T(8,128)(2,1)} async-done(((bf16[8,64,4096]{2,1,0:T(8,128)(2,1)}), bf16[8,64,4096]{2,1,0:T(8,128)(2,1)}, u32[]{:S(2)}, u32[]{:S(2)}) %all-to-all-start.2) | async-done | bytes 4194336 | tf_op jit(solution)/shard_map/all_to_all | solution.py:48
  247.3 8.3 %convolution_convert_fusion = bf16[4096,768]{1,0:T(8,128)(2,1)} fusion(bf16[512,4096]{1,0:T(8,128)(2,1)} %bitcast.6, bf16[512,768]{1,0:T(8,128)(2,1)S(1)} %multiply_convert_fusion), kind=kOutput, calls=%fused_computation.10 | convolution fusion | flops 3224371200 | bytes 11272192 | tf_op jit(solution)/shard_map/dot_general | solution.py:80
  255.6 0.0 copy-start.3
  255.6 0.0 reduce-scatter.5.cloned.1.call-update
  255.6 0.0 reduce-scatter.3.cloned.1.call-start
  255.7 1.1 copy-done.3
  256.7 10.1 %fusion.5 = f32[768,4096]{1,0:T(8,128)} fusion(bf16[512,4096]{1,0:T(8,128)(2,1)} %bitcast.24, f32[512]{0:T(512)S(1)} %reshape.110, bf16[512,768]{1,0:T(8,128)(2,1)S(1)} %copy-done.3, bf16[512,768]{1,0:T(8,128)(2,1)S(1)} %copy-done.2), kind=kOutput, calls=%fused_computation.14 | convolution fusion | flops 3230662656 | bytes 18352128 | tf_op jit(solution)/shard_map/dot_general | solution.py:72
  266.9 0.0 reduce-scatter.3.cloned.1.call-update
  266.9 0.1 reshape.129
  267.0 7.6 %fusion.1 = f32[512]{0:T(512)S(1)} fusion(bf16[512,4096]{1,0:T(8,128)(2,1)} %bitcast.25, bf16[1,768,4096]{2,1,0:T(8,128)(2,1)} %param.13, bf16[512,768]{1,0:T(8,128)(2,1)S(1)} %copy-done.3, bf16[512,768]{1,0:T(8,128)(2,1)S(1)} %copy-done.2), kind=kOutput, calls=%fused_computation.9 | convolution fusion | flops 3230662144 | bytes 12060672 | tf_op jit(solution)/shard_map/dot_general | solution.py:61
  274.6 0.7 all_to_all.22
  275.3 4.6 %all-to-all-start.3 = ((f32[8,1,64]{2,1,0:T(1,128)}), f32[8,1,64]{2,1,0:T(1,128)S(1)}, u32[]{:S(2)}, u32[]{:S(2)}) async-start(f32[8,1,64]{2,1,0:T(1,128)} %all_to_all.22), calls=%async_computation.5 | async-start | bytes 8192 | tf_op jit(solution)/shard_map/all_to_all | solution.py:63
  279.9 6.4 %all-to-all-done.3 = f32[8,1,64]{2,1,0:T(1,128)S(1)} async-done(((f32[8,1,64]{2,1,0:T(1,128)}), f32[8,1,64]{2,1,0:T(1,128)S(1)}, u32[]{:S(2)}, u32[]{:S(2)}) %all-to-all-start.3) | async-done | bytes 2080 | tf_op jit(solution)/shard_map/all_to_all | solution.py:63
  286.3 0.5 broadcast.114
  286.8 0.7 reduce.7
  287.5 0.1 reshape.109
  287.6 6.9 %gather_fusion.2 = f32[1024]{0:T(1024)S(1)} fusion(f32[512]{0:T(512)S(1)} %reshape.109, s32[1024]{0:T(1024)S(1)} %broadcast_clamp_fusion), kind=kCustom, calls=%fused_computation.2 | custom fusion | bytes 12288 | tf_op jit(solution)/shard_map/gather | solution.py:66
  294.4 0.1 reshape.128
  294.5 0.1 broadcast_select_fusion.2
  294.6 0.7 copy.35
  295.2 18.0 %reduce-scatter.5.cloned.1.call-done = bf16[1024,768]{1,0:T(8,128)(2,1)} async-done(((bf16[4096,768]{1,0:T(8,128)(2,1)}), bf16[1024,768]{1,0:T(8,128)(2,1)}) %reduce-scatter.5.cloned.1.call-update) | async-done | bytes 1572880 | tf_op jit(solution)/shard_map/reduce_scatter | solution.py:83
  313.2 102.4 %reduce-scatter.3.cloned.1.call-done = f32[192,4096]{1,0:T(8,128)} async-done(((f32[768,4096]{1,0:T(8,128)}), f32[192,4096]{1,0:T(8,128)}) %reduce-scatter.3.cloned.1.call-update) | async-done | bytes 3145744 | tf_op jit(solution)/shard_map/reduce_scatter | solution.py:71
  (11 shorter events, 0.2 us)
Async XLA Ops:
  7.2 29.9 %copy-start = (bf16[128,4096]{1,0:T(8,128)(2,1)S(1)}, bf16[128,4096]{1,0:T(8,128)(2,1)}, u32[]{:S(2)}) copy-start(bf16[128,4096]{1,0:T(8,128)(2,1)} %param.7) | copy-start | bytes 3145732
  25.2 26.3 %all-to-all-start = ((bf16[8,1,64]{2,1,0:T(2,128)(2,1)}), bf16[8,1,64]{2,1,0:T(2,128)(2,1)S(1)}, u32[]{:S(2)}, u32[]{:S(2)}) async-start(bf16[8,1,64]{2,1,0:T(2,128)(2,1)} %all_to_all.24), calls=%async_computation | async-start | bytes 8192 | tf_op jit(solution)/shard_map/all_to_all | solution.py:50
  37.0 4.4 %copy-start.1 = (bf16[128,4096]{1,0:T(8,128)(2,1)S(1)}, bf16[128,4096]{1,0:T(8,128)(2,1)}, u32[]{:S(2)}) copy-start(bf16[128,4096]{1,0:T(8,128)(2,1)} %param.8) | copy-start | bytes 3145732
  150.5 5.0 %copy-start.2 = (bf16[512,768]{1,0:T(8,128)(2,1)S(1)}, bf16[512,768]{1,0:T(8,128)(2,1)}, u32[]{:S(2)}) copy-start(bf16[512,768]{1,0:T(8,128)(2,1)} %param.11) | copy-start | bytes 2359300
  150.5 96.8 %all-to-all-start.2 = ((bf16[8,64,4096]{2,1,0:T(8,128)(2,1)}), bf16[8,64,4096]{2,1,0:T(8,128)(2,1)}, u32[]{:S(2)}, u32[]{:S(2)}) async-start(bf16[8,64,4096]{2,1,0:T(8,128)(2,1)} %get-tuple-element.16), calls=%async_computation.3 | async-start | bytes 8388608 | tf_op jit(solution)/shard_map/all_to_all | solution.py:48
  155.2 158.0 %reduce-scatter.5.cloned.1.call-start = ((), (), s32[]{:S(2)}) async-start(), calls=%async_computation.7 | async-start | bytes 7864320 | tf_op jit(solution)/shard_map/reduce_scatter | solution.py:83
  255.6 1.1 copy-start.3
  255.6 160.1 %reduce-scatter.3.cloned.1.call-start = ((), (), s32[]{:S(2)}) async-start(), calls=%async_computation.6 | async-start | bytes 15728640 | tf_op jit(solution)/shard_map/reduce_scatter | solution.py:71
  275.3 11.0 %all-to-all-start.3 = ((f32[8,1,64]{2,1,0:T(1,128)}), f32[8,1,64]{2,1,0:T(1,128)S(1)}, u32[]{:S(2)}, u32[]{:S(2)}) async-start(f32[8,1,64]{2,1,0:T(1,128)} %all_to_all.22), calls=%async_computation.5 | async-start | bytes 8192 | tf_op jit(solution)/shard_map/all_to_all | solution.py:63
Sparse Core Ops, SparseCore 0:
  255.8 57.4 reduce-scatter.4
  316.6 99.0 reduce-scatter.2
where the time goes:
time: 423 us
  waiting for transfers between devices  211 us (50%)
  blocking collectives  98.9 us (23%)
  local copies, waits for them, and re-layouts  40.9 us (10%)
  matrix products  33.7 us (8%)
  starting transfers between devices  16.8 us (4%)
  between operations  14.2 us (3%)
  other arithmetic  6.94 us (2%)
    reduce_scatter x1, waiting for transfers between devices, per_device(): lax.psum_scatter(lax.dot_general(column_block, scaled, (((0,), (0,)), (()...  102 us
    all_to_all x1, blocking collectives, per_device(): lax.all_to_all(send_dy, 'expert', split_axis=0, concat_axis=0, tiled=True)  98.9 us
    all_to_all x1, waiting for transfers between devices, per_device(): lax.all_to_all(send_x, 'expert', split_axis=0, concat_axis=0, tiled=True)  84.1 us
    reduce_scatter x1, waiting for transfers between devices, per_device(): lax.psum_scatter(lax.optimization_barrier(product.astype(jnp.bfloat16)).a...  18 us
    dot_general x1, matrix products, per_device(): lax.dot_general(column_block, scaled, (((0,), (0,)), ((), ())), preferred...  10.1 us
  transfers between devices with their start and end apart: 5, of which 4 were waited for; matrix products, arithmetic and copies ran while one was open for 13% of the time, Pallas kernels for 0%

commit v1 on v0

v1 whole, which is shorter than its diff:
```python
import functools

import jax
import jax.numpy as jnp
from jax import lax
from jax.experimental import pallas as pl
from jax.experimental.pallas import tpu as pltpu
from jax.sharding import PartitionSpec as P

EXP_DEV = 4
X_PARTS = 2
X_CHUNKS = 2
COLUMNS = 512
VMEM = 48 * 1024 * 1024


COST = 0.0


def cost(flops, size):
    return pl.CostEstimate(
        flops=int(COST * flops), bytes_accessed=int(COST * size), transcendentals=0
    )


def after(value, *deps):
    return lax.optimization_barrier((value, *deps))[0]


def swap(value, axis, bit):
    size = lax.axis_size(axis)
    return lax.ppermute(value, axis, [(i, i ^ bit) for i in range(size)])


def exchange(table, axis):
    count = table.shape[0]
    bit = 1
    while bit < count:
        split = table.reshape(count // (2 * bit), 2, bit, table.shape[1])
        moved = swap(split[:, 1], axis, bit)
        table = jnp.stack([split[:, 0], moved], axis=1).reshape(table.shape)
        bit *= 2
    return table


def scatter_sum(kept, sent, axis):
    bit = 1
    while True:
        got = swap(sent, axis, bit)
        blocks = [kept[i] + got[i].astype(jnp.float32) for i in range(len(kept))]
        if len(blocks) == 1:
            return blocks[0]
        kept = blocks[0::2]
        sent = jnp.stack(blocks[1::2]).astype(jnp.bfloat16)
        bit *= 2


def slot_positions(table, capacity):
    tokens = table.shape[1]
    routed = table > 0
    earlier = (
        lax.broadcasted_iota(jnp.int32, (tokens, tokens), 0)
        < lax.broadcasted_iota(jnp.int32, (tokens, tokens), 1)
    )
    before = jnp.dot(
        jnp.where(routed, 1.0, 0.0).astype(jnp.bfloat16),
        jnp.where(earlier, 1.0, 0.0).astype(jnp.bfloat16),
        preferred_element_type=jnp.float32,
    ).astype(jnp.int32)
    return jnp.where(routed & (before < capacity), before, -1)


def place_kernel(parts, scaled, half, capacity, where, *refs):
    sources = 1 + max(source for part in parts for source, _, _ in part)
    tables, rows = refs[:sources], refs[sources : 2 * sources]
    outs = refs[2 * sources : 2 * sources + half]
    choices = refs[2 * sources + half :]
    step = pl.program_id(0)

    @pl.when(step == 0)
    def _():
        tokens = rows[0].shape[0]
        slot = lax.broadcasted_iota(jnp.int32, (capacity, tokens), 0)
        for s in range(sources):
            table = tables[s][...]
            position = slot_positions(table, capacity)
            value = table if scaled else jnp.where(table > 0, 1.0, 0.0)
            owner = lax.broadcasted_iota(jnp.int32, table.shape, 0)
            for k in range(half):
                mine = owner == (where[0] ^ k)
                wanted = jnp.sum(jnp.where(mine, position, 0), axis=0, keepdims=True)
                entry = jnp.sum(jnp.where(mine, value, 0.0), axis=0, keepdims=True)
                choices[s][k * capacity : (k + 1) * capacity, :] = jnp.where(
                    slot == wanted, entry, 0.0
                ).astype(jnp.bfloat16)

    for p, part in enumerate(parts):
        for source, start, end in part:

            @pl.when((step >= start) & (step < end))
            def _():
                placed = jnp.dot(
                    choices[source][...], rows[source][...], preferred_element_type=jnp.float32
                ).astype(jnp.bfloat16)
                for k in range(half):
                    outs[k][p * capacity : (p + 1) * capacity, :] = placed[
                        k * capacity : (k + 1) * capacity, :
                    ]


def place(where, tables, rows, maps, parts, steps, width, half, capacity, scaled):
    owners, tokens = tables[0].shape
    sources = len(tables)
    out_shape = (len(parts) * capacity, steps * width)
    return pl.pallas_call(
        functools.partial(place_kernel, parts, scaled, half, capacity),
        grid_spec=pltpu.PrefetchScalarGridSpec(
            num_scalar_prefetch=1,
            grid=(steps,),
            in_specs=[pl.BlockSpec((owners, tokens), lambda i, w: (0, 0))] * sources
            + [
                pl.BlockSpec((tokens, width), functools.partial(lambda m, i, w: (0, m(i, w)), m))
                for m in maps
            ],
            out_specs=[pl.BlockSpec((out_shape[0], width), lambda i, w: (0, i))] * half,
            scratch_shapes=[pltpu.VMEM((half * capacity, tokens), jnp.bfloat16)] * sources,
        ),
        out_shape=[jax.ShapeDtypeStruct(out_shape, jnp.bfloat16)] * half,
        compiler_params=pltpu.CompilerParams(vmem_limit_bytes=VMEM),
        cost_estimate=cost(
            2 * half * out_shape[0] * out_shape[1] * tokens,
            2 * (half * out_shape[0] + sources * tokens) * out_shape[1],
        ),
        name="place",
    )(where, *tables, *rows)


def down_kernel(pieces, first, weighted, matrix, *refs):
    dy = jnp.concatenate([ref[...] for ref in refs[:pieces]], axis=0)
    rest = refs[pieces:]
    back, kept, sent = rest[-3:]

    @pl.when(pl.program_id(0) == 0)
    def _():
        back[...] = jnp.zeros_like(back) if first else rest[0][...]

    back[...] += lax.dot_general(
        dy, matrix[...], (((1,), (1,)), ((), ())), preferred_element_type=jnp.float32
    )
    middle = kept.shape[0]
    kept[...] = jnp.dot(weighted[:middle, :], dy, preferred_element_type=jnp.float32)
    sent[...] = jnp.dot(weighted[middle:, :], dy, preferred_element_type=jnp.float32).astype(
        jnp.bfloat16
    )


def down_step(weighted, matrix, pieces, starts, capacity, back, start, width):
    hidden_width, slots = weighted.shape
    steps = width // COLUMNS
    offset = start // COLUMNS
    first = back is None
    constant = lambda i: (0, 0)
    column = lambda i: (0, i)
    middle = hidden_width // 2
    return pl.pallas_call(
        functools.partial(down_kernel, len(pieces), first),
        grid=(steps,),
        in_specs=[
            pl.BlockSpec((hidden_width, slots), constant),
            pl.BlockSpec((hidden_width, COLUMNS), lambda i: (0, i + offset)),
        ]
        + [
            pl.BlockSpec((capacity, COLUMNS), functools.partial(lambda o, i: (0, i + o), o // COLUMNS))
            for o in starts
        ]
        + ([] if first else [pl.BlockSpec((slots, hidden_width), constant)]),
        out_specs=[
            pl.BlockSpec((slots, hidden_width), constant),
            pl.BlockSpec((middle, COLUMNS), column),
            pl.BlockSpec((middle, COLUMNS), column),
        ],
        out_shape=[
            jax.ShapeDtypeStruct((slots, hidden_width), jnp.float32),
            jax.ShapeDtypeStruct((middle, width), jnp.float32),
            jax.ShapeDtypeStruct((middle, width), jnp.bfloat16),
        ],
        compiler_params=pltpu.CompilerParams(vmem_limit_bytes=VMEM),
        cost_estimate=cost(4 * slots * hidden_width * width, 2 * width * (slots + hidden_width) + 3 * width * hidden_width),
        name="down_step",
    )(weighted, matrix, *pieces, *([] if first else [back]))


def up_kernel(half, capacity, grad_pre, *refs):
    pieces = refs[:half]
    kept, sent = refs[half:]
    x = jnp.concatenate(
        [ref[:capacity, :] for ref in pieces] + [ref[capacity:, :] for ref in pieces], axis=0
    )
    width = kept.shape[0]
    contract = (((0,), (0,)), ((), ()))
    kept[...] = lax.dot_general(
        x[:, :width], grad_pre[...], contract, preferred_element_type=jnp.float32
    )
    sent[...] = lax.dot_general(
        x[:, width:], grad_pre[...], contract, preferred_element_type=jnp.float32
    ).astype(jnp.bfloat16)


def up_step(grad_pre, pieces, groups, capacity):
    slots, hidden_width = grad_pre.shape
    columns = pieces[0].shape[1]
    width = columns // groups
    pairs = groups // 2
    rows = pairs * width
    out = pl.BlockSpec((width, hidden_width), lambda i: (i, 0))
    return pl.pallas_call(
        functools.partial(up_kernel, len(pieces), capacity),
        grid=(pairs,),
        in_specs=[pl.BlockSpec((slots, hidden_width), lambda i: (0, 0))]
        + [pl.BlockSpec((piece.shape[0], 2 * width), lambda i: (0, i)) for piece in pieces],
        out_specs=[out, out],
        out_shape=[
            jax.ShapeDtypeStruct((rows, hidden_width), jnp.float32),
            jax.ShapeDtypeStruct((rows, hidden_width), jnp.bfloat16),
        ],
        compiler_params=pltpu.CompilerParams(vmem_limit_bytes=VMEM),
        cost_estimate=cost(2 * slots * hidden_width * columns, 2 * columns * slots + 3 * columns * hidden_width),
        name="up_step",
    )(grad_pre, *pieces)


def pick(table, index):
    return lax.dynamic_index_in_dim(table, index, 0, keepdims=False)


def per_device(tokens, out_grad, probs, routes, saved_gate, saved_up, down_weight):
    owners = lax.axis_size("expert")
    groups = lax.axis_size("dp")
    me = lax.axis_index("expert")
    group = lax.axis_index("dp")
    where = jnp.stack([me, group]).astype(jnp.int32)
    half = owners // 2
    tok_count, model_width = tokens.shape
    slot_rows, hidden_width = saved_gate.shape
    capacity = slot_rows // owners
    cuts = [0, model_width // 4, model_width]
    spans = list(zip(cuts[:-1], cuts[1:]))

    dy_far = []
    for lo, hi in spans:
        rows = out_grad[:, lo:hi]
        dy_far.append(swap(after(rows, dy_far[-1]) if dy_far else rows, "expert", half))

    owner_ids = jnp.arange(owners, dtype=jnp.int32) * EXP_DEV
    named = routes.T[None, :, :] == owner_ids[:, None, None]
    table_own = jnp.sum(jnp.where(named, probs.T[None, :, :].astype(jnp.float32), 0.0), axis=1)
    table_far = swap(table_own, "expert", half)

    order = me ^ jnp.arange(owners, dtype=jnp.int32)
    gate = saved_gate.reshape(owners, capacity, hidden_width)[order]
    up = saved_up.reshape(owners, capacity, hidden_width)[order]
    gate_act = jax.nn.silu(gate.reshape(slot_rows, hidden_width).astype(jnp.float32))
    hidden = (gate_act * up.reshape(slot_rows, hidden_width).astype(jnp.float32)).astype(
        jnp.bfloat16
    )
    block = hidden_width // groups
    hidden_t = hidden.T.reshape(groups, block, slot_rows)
    turns = list(range(0, groups, 2)) + list(range(1, groups, 2))
    hidden_t = jnp.concatenate([pick(hidden_t, group ^ r) for r in turns], axis=0)
    matrix = down_weight[0]

    def spread(sent):
        return [sent[0]] + [swap(sent[k], "expert", k) for k in range(1, half)]

    wide = model_width // COLUMNS
    extra = spans[0][1] // COLUMNS
    near = spread(
        place(
            where,
            [table_own, table_far],
            [out_grad, dy_far[0]],
            [lambda i, w: jnp.minimum(i, wide - 1), lambda i, w: jnp.maximum(i - wide, 0)],
            [[(0, 0, wide), (1, wide, wide + extra)]],
            wide + extra,
            COLUMNS,
            half,
            capacity,
            True,
        )
    )
    steps = (spans[1][1] - spans[1][0]) // COLUMNS
    far = spread(
        place(
            where,
            [table_far],
            [dy_far[1]],
            [lambda i, w: i],
            [[(0, 0, steps)]],
            steps,
            COLUMNS,
            half,
            capacity,
            True,
        )
    )

    share = model_width // groups
    part_width = share // X_PARTS
    width = part_width // X_CHUNKS
    x_far = []
    for part in range(X_PARTS):
        rows = jnp.concatenate(
            [
                tokens[:, b * share + part * part_width : b * share + (part + 1) * part_width]
                for b in range(groups)
            ],
            axis=1,
        )
        x_far.append(swap(after(rows, x_far[-1] if x_far else dy_far[-1]), "expert", half))

    down = []
    back = None
    for n, (lo, hi) in enumerate(spans):
        if n == 0:
            pieces, starts = near + near, [lo] * half + [model_width] * half
        else:
            pieces, starts = near + far, [lo] * half + [0] * half
            back = after(back, x_far[0])
        back, kept, sent = down_step(
            hidden_t, matrix, pieces, starts, capacity, back, lo, hi - lo
        )
        pairs = (groups // 2, block, hi - lo)
        down.append(scatter_sum(kept.reshape(pairs), sent.reshape(pairs), "dp"))
    down_share = jnp.concatenate(down, axis=1)

    slot_grad = jnp.sum(hidden.astype(jnp.float32) * back, axis=1)
    grad_pre = (back * gate_act).astype(jnp.bfloat16)
    returned = exchange(slot_grad.reshape(owners, capacity), "expert")[order]
    position_own = slot_positions(table_own, capacity)
    chosen_own = (
        lax.broadcasted_iota(jnp.int32, (owners, capacity, tok_count), 1) == position_own[:, None, :]
    )
    token_grad = jnp.sum(jnp.where(chosen_own, returned[:, :, None], 0.0), axis=1)
    token_grad = jnp.where(
        position_own >= 0, token_grad / jnp.where(table_own > 0, table_own, 1.0), 0.0
    )
    prob_grad = jnp.sum(jnp.where(named, token_grad[:, None, :], 0.0), axis=0).T

    up_parts = []
    for part in range(X_PARTS):
        for chunk in range(X_CHUNKS):
            n = len(up_parts)
            own_map = lambda i, w, c=n: (w[1] ^ i) * (X_PARTS * X_CHUNKS) + c
            far_map = lambda i, w, c=chunk: (w[1] ^ i) * X_CHUNKS + c
            far_rows = x_far[part]
            if n >= 2:
                far_rows = after(far_rows, down[n - 2])
            pieces = spread(
                place(
                    where,
                    [table_own, table_far],
                    [tokens, far_rows],
                    [own_map, far_map],
                    [[(0, 0, groups)], [(1, 0, groups)]],
                    groups,
                    width,
                    half,
                    capacity,
                    False,
                )
            )
            if n == 0:
                pieces[-1] = after(pieces[-1], x_far[1])
            kept, sent = up_step(grad_pre, pieces, groups, capacity)
            pairs = (groups // 2, width, hidden_width)
            up_parts.append(scatter_sum(kept.reshape(pairs), sent.reshape(pairs), "dp"))
    up_share = jnp.concatenate(up_parts, axis=0).astype(jnp.bfloat16)
    return down_share[None], up_share[None], prob_grad


def solution(mesh):
    in_specs = (
        P(("dp", "expert"), None),
        P(("dp", "expert"), None),
        P(("dp", "expert"), None),
        P(("dp", "expert"), None),
        P(("dp", "expert"), None),
        P(("dp", "expert"), None),
        P("expert", None, None),
    )
    out_specs = (P("expert", "dp", None), P("expert", "dp", None), P(("dp", "expert"), None))
    return jax.shard_map(
        per_device, mesh=mesh, in_specs=in_specs, out_specs=out_specs, check_vma=False
    )
```

time: 423 us -> 234 us (0.55)
  waiting for transfers between devices: 211 us -> 109 us
  blocking collectives: 98.9 us -> 0 us
  Pallas kernels: 0 us -> 41.8 us
  matrix products: 33.7 us -> 0.13 us
  local copies, waits for them, and re-layouts: 40.9 us -> 16.4 us
  starting transfers between devices: 16.8 us -> 38.8 us
  other arithmetic: 6.94 us -> 25.3 us
  between operations: 14.2 us -> 1.05 us
    reduce_scatter x2 -> x0, waiting for transfers between devices: 120 us -> none  [the longest x1 102 us: per_device(): lax.psum_scatter(lax.dot_general(column_block, scaled, (((0,), (0,)), (()...]
    ppermute x0 -> x38, waiting for transfers between devices: none -> 109 us  [swap(): return lax.ppermute(value, axis, [(i, i ^ bit) for i in range(size)])]
    all_to_all x1 -> x0, blocking collectives: 98.9 us -> none  [per_device(): lax.all_to_all(send_dy, 'expert', split_axis=0, concat_axis=0, tiled=True)]
    all_to_all x3 -> x0, waiting for transfers between devices: 90.5 us -> none  [the longest x1 84.1 us: per_device(): lax.all_to_all(send_x, 'expert', split_axis=0, concat_axis=0, tiled=True)]
    pallas_call x0 -> x12, Pallas kernels: none -> 41.8 us  [the longest x6 20 us: place(): pl.pallas_call(functools.partial(place_kernel, parts, scaled, half, capac...]
    ppermute x0 -> x38, starting transfers between devices: none -> 38.8 us  [swap(): return lax.ppermute(value, axis, [(i, i ^ bit) for i in range(size)])]
    dot_general x4 -> x1, matrix products: 33.7 us -> 0.13 us  [slot_positions(): jnp.dot(jnp.where(routed, 1.0, 0.0).astype(jnp.bfloat16), jnp.where(earli...]
    gather x7 -> x3, local copies, waits for them, and re-layouts: 22.9 us -> 4.64 us  [the longest x1 2.61 us: per_device(): up = saved_up.reshape(owners, capacity, hidden_width)[order]]
  transfers between devices with their start and end apart: 5 -> 38, of which waited for: 4 -> 18; matrix products, arithmetic and copies ran while one was open for 13% -> 15% of each run, Pallas kernels for 0% -> 13%
where the time goes in v1:
time: 234 us; the launch traced here: 233 us
  waiting for transfers between devices  109 us (47%)
  Pallas kernels  41.8 us (18%)
  starting transfers between devices  38.8 us (17%)
  other arithmetic  25.3 us (11%)
  local copies, waits for them, and re-layouts  16.4 us (7%)
    ppermute x38, waiting for transfers between devices, swap(): return lax.ppermute(value, axis, [(i, i ^ bit) for i in range(size)])  109 us
    ppermute x38, starting transfers between devices, swap(): return lax.ppermute(value, axis, [(i, i ^ bit) for i in range(size)])  38.8 us
    pallas_call x6, Pallas kernels, place(): pl.pallas_call(functools.partial(place_kernel, parts, scaled, half, capac...  20 us
    pallas_call x2, Pallas kernels, down_step(): pl.pallas_call(functools.partial(down_kernel, len(pieces), first), grid=(...  14.9 us
    pallas_call x4, Pallas kernels, up_step(): pl.pallas_call(functools.partial(up_kernel, len(pieces), capacity), grid=...  6.78 us
    convert_element_type x6, other arithmetic, scatter_sum(): sent = jnp.stack(blocks[1::2]).astype(jnp.bfloat16)  6.11 us
    add x2, other arithmetic, scatter_sum(): blocks = [kept[i] + got[i].astype(jnp.float32) for i in range(len(kept))]  5.14 us
  transfers between devices with their start and end apart: 38, of which 18 were waited for; matrix products, arithmetic and copies ran while one was open for 15% of the time, Pallas kernels for 13%

profile of v1, /device:TPU:0, one launch (start us, length us, event | category | flops | bytes accessed | tf_op | source)
XLA Modules:
  0.0 232.6 jit_solution(9612509344850472953)
XLA Ops:
  0.7 1.1 slice.132
  1.8 4.1 %collective-permute-start.1 = (bf16[128,1024]{1,0:T(8,128)(2,1)S(1)}, bf16[128,1024]{1,0:T(8,128)(2,1)S(1)}, u32[]{:S(2)}, u32[]{:S(2)}) collective-permute-start(bf16[128,1024]{1,0:T(8,128)(2,1)S(1)} %slice.132), channel_id=1, source_target_pairs={{0,4},{1,5},{2,6},{3,7},{4,0},{5,1},{6,2},{7,3},{8,12},{9,13},{10,... | collective-permute-start | bytes 786440 | tf_op jit(solution)/shard_map/ppermute | solution.py:32
  7.5 2.1 slice.137
  9.6 8.4 %collective-permute-done.1.refs_3_ = bf16[128,1024]{1,0:T(8,128)(2,1)S(1)} collective-permute-done((bf16[128,1024]{1,0:T(8,128)(2,1)S(1)}, bf16[128,1024]{1,0:T(8,128)(2,1)S(1)}, u32[]{:S(2)}, u32[]{:S(2)}) %collective-permute-start.1) | collective-permute-done | bytes 262176 | tf_op jit(solution)/shard_map/ppermute | solution.py:32
  19.7 5.7 %place.6 = (bf16[64,5120]{1,0:T(8,128)(2,1)S(1)}, bf16[64,5120]{1,0:T(8,128)(2,1)}, bf16[64,5120]{1,0:T(8,128)(2,1)}, bf16[64,5120]{1,0:T(8,128)(2,1)}) custom-call(s32[2]{0:T(128)S(1)} %pad_add_fusion.where, f32[8,128]{1,0:T(8,128)S(1)} %fusion.18.refs_0_, f32[8,128]{1,0:T(8,128)S(1)} %collective-permute-done.refs_1_.refs_0_, ...), custom_call_target="tpu_custom_call" | custom-call | tf_op jit(solution)/shard_map/place/pallas_call | solution.py:115
  25.4 1.5 collective-permute-start.2
  27.0 4.1 %collective-permute-start.3 = (bf16[64,5120]{1,0:T(8,128)(2,1)}, bf16[64,5120]{1,0:T(8,128)(2,1)}, u32[]{:S(2)}, u32[]{:S(2)}) collective-permute-start(bf16[64,5120]{1,0:T(8,128)(2,1)} %get-tuple-element.50), channel_id=1, source_target_pairs={{0,2},{1,3},{2,0},{3,1},{4,6},{5,7},{6,4},{7,5},{8,10},{9,11},{10,... | collective-permute-start | bytes 1966088 | tf_op jit(solution)/shard_map/ppermute | solution.py:32
  32.8 1.5 gather_fusion
  34.3 2.6 %gather_fusion.1 = bf16[8,64,768]{2,1,0:T(8,128)(2,1)} fusion(bf16[8,64,768]{2,1,0:T(8,128)(2,1)} %bitcast.139, s32[1024]{0:T(1024)S(1)} %pad_clamp_fusion), kind=kCustom, calls=%fused_computation.1 | custom fusion | bytes 1572896 | tf_op jit(solution)/shard_map/gather | solution.py:261
  36.9 18.6 %collective-permute-done.7.refs_1_ = bf16[128,3072]{1,0:T(8,128)(2,1)} collective-permute-done((bf16[128,3072]{1,0:T(8,128)(2,1)}, bf16[128,3072]{1,0:T(8,128)(2,1)}, u32[]{:S(2)}, u32[]{:S(2)}) %collective-permute-start.7) | collective-permute-done | bytes 786464 | tf_op jit(solution)/shard_map/ppermute | solution.py:32
  55.5 5.6 %place.7 = (bf16[64,3072]{1,0:T(8,128)(2,1)S(1)}, bf16[64,3072]{1,0:T(8,128)(2,1)}, bf16[64,3072]{1,0:T(8,128)(2,1)}, bf16[64,3072]{1,0:T(8,128)(2,1)}) custom-call(s32[2]{0:T(128)S(1)} %pad_add_fusion.where, f32[8,128]{1,0:T(8,128)S(1)} %collective-permute-done.refs_1_.refs_0_, bf16[128,3072]{1,0:T(8,128)(2,1)} %collective-permute-done.7.refs_1_), custom_call_target="tpu_custom_call" | custom-call | tf_op jit(solution)/shard_map/place/pallas_call | solution.py:115
  61.1 2.4 %collective-permute-start.10 = (bf16[64,3072]{1,0:T(8,128)(2,1)}, bf16[64,3072]{1,0:T(8,128)(2,1)}, u32[]{:S(2)}, u32[]{:S(2)}) collective-permute-start(bf16[64,3072]{1,0:T(8,128)(2,1)} %get-tuple-element.58), channel_id=1, source_target_pairs={{0,3},{1,2},{2,1},{3,0},{4,7},{5,6},{6,5},{7,4},{8,11},{9,10},{10,... | collective-permute-start | bytes 1179656 | tf_op jit(solution)/shard_map/ppermute | solution.py:32
  64.3 8.6 %collective-permute-done.3.refs_2_.refs_6_ = bf16[64,5120]{1,0:T(8,128)(2,1)} collective-permute-done((bf16[64,5120]{1,0:T(8,128)(2,1)}, bf16[64,5120]{1,0:T(8,128)(2,1)}, u32[]{:S(2)}, u32[]{:S(2)}) %collective-permute-start.3) | collective-permute-done | bytes 655392 | tf_op jit(solution)/shard_map/ppermute | solution.py:32
  72.9 2.7 %fusion.4 = bf16[512,768]{1,0:T(8,128)(2,1)} fusion(bf16[8,64,768]{2,1,0:T(8,128)(2,1)} %gather_fusion.1, bf16[8,64,768]{2,1,0:T(8,128)(2,1)} %gather_fusion), kind=kLoop, calls=%fused_computation.15 | loop fusion | flops 3145728 | bytes 2359296 | tf_op jit(solution)/shard_map/convert_element_type | solution.py:263
  75.6 2.3 copy.23
  77.9 1.3 dynamic-slice_bitcast_fusion.3
  79.3 7.9 %collective-permute-done.4.refs_3_.refs_7_ = bf16[64,5120]{1,0:T(8,128)(2,1)} collective-permute-done((bf16[64,5120]{1,0:T(8,128)(2,1)}, bf16[64,5120]{1,0:T(8,128)(2,1)}, u32[]{:S(2)}, u32[]{:S(2)}) %collective-permute-start.4) | collective-permute-done | bytes 655392 | tf_op jit(solution)/shard_map/ppermute | solution.py:32
  87.2 4.3 %down_step.2 = (f32[512,768]{1,0:T(8,128)S(1)}, f32[384,1024]{1,0:T(8,128)}, bf16[384,1024]{1,0:T(8,128)(2,1)}) custom-call(bf16[768,512]{1,0:T(8,128)(2,1)S(1)} %pad_maximum_fusion.1.weighted, bf16[768,4096]{1,0:T(8,128)(2,1)} %bitcast.135, bf16[64,5120]{1,0:T(8,128)(2,1)S(1)} %get-tuple-element.48.refs_0_.refs_4_, ...), custom_call_target="tpu_custom_call" | custom-call | tf_op jit(solution)/shard_map/down_step/pallas_call | solution.py:165
  91.5 1.2 copy-done.6
  92.7 2.9 %collective-permute-done.10.refs_7_ = bf16[64,3072]{1,0:T(8,128)(2,1)} collective-permute-done((bf16[64,3072]{1,0:T(8,128)(2,1)}, bf16[64,3072]{1,0:T(8,128)(2,1)}, u32[]{:S(2)}, u32[]{:S(2)}) %collective-permute-start.10) | collective-permute-done | bytes 393248 | tf_op jit(solution)/shard_map/ppermute | solution.py:32
  95.6 1.1 collective-permute-done.8.refs_5_
  96.7 6.2 %collective-permute-done.9.refs_6_ = bf16[64,3072]{1,0:T(8,128)(2,1)} collective-permute-done((bf16[64,3072]{1,0:T(8,128)(2,1)}, bf16[64,3072]{1,0:T(8,128)(2,1)}, u32[]{:S(2)}, u32[]{:S(2)}) %collective-permute-start.9) | collective-permute-done | bytes 393248 | tf_op jit(solution)/shard_map/ppermute | solution.py:32
  102.9 10.7 %down_step.3 = (f32[512,768]{1,0:T(8,128)}, f32[384,3072]{1,0:T(8,128)}, bf16[384,3072]{1,0:T(8,128)(2,1)}) custom-call(bf16[768,512]{1,0:T(8,128)(2,1)S(1)} %pad_maximum_fusion.1.weighted, bf16[768,4096]{1,0:T(8,128)(2,1)} %bitcast.136, bf16[64,5120]{1,0:T(8,128)(2,1)S(1)} %get-tuple-element.48.refs_0_.refs_4_, ...), custom_call_target="tpu_custom_call" | custom-call | tf_op jit(solution)/shard_map/down_step/pallas_call | solution.py:165
  114.2 2.1 multiply_reduce_fusion
  116.8 1.9 place.9
  118.7 1.8 collective-permute-start.20
  120.7 1.1 fusion.13
  121.8 1.3 collective-permute-start.6
  123.2 3.9 %collective-permute-start.17 = (bf16[128,2048]{1,0:T(8,128)(2,1)S(1)}, bf16[128,2048]{1,0:T(8,128)(2,1)S(1)}, u32[]{:S(2)}, u32[]{:S(2)}) collective-permute-start(bf16[128,2048]{1,0:T(8,128)(2,1)S(1)} %pad_maximum_fusion.3), channel_id=1, source_target_pairs={{0,4},{1,5},{2,6},{3,7},{4,0},{5,1},{6,2},{7,3},{8,12},{9,13},{10,... | collective-permute-start | bytes 1572872 | tf_op jit(solution)/shard_map/ppermute | solution.py:32
  127.1 2.0 place.8
  129.2 2.0 collective-permute-start.22
  131.2 13.9 %collective-permute-done.21.refs_2_ = bf16[128,1024]{1,0:T(8,128)(2,1)S(1)} collective-permute-done((bf16[128,1024]{1,0:T(8,128)(2,1)S(1)}, bf16[128,1024]{1,0:T(8,128)(2,1)S(1)}, u32[]{:S(2)}, u32[]{:S(2)}) %collective-permute-start.21) | collective-permute-done | bytes 262176 | tf_op jit(solution)/shard_map/ppermute | solution.py:32
  145.1 2.5 %collective-permute-start.16 = (bf16[128,1024]{1,0:T(8,128)(2,1)S(1)}, bf16[128,1024]{1,0:T(8,128)(2,1)S(1)}, u32[]{:S(2)}, u32[]{:S(2)}) collective-permute-start(bf16[128,1024]{1,0:T(8,128)(2,1)S(1)} %get-tuple-element.68), channel_id=1, source_target_pairs={{0,3},{1,2},{2,1},{3,0},{4,7},{5,6},{6,5},{7,4},{8,11},{9,10},{10,... | collective-permute-start | bytes 786440 | tf_op jit(solution)/shard_map/ppermute | solution.py:32
  147.6 7.5 %collective-permute-done.22.refs_3_ = bf16[128,1024]{1,0:T(8,128)(2,1)S(1)} collective-permute-done((bf16[128,1024]{1,0:T(8,128)(2,1)S(1)}, bf16[128,1024]{1,0:T(8,128)(2,1)S(1)}, u32[]{:S(2)}, u32[]{:S(2)}) %collective-permute-start.22) | collective-permute-done | bytes 262176 | tf_op jit(solution)/shard_map/ppermute | solution.py:32
  155.0 1.5 collective-permute-start.14
  156.5 2.1 up_step.5
  158.6 2.3 %convert_add_fusion.10 = f32[192,1024]{1,0:T(8,128)} fusion(f32[384,1024]{1,0:T(8,128)S(1)} %copy-done.21, bf16[2,192,1024]{2,1,0:T(8,128)(2,1)} %collective-permute-done.5, bf16[1,192,1024]{2,1,0:T(8,128)(2,1)S(1)} %collective-permute-done.6), kind=kLoop, calls=%fused_computation.33 | loop fusion | flops 786432 | bytes 2359296 | tf_op jit(solution)/shard_map/add | solution.py:50
  160.9 2.8 %place.10 = (bf16[128,1024]{1,0:T(8,128)(2,1)S(1)}, bf16[128,1024]{1,0:T(8,128)(2,1)}, bf16[128,1024]{1,0:T(8,128)(2,1)S(1)}, bf16[128,1024]{1,0:T(8,128)(2,1)S(1)}) custom-call(s32[2]{0:T(128)S(1)} %pad_add_fusion.where, f32[8,128]{1,0:T(8,128)S(1)} %fusion.18.refs_0_, f32[8,128]{1,0:T(8,128)S(1)} %collective-permute-done.refs_1_.refs_0_, ...), custom_call_target="tpu_custom_call" | custom-call | tf_op jit(solution)/shard_map/place/pallas_call | solution.py:115
  163.9 2.7 %fusion = bf16[1,192,3072]{2,1,0:T(8,128)(2,1)} fusion(f32[384,3072]{1,0:T(8,128)S(1)} %copy-done.19, bf16[2,192,3072]{2,1,0:T(8,128)(2,1)} %collective-permute-done.12), kind=kLoop, calls=%fused_computation.7 | loop fusion | flops 1769472 | bytes 4718592 | tf_op jit(solution)/shard_map/convert_element_type | solution.py:54
  167.8 2.1 up_step.4
  169.9 1.1 copy-done.9
  171.8 1.8 collective-permute-start.26
  173.6 1.9 collective-permute-done.25.refs_1_
  175.4 1.7 collective-permute-start.27
  177.9 3.1 %collective-permute-done.26.refs_2_ = bf16[128,1024]{1,0:T(8,128)(2,1)S(1)} collective-permute-done((bf16[128,1024]{1,0:T(8,128)(2,1)S(1)}, bf16[128,1024]{1,0:T(8,128)(2,1)S(1)}, u32[]{:S(2)}, u32[]{:S(2)}) %collective-permute-start.26) | collective-permute-done | bytes 262176 | tf_op jit(solution)/shard_map/ppermute | solution.py:32
  181.0 5.9 %collective-permute-done.27.refs_3_ = bf16[128,1024]{1,0:T(8,128)(2,1)S(1)} collective-permute-done((bf16[128,1024]{1,0:T(8,128)(2,1)S(1)}, bf16[128,1024]{1,0:T(8,128)(2,1)S(1)}, u32[]{:S(2)}, u32[]{:S(2)}) %collective-permute-start.27) | collective-permute-done | bytes 262176 | tf_op jit(solution)/shard_map/ppermute | solution.py:32
  186.9 1.3 up_step.6
  188.3 1.1 fusion.11
  189.4 1.8 collective-permute-start.24
  192.7 3.7 %collective-permute-done.13 = bf16[1,192,3072]{2,1,0:T(8,128)(2,1)} collective-permute-done((bf16[1,192,3072]{2,1,0:T(8,128)(2,1)}, bf16[1,192,3072]{2,1,0:T(8,128)(2,1)}, u32[]{:S(2)}, u32[]{:S(2)}) %collective-permute-start.13) | collective-permute-done | bytes 1179680 | tf_op jit(solution)/shard_map/ppermute | solution.py:32
  196.4 2.8 %convert_add_fusion = f32[192,3072]{1,0:T(8,128)S(1)} fusion(f32[384,3072]{1,0:T(8,128)} %get-tuple-element.62, bf16[2,192,3072]{2,1,0:T(8,128)(2,1)} %collective-permute-done.12, bf16[1,192,3072]{2,1,0:T(8,128)(2,1)} %collective-permute-done.13), kind=kLoop, calls=%fused_computation.4 | loop fusion | flops 2359296 | bytes 7077888 | tf_op jit(solution)/shard_map/add | solution.py:50
  199.2 2.0 place.11
  201.1 1.5 collective-permute-start.30
  202.7 1.7 collective-permute-start.31
  204.8 4.8 %collective-permute-done.30.refs_1_ = bf16[128,1024]{1,0:T(8,128)(2,1)S(1)} collective-permute-done((bf16[128,1024]{1,0:T(8,128)(2,1)S(1)}, bf16[128,1024]{1,0:T(8,128)(2,1)S(1)}, u32[]{:S(2)}, u32[]{:S(2)}) %collective-permute-start.30) | collective-permute-done | bytes 262176 | tf_op jit(solution)/shard_map/ppermute | solution.py:32
  210.0 1.8 collective-permute-done.31.refs_2_
  211.8 2.8 %collective-permute-done.32.refs_3_ = bf16[128,1024]{1,0:T(8,128)(2,1)S(1)} collective-permute-done((bf16[128,1024]{1,0:T(8,128)(2,1)S(1)}, bf16[128,1024]{1,0:T(8,128)(2,1)S(1)}, u32[]{:S(2)}, u32[]{:S(2)}) %collective-permute-start.32) | collective-permute-done | bytes 262176 | tf_op jit(solution)/shard_map/ppermute | solution.py:32
  214.6 1.3 up_step.7
  216.0 1.1 fusion.15
  217.2 1.1 fusion.14
  218.3 2.3 %collective-permute-done.29 = bf16[1,256,768]{2,1,0:T(8,128)(2,1)S(1)} collective-permute-done((bf16[1,256,768]{2,1,0:T(8,128)(2,1)S(1)}, bf16[1,256,768]{2,1,0:T(8,128)(2,1)S(1)}, u32[]{:S(2)}, u32[]{:S(2)}) %collective-permute-start.29) | collective-permute-done | bytes 393248 | tf_op jit(solution)/shard_map/ppermute | solution.py:32
  221.4 2.0 maximum_bitcast_fusion
  223.4 7.7 %collective-permute-done.34 = bf16[1,256,768]{2,1,0:T(8,128)(2,1)S(1)} collective-permute-done((bf16[1,256,768]{2,1,0:T(8,128)(2,1)S(1)}, bf16[1,256,768]{2,1,0:T(8,128)(2,1)S(1)}, u32[]{:S(2)}, u32[]{:S(2)}) %collective-permute-start.34) | collective-permute-done | bytes 393248 | tf_op jit(solution)/shard_map/ppermute | solution.py:32
  231.3 1.2 pad_maximum_fusion
  (125 shorter events, 13.4 us)
Async XLA Ops:
  0.6 32.2 %copy-start = (bf16[512,768]{1,0:T(8,128)(2,1)S(1)}, bf16[512,768]{1,0:T(8,128)(2,1)}, u32[]{:S(2)}) copy-start(bf16[512,768]{1,0:T(8,128)(2,1)} %param.11) | copy-start | bytes 2359300
  0.6 18.1 %copy-start.3 = (bf16[128,4096]{1,0:T(8,128)(2,1)S(1)}, bf16[128,4096]{1,0:T(8,128)(2,1)}, u32[]{:S(2)}) copy-start(bf16[128,4096]{1,0:T(8,128)(2,1)} %refs_2_.5) | copy-start | bytes 3145732
  1.8 29.3 %copy-start.2 = (bf16[128,4096]{1,0:T(8,128)(2,1)S(1)}, bf16[128,4096]{1,0:T(8,128)(2,1)}, u32[]{:S(2)}) copy-start(bf16[128,4096]{1,0:T(8,128)(2,1)} %refs_2_.9) | copy-start | bytes 3145732
  1.8 16.2 %collective-permute-start.1 = (bf16[128,1024]{1,0:T(8,128)(2,1)S(1)}, bf16[128,1024]{1,0:T(8,128)(2,1)S(1)}, u32[]{:S(2)}, u32[]{:S(2)}) collective-permute-start(bf16[128,1024]{1,0:T(8,128)(2,1)S(1)} %slice.132), channel_id=1, source_target_pairs={{0,4},{1,5},{2,6},{3,7},{4,0},{5,1},{6,2},{7,3},{8,12},{9,13},{10,... | collective-permute-start | bytes 786440 | tf_op jit(solution)/shard_map/ppermute | solution.py:32
  6.6 12.1 %copy-start.27 = (s32[8]{0:T(128)}, s32[8]{0:T(128)S(1)}, u32[]{:S(2)}) copy-start(s32[8]{0:T(128)S(1)} %iota_multiply_fusion) | copy-start | bytes 100
  7.3 11.4 %collective-permute-start = (f32[8,128]{1,0:T(8,128)S(1)}, f32[8,128]{1,0:T(8,128)S(1)}, u32[]{:S(2)}, u32[]{:S(2)}) collective-permute-start(f32[8,128]{1,0:T(8,128)S(1)} %fusion.18.refs_0_), channel_id=1, source_target_pairs={{0,4},{1,5},{2,6},{3,7},{4,0},{5,1},{6,2},{7,3},{8,12},{9,13},{10,... | collective-permute-start | bytes 12296 | tf_op jit(solution)/shard_map/ppermute | solution.py:32
  18.6 36.9 %collective-permute-start.7 = (bf16[128,3072]{1,0:T(8,128)(2,1)}, bf16[128,3072]{1,0:T(8,128)(2,1)}, u32[]{:S(2)}, u32[]{:S(2)}) collective-permute-start(bf16[128,3072]{1,0:T(8,128)(2,1)} %slice.137), channel_id=1, source_target_pairs={{0,4},{1,5},{2,6},{3,7},{4,0},{5,1},{6,2},{7,3},{8,12},{9,13},{10,... | collective-permute-start | bytes 2359304 | tf_op jit(solution)/shard_map/ppermute | solution.py:32
  25.4 38.1 %collective-permute-start.2 = (bf16[64,5120]{1,0:T(8,128)(2,1)}, bf16[64,5120]{1,0:T(8,128)(2,1)S(1)}, u32[]{:S(2)}, u32[]{:S(2)}) collective-permute-start(bf16[64,5120]{1,0:T(8,128)(2,1)} %get-tuple-element.49), channel_id=1, source_target_pairs={{0,1},{1,0},{2,3},{3,2},{4,5},{5,4},{6,7},{7,6},{8,9},{9,8},{10,11... | collective-permute-start | bytes 1966088 | tf_op jit(solution)/shard_map/ppermute | solution.py:32
  27.0 45.9 %collective-permute-start.3 = (bf16[64,5120]{1,0:T(8,128)(2,1)}, bf16[64,5120]{1,0:T(8,128)(2,1)}, u32[]{:S(2)}, u32[]{:S(2)}) collective-permute-start(bf16[64,5120]{1,0:T(8,128)(2,1)} %get-tuple-element.50), channel_id=1, source_target_pairs={{0,2},{1,3},{2,0},{3,1},{4,6},{5,7},{6,4},{7,5},{8,10},{9,11},{10,... | collective-permute-start | bytes 1966088 | tf_op jit(solution)/shard_map/ppermute | solution.py:32
  32.8 54.4 %collective-permute-start.4 = (bf16[64,5120]{1,0:T(8,128)(2,1)}, bf16[64,5120]{1,0:T(8,128)(2,1)}, u32[]{:S(2)}, u32[]{:S(2)}) collective-permute-start(bf16[64,5120]{1,0:T(8,128)(2,1)} %get-tuple-element.51), channel_id=1, source_target_pairs={{0,3},{1,2},{2,1},{3,0},{4,7},{5,6},{6,5},{7,4},{8,11},{9,10},{10,... | collective-permute-start | bytes 1966088 | tf_op jit(solution)/shard_map/ppermute | solution.py:32
  55.5 37.2 %collective-permute-start.11 = (bf16[128,2048]{1,0:T(8,128)(2,1)}, bf16[128,2048]{1,0:T(8,128)(2,1)S(1)}, u32[]{:S(2)}, u32[]{:S(2)}) collective-permute-start(bf16[128,2048]{1,0:T(8,128)(2,1)} %pad_maximum_fusion.2), channel_id=1, source_target_pairs={{0,4},{1,5},{2,6},{3,7},{4,0},{5,1},{6,2},{7,3},{8,12},{9,13},{10,... | collective-permute-start | bytes 1572872 | tf_op jit(solution)/shard_map/ppermute | solution.py:32
  61.1 34.5 %collective-permute-start.10 = (bf16[64,3072]{1,0:T(8,128)(2,1)}, bf16[64,3072]{1,0:T(8,128)(2,1)}, u32[]{:S(2)}, u32[]{:S(2)}) collective-permute-start(bf16[64,3072]{1,0:T(8,128)(2,1)} %get-tuple-element.58), channel_id=1, source_target_pairs={{0,3},{1,2},{2,1},{3,0},{4,7},{5,6},{6,5},{7,4},{8,11},{9,10},{10,... | collective-permute-start | bytes 1179656 | tf_op jit(solution)/shard_map/ppermute | solution.py:32
  63.5 33.2 %collective-permute-start.8 = (bf16[64,3072]{1,0:T(8,128)(2,1)}, bf16[64,3072]{1,0:T(8,128)(2,1)}, u32[]{:S(2)}, u32[]{:S(2)}) collective-permute-start(bf16[64,3072]{1,0:T(8,128)(2,1)} %get-tuple-element.56), channel_id=1, source_target_pairs={{0,1},{1,0},{2,3},{3,2},{4,5},{5,4},{6,7},{7,6},{8,9},{9,8},{10,11... | collective-permute-start | bytes 1179656 | tf_op jit(solution)/shard_map/ppermute | solution.py:32
  72.9 30.0 %collective-permute-start.9 = (bf16[64,3072]{1,0:T(8,128)(2,1)}, bf16[64,3072]{1,0:T(8,128)(2,1)}, u32[]{:S(2)}, u32[]{:S(2)}) collective-permute-start(bf16[64,3072]{1,0:T(8,128)(2,1)} %get-tuple-element.57), channel_id=1, source_target_pairs={{0,2},{1,3},{2,0},{3,1},{4,6},{5,7},{6,4},{7,5},{8,10},{9,11},{10,... | collective-permute-start | bytes 1179656 | tf_op jit(solution)/shard_map/ppermute | solution.py:32
  91.5 1.2 copy-start.6
  92.6 21.0 %copy-start.4 = (bf16[128,2048]{1,0:T(8,128)(2,1)}, bf16[128,2048]{1,0:T(8,128)(2,1)S(1)}, u32[]{:S(2)}) copy-start(bf16[128,2048]{1,0:T(8,128)(2,1)S(1)} %collective-permute-done.11.refs_3_) | copy-start | bytes 1572868
  102.9 11.3 %copy-start.17 = (bf16[8,64,768]{2,1,0:T(8,128)(2,1)S(1)}, bf16[8,64,768]{2,1,0:T(8,128)(2,1)}, u32[]{:S(2)}) copy-start(bf16[8,64,768]{2,1,0:T(8,128)(2,1)} %gather_fusion) | copy-start | bytes 2359300
  102.9 11.3 %copy-start.18 = (bf16[512,768]{1,0:T(8,128)(2,1)S(1)}, bf16[512,768]{1,0:T(8,128)(2,1)}, u32[]{:S(2)}) copy-start(bf16[512,768]{1,0:T(8,128)(2,1)} %fusion.4) | copy-start | bytes 2359300
  113.6 50.2 %collective-permute-start.12 = (bf16[2,192,3072]{2,1,0:T(8,128)(2,1)}, bf16[2,192,3072]{2,1,0:T(8,128)(2,1)}, u32[]{:S(2)}, u32[]{:S(2)}) collective-permute-start(bf16[2,192,3072]{2,1,0:T(8,128)(2,1)} %bitcast.154), channel_id=1, source_target_pairs={{0,8},{8,0},{16,24},{24,16},{1,9},{9,1},{17,25},{25,17},{2,10},{10... | collective-permute-start | bytes 7077896 | tf_op jit(solution)/shard_map/ppermute | solution.py:32
  113.7 6.9 %collective-permute-start.5 = (bf16[2,192,1024]{2,1,0:T(8,128)(2,1)}, bf16[2,192,1024]{2,1,0:T(8,128)(2,1)}, u32[]{:S(2)}, u32[]{:S(2)}) collective-permute-start(bf16[2,192,1024]{2,1,0:T(8,128)(2,1)} %bitcast.17), channel_id=1, source_target_pairs={{0,8},{8,0},{16,24},{24,16},{1,9},{9,1},{17,25},{25,17},{2,10},{10... | collective-permute-start | bytes 2359304 | tf_op jit(solution)/shard_map/ppermute | solution.py:32
  114.2 2.6 %copy-start.5 = (bf16[128,2048]{1,0:T(8,128)(2,1)S(1)}, bf16[128,2048]{1,0:T(8,128)(2,1)}, u32[]{:S(2)}) copy-start(bf16[128,2048]{1,0:T(8,128)(2,1)} %copy-done.4) | copy-start | bytes 1572868
  116.4 4.3 %copy-start.21 = (f32[384,1024]{1,0:T(8,128)S(1)}, f32[384,1024]{1,0:T(8,128)}, u32[]{:S(2)}) copy-start(f32[384,1024]{1,0:T(8,128)} %get-tuple-element.52) | copy-start | bytes 4718596
  116.4 6.7 %copy-start.22 = (bf16[128,512]{1,0:T(8,128)(2,1)S(1)}, bf16[128,512]{1,0:T(8,128)(2,1)}, u32[]{:S(2)}) copy-start(bf16[128,512]{1,0:T(8,128)(2,1)} %get-tuple-element.95) | copy-start | bytes 393220
  116.4 6.7 %copy-start.23 = (bf16[128,512]{1,0:T(8,128)(2,1)S(1)}, bf16[128,512]{1,0:T(8,128)(2,1)}, u32[]{:S(2)}) copy-start(bf16[128,512]{1,0:T(8,128)(2,1)} %get-tuple-element.96) | copy-start | bytes 393220
  116.4 6.7 %copy-start.24 = (bf16[128,512]{1,0:T(8,128)(2,1)S(1)}, bf16[128,512]{1,0:T(8,128)(2,1)}, u32[]{:S(2)}) copy-start(bf16[128,512]{1,0:T(8,128)(2,1)} %get-tuple-element.97) | copy-start | bytes 393220
  116.4 6.7 %copy-start.25 = (bf16[128,512]{1,0:T(8,128)(2,1)S(1)}, bf16[128,512]{1,0:T(8,128)(2,1)}, u32[]{:S(2)}) copy-start(bf16[128,512]{1,0:T(8,128)(2,1)} %get-tuple-element.98) | copy-start | bytes 393220
  116.4 4.1 %collective-permute-start.35 = (f32[4,1,64]{2,0,1:T(4,128)S(1)}, f32[4,1,64]{2,0,1:T(4,128)S(1)}, u32[]{:S(2)}, u32[]{:S(2)}) collective-permute-start(f32[4,1,64]{2,0,1:T(4,128)S(1)} %bitcast.153), channel_id=1, source_target_pairs={{0,1},{1,0},{2,3},{3,2},{4,5},{5,4},{6,7},{7,6},{8,9},{9,8},{10,11... | collective-permute-start | bytes 3080 | tf_op jit(solution)/shard_map/ppermute | solution.py:32
  118.7 10.5 %collective-permute-start.20 = (bf16[128,1024]{1,0:T(8,128)(2,1)S(1)}, bf16[128,1024]{1,0:T(8,128)(2,1)S(1)}, u32[]{:S(2)}, u32[]{:S(2)}) collective-permute-start(bf16[128,1024]{1,0:T(8,128)(2,1)S(1)} %get-tuple-element.74), channel_id=1, source_target_pairs={{0,1},{1,0},{2,3},{3,2},{4,5},{5,4},{6,7},{7,6},{8,9},{9,8},{10,11... | collective-permute-start | bytes 786440 | tf_op jit(solution)/shard_map/ppermute | solution.py:32
  120.6 8.5 %collective-permute-start.36 = (f32[2,2,64]{2,0,1:T(2,128)S(1)}, f32[2,2,64]{2,0,1:T(2,128)S(1)}, u32[]{:S(2)}, u32[]{:S(2)}) collective-permute-start(f32[2,2,64]{2,0,1:T(2,128)S(1)} %bitcast.151), channel_id=1, source_target_pairs={{0,2},{1,3},{2,0},{3,1},{4,6},{5,7},{6,4},{7,5},{8,10},{9,11},{10,... | collective-permute-start | bytes 3080 | tf_op jit(solution)/shard_map/ppermute | solution.py:32
  121.8 36.8 %collective-permute-start.6 = (bf16[1,192,1024]{2,1,0:T(8,128)(2,1)S(1)}, bf16[1,192,1024]{2,1,0:T(8,128)(2,1)S(1)}, u32[]{:S(2)}, u32[]{:S(2)}) collective-permute-start(bf16[1,192,1024]{2,1,0:T(8,128)(2,1)S(1)} %fusion.13), channel_id=1, source_target_pairs={{0,16},{8,24},{16,0},{24,8},{1,17},{9,25},{17,1},{25,9},{2,18},{10... | collective-permute-start | bytes 1179656 | tf_op jit(solution)/shard_map/ppermute | solution.py:32
  123.2 37.8 %collective-permute-start.17 = (bf16[128,2048]{1,0:T(8,128)(2,1)S(1)}, bf16[128,2048]{1,0:T(8,128)(2,1)S(1)}, u32[]{:S(2)}, u32[]{:S(2)}) collective-permute-start(bf16[128,2048]{1,0:T(8,128)(2,1)S(1)} %pad_maximum_fusion.3), channel_id=1, source_target_pairs={{0,4},{1,5},{2,6},{3,7},{4,0},{5,1},{6,2},{7,3},{8,12},{9,13},{10,... | collective-permute-start | bytes 1572872 | tf_op jit(solution)/shard_map/ppermute | solution.py:32
  129.1 16.0 %collective-permute-start.21 = (bf16[128,1024]{1,0:T(8,128)(2,1)S(1)}, bf16[128,1024]{1,0:T(8,128)(2,1)S(1)}, u32[]{:S(2)}, u32[]{:S(2)}) collective-permute-start(bf16[128,1024]{1,0:T(8,128)(2,1)S(1)} %get-tuple-element.75), channel_id=1, source_target_pairs={{0,2},{1,3},{2,0},{3,1},{4,6},{5,7},{6,4},{7,5},{8,10},{9,11},{10,... | collective-permute-start | bytes 786440 | tf_op jit(solution)/shard_map/ppermute | solution.py:32
  129.2 25.9 %collective-permute-start.22 = (bf16[128,1024]{1,0:T(8,128)(2,1)S(1)}, bf16[128,1024]{1,0:T(8,128)(2,1)S(1)}, u32[]{:S(2)}, u32[]{:S(2)}) collective-permute-start(bf16[128,1024]{1,0:T(8,128)(2,1)S(1)} %get-tuple-element.76), channel_id=1, source_target_pairs={{0,3},{1,2},{2,1},{3,0},{4,7},{5,6},{6,5},{7,4},{8,11},{9,10},{10,... | collective-permute-start | bytes 786440 | tf_op jit(solution)/shard_map/ppermute | solution.py:32
  145.1 21.5 %collective-permute-start.16 = (bf16[128,1024]{1,0:T(8,128)(2,1)S(1)}, bf16[128,1024]{1,0:T(8,128)(2,1)S(1)}, u32[]{:S(2)}, u32[]{:S(2)}) collective-permute-start(bf16[128,1024]{1,0:T(8,128)(2,1)S(1)} %get-tuple-element.68), channel_id=1, source_target_pairs={{0,3},{1,2},{2,1},{3,0},{4,7},{5,6},{6,5},{7,4},{8,11},{9,10},{10,... | collective-permute-start | bytes 786440 | tf_op jit(solution)/shard_map/ppermute | solution.py:32
  155.0 12.2 %collective-permute-start.14 = (bf16[128,1024]{1,0:T(8,128)(2,1)S(1)}, bf16[128,1024]{1,0:T(8,128)(2,1)S(1)}, u32[]{:S(2)}, u32[]{:S(2)}) collective-permute-start(bf16[128,1024]{1,0:T(8,128)(2,1)S(1)} %get-tuple-element.66), channel_id=1, source_target_pairs={{0,1},{1,0},{2,3},{3,2},{4,5},{5,4},{6,7},{7,6},{8,9},{9,8},{10,11... | collective-permute-start | bytes 786440 | tf_op jit(solution)/shard_map/ppermute | solution.py:32
  156.5 7.3 %copy-start.19 = (f32[384,3072]{1,0:T(8,128)S(1)}, f32[384,3072]{1,0:T(8,128)}, u32[]{:S(2)}) copy-start(f32[384,3072]{1,0:T(8,128)} %get-tuple-element.62) | copy-start | bytes 14155780
  158.6 2.4 %copy-start.7 = (f32[512,768]{1,0:T(8,128)}, f32[512,768]{1,0:T(8,128)S(1)}, u32[]{:S(2)}) copy-start(f32[512,768]{1,0:T(8,128)S(1)} %get-tuple-element.77) | copy-start | bytes 4718596
  158.6 9.2 %collective-permute-start.15 = (bf16[128,1024]{1,0:T(8,128)(2,1)S(1)}, bf16[128,1024]{1,0:T(8,128)(2,1)S(1)}, u32[]{:S(2)}, u32[]{:S(2)}) collective-permute-start(bf16[128,1024]{1,0:T(8,128)(2,1)S(1)} %get-tuple-element.67), channel_id=1, source_target_pairs={{0,2},{1,3},{2,0},{3,1},{4,6},{5,7},{6,4},{7,5},{8,10},{9,11},{10,... | collective-permute-start | bytes 786440 | tf_op jit(solution)/shard_map/ppermute | solution.py:32
  160.9 10.1 %collective-permute-start.37 = (f32[1,4,64]{2,1,0:T(4,128)S(1)}, f32[1,4,64]{2,1,0:T(4,128)S(1)}, u32[]{:S(2)}, u32[]{:S(2)}) collective-permute-start(f32[1,4,64]{2,1,0:T(4,128)S(1)} %bitcast.148), channel_id=1, source_target_pairs={{0,4},{1,5},{2,6},{3,7},{4,0},{5,1},{6,2},{7,3},{8,12},{9,13},{10,... | collective-permute-start | bytes 3080 | tf_op jit(solution)/shard_map/ppermute | solution.py:32
  163.8 2.8 %copy-start.13 = (bf16[128,1024]{1,0:T(8,128)(2,1)}, bf16[128,1024]{1,0:T(8,128)(2,1)S(1)}, u32[]{:S(2)}) copy-start(bf16[128,1024]{1,0:T(8,128)(2,1)S(1)} %get-tuple-element.83) | copy-start | bytes 786436
  163.8 2.8 %copy-start.15 = (bf16[128,1024]{1,0:T(8,128)(2,1)}, bf16[128,1024]{1,0:T(8,128)(2,1)S(1)}, u32[]{:S(2)}) copy-start(bf16[128,1024]{1,0:T(8,128)(2,1)S(1)} %get-tuple-element.82) | copy-start | bytes 786436
  163.8 24.5 %collective-permute-start.23 = (bf16[2,256,768]{2,1,0:T(8,128)(2,1)}, bf16[2,256,768]{2,1,0:T(8,128)(2,1)}, u32[]{:S(2)}, u32[]{:S(2)}) collective-permute-start(bf16[2,256,768]{2,1,0:T(8,128)(2,1)} %bitcast.31), channel_id=1, source_target_pairs={{0,8},{8,0},{16,24},{24,16},{1,9},{9,1},{17,25},{25,17},{2,10},{10... | collective-permute-start | bytes 2359304 | tf_op jit(solution)/shard_map/ppermute | solution.py:32
  166.6 10.6 %copy-start.26 = (s32[128,8]{0,1:T(8,128)S(1)}, s32[128,8]{0,1:T(8,128)}, u32[]{:S(2)}) copy-start(s32[128,8]{0,1:T(8,128)} %param.10) | copy-start | bytes 12292
  166.6 10.6 %copy-start.28 = (s32[8]{0:T(128)S(1)}, s32[8]{0:T(128)}, u32[]{:S(2)}) copy-start(s32[8]{0:T(128)} %copy-done.27) | copy-start | bytes 100
  166.6 8.9 %collective-permute-start.25 = (bf16[128,1024]{1,0:T(8,128)(2,1)}, bf16[128,1024]{1,0:T(8,128)(2,1)S(1)}, u32[]{:S(2)}, u32[]{:S(2)}) collective-permute-start(bf16[128,1024]{1,0:T(8,128)(2,1)} %get-tuple-element.81), channel_id=1, source_target_pairs={{0,1},{1,0},{2,3},{3,2},{4,5},{5,4},{6,7},{7,6},{8,9},{9,8},{10,11... | collective-permute-start | bytes 786440 | tf_op jit(solution)/shard_map/ppermute | solution.py:32
  167.2 8.2 %copy-start.14 = (bf16[128,1024]{1,0:T(8,128)(2,1)S(1)}, bf16[128,1024]{1,0:T(8,128)(2,1)}, u32[]{:S(2)}) copy-start(bf16[128,1024]{1,0:T(8,128)(2,1)} %copy-done.13) | copy-start | bytes 786436
  167.2 29.1 %collective-permute-start.13 = (bf16[1,192,3072]{2,1,0:T(8,128)(2,1)}, bf16[1,192,3072]{2,1,0:T(8,128)(2,1)}, u32[]{:S(2)}, u32[]{:S(2)}) collective-permute-start(bf16[1,192,3072]{2,1,0:T(8,128)(2,1)} %fusion), channel_id=1, source_target_pairs={{0,16},{8,24},{16,0},{24,8},{1,17},{9,25},{17,1},{25,9},{2,18},{10... | collective-permute-start | bytes 3538952 | tf_op jit(solution)/shard_map/ppermute | solution.py:32
  167.8 3.9 %copy-start.16 = (bf16[128,1024]{1,0:T(8,128)(2,1)S(1)}, bf16[128,1024]{1,0:T(8,128)(2,1)}, u32[]{:S(2)}) copy-start(bf16[128,1024]{1,0:T(8,128)(2,1)} %copy-done.15) | copy-start | bytes 786436
  171.0 20.2 %collective-permute-start.18 = (bf16[2,256,768]{2,1,0:T(8,128)(2,1)}, bf16[2,256,768]{2,1,0:T(8,128)(2,1)}, u32[]{:S(2)}, u32[]{:S(2)}) collective-permute-start(bf16[2,256,768]{2,1,0:T(8,128)(2,1)} %bitcast.26), channel_id=1, source_target_pairs={{0,8},{8,0},{16,24},{24,16},{1,9},{9,1},{17,25},{25,17},{2,10},{10... | collective-permute-start | bytes 2359304 | tf_op jit(solution)/shard_map/ppermute | solution.py:32
  171.6 16.7 %copy-start.8 = (f32[512,768]{1,0:T(8,128)S(1)}, f32[512,768]{1,0:T(8,128)}, u32[]{:S(2)}) copy-start(f32[512,768]{1,0:T(8,128)} %copy-done.7) | copy-start | bytes 4718596
  171.8 9.2 %collective-permute-start.26 = (bf16[128,1024]{1,0:T(8,128)(2,1)S(1)}, bf16[128,1024]{1,0:T(8,128)(2,1)S(1)}, u32[]{:S(2)}, u32[]{:S(2)}) collective-permute-start(bf16[128,1024]{1,0:T(8,128)(2,1)S(1)} %copy-done.16), channel_id=1, source_target_pairs={{0,2},{1,3},{2,0},{3,1},{4,6},{5,7},{6,4},{7,5},{8,10},{9,11},{10,... | collective-permute-start | bytes 786440 | tf_op jit(solution)/shard_map/ppermute | solution.py:32
  175.4 11.4 %collective-permute-start.27 = (bf16[128,1024]{1,0:T(8,128)(2,1)S(1)}, bf16[128,1024]{1,0:T(8,128)(2,1)S(1)}, u32[]{:S(2)}, u32[]{:S(2)}) collective-permute-start(bf16[128,1024]{1,0:T(8,128)(2,1)S(1)} %copy-done.14), channel_id=1, source_target_pairs={{0,3},{1,2},{2,1},{3,0},{4,7},{5,6},{6,5},{7,4},{8,11},{9,10},{10,... | collective-permute-start | bytes 786440 | tf_op jit(solution)/shard_map/ppermute | solution.py:32
  186.9 4.4 %copy-start.10 = (f32[512,768]{1,0:T(8,128)S(1)}, f32[512,768]{1,0:T(8,128)}, u32[]{:S(2)}) copy-start(f32[512,768]{1,0:T(8,128)} %copy-done.9) | copy-start | bytes 4718596
  188.2 16.2 %collective-permute-start.28 = (bf16[2,256,768]{2,1,0:T(8,128)(2,1)S(1)}, bf16[2,256,768]{2,1,0:T(8,128)(2,1)S(1)}, u32[]{:S(2)}, u32[]{:S(2)}) collective-permute-start(bf16[2,256,768]{2,1,0:T(8,128)(2,1)S(1)} %bitcast.133), channel_id=1, source_target_pairs={{0,8},{8,0},{16,24},{24,16},{1,9},{9,1},{17,25},{25,17},{2,10},{10... | collective-permute-start | bytes 2359304 | tf_op jit(solution)/shard_map/ppermute | solution.py:32
  189.4 26.6 %collective-permute-start.24 = (bf16[1,256,768]{2,1,0:T(8,128)(2,1)S(1)}, bf16[1,256,768]{2,1,0:T(8,128)(2,1)S(1)}, u32[]{:S(2)}, u32[]{:S(2)}) collective-permute-start(bf16[1,256,768]{2,1,0:T(8,128)(2,1)S(1)} %fusion.11), channel_id=1, source_target_pairs={{0,16},{8,24},{16,0},{24,8},{1,17},{9,25},{17,1},{25,9},{2,18},{10... | collective-permute-start | bytes 1179656 | tf_op jit(solution)/shard_map/ppermute | solution.py:32
  192.3 24.8 %collective-permute-start.19 = (bf16[1,256,768]{2,1,0:T(8,128)(2,1)S(1)}, bf16[1,256,768]{2,1,0:T(8,128)(2,1)S(1)}, u32[]{:S(2)}, u32[]{:S(2)}) collective-permute-start(bf16[1,256,768]{2,1,0:T(8,128)(2,1)S(1)} %fusion.12), channel_id=1, source_target_pairs={{0,16},{8,24},{16,0},{24,8},{1,17},{9,25},{17,1},{25,9},{2,18},{10... | collective-permute-start | bytes 1179656 | tf_op jit(solution)/shard_map/ppermute | solution.py:32
  201.1 8.4 %collective-permute-start.30 = (bf16[128,1024]{1,0:T(8,128)(2,1)S(1)}, bf16[128,1024]{1,0:T(8,128)(2,1)S(1)}, u32[]{:S(2)}, u32[]{:S(2)}) collective-permute-start(bf16[128,1024]{1,0:T(8,128)(2,1)S(1)} %get-tuple-element.88), channel_id=1, source_target_pairs={{0,1},{1,0},{2,3},{3,2},{4,5},{5,4},{6,7},{7,6},{8,9},{9,8},{10,11... | collective-permute-start | bytes 786440 | tf_op jit(solution)/shard_map/ppermute | solution.py:32
  202.7 9.1 %collective-permute-start.31 = (bf16[128,1024]{1,0:T(8,128)(2,1)S(1)}, bf16[128,1024]{1,0:T(8,128)(2,1)S(1)}, u32[]{:S(2)}, u32[]{:S(2)}) collective-permute-start(bf16[128,1024]{1,0:T(8,128)(2,1)S(1)} %get-tuple-element.89), channel_id=1, source_target_pairs={{0,2},{1,3},{2,0},{3,1},{4,6},{5,7},{6,4},{7,5},{8,10},{9,11},{10,... | collective-permute-start | bytes 786440 | tf_op jit(solution)/shard_map/ppermute | solution.py:32
  204.4 10.2 %collective-permute-start.32 = (bf16[128,1024]{1,0:T(8,128)(2,1)S(1)}, bf16[128,1024]{1,0:T(8,128)(2,1)S(1)}, u32[]{:S(2)}, u32[]{:S(2)}) collective-permute-start(bf16[128,1024]{1,0:T(8,128)(2,1)S(1)} %get-tuple-element.90), channel_id=1, source_target_pairs={{0,3},{1,2},{2,1},{3,0},{4,7},{5,6},{6,5},{7,4},{8,11},{9,10},{10,... | collective-permute-start | bytes 786440 | tf_op jit(solution)/shard_map/ppermute | solution.py:32
  209.5 11.1 %collective-permute-start.29 = (bf16[1,256,768]{2,1,0:T(8,128)(2,1)S(1)}, bf16[1,256,768]{2,1,0:T(8,128)(2,1)S(1)}, u32[]{:S(2)}, u32[]{:S(2)}) collective-permute-start(bf16[1,256,768]{2,1,0:T(8,128)(2,1)S(1)} %fusion.10), channel_id=1, source_target_pairs={{0,16},{8,24},{16,0},{24,8},{1,17},{9,25},{17,1},{25,9},{2,18},{10... | collective-permute-start | bytes 1179656 | tf_op jit(solution)/shard_map/ppermute | solution.py:32
  215.9 4.9 %collective-permute-start.33 = (bf16[2,256,768]{2,1,0:T(8,128)(2,1)S(1)}, bf16[2,256,768]{2,1,0:T(8,128)(2,1)S(1)}, u32[]{:S(2)}, u32[]{:S(2)}) collective-permute-start(bf16[2,256,768]{2,1,0:T(8,128)(2,1)S(1)} %bitcast.134), channel_id=1, source_target_pairs={{0,8},{8,0},{16,24},{24,16},{1,9},{9,1},{17,25},{25,17},{2,10},{10... | collective-permute-start | bytes 2359304 | tf_op jit(solution)/shard_map/ppermute | solution.py:32
  218.3 3.1 %copy-start.20 = (f32[192,1024]{1,0:T(8,128)S(1)}, f32[192,1024]{1,0:T(8,128)}, u32[]{:S(2)}) copy-start(f32[192,1024]{1,0:T(8,128)} %convert_add_fusion.10) | copy-start | bytes 2359300
  220.9 10.3 %collective-permute-start.34 = (bf16[1,256,768]{2,1,0:T(8,128)(2,1)S(1)}, bf16[1,256,768]{2,1,0:T(8,128)(2,1)S(1)}, u32[]{:S(2)}, u32[]{:S(2)}) collective-permute-start(bf16[1,256,768]{2,1,0:T(8,128)(2,1)S(1)} %fusion.9), channel_id=1, source_target_pairs={{0,16},{8,24},{16,0},{24,8},{1,17},{9,25},{17,1},{25,9},{2,18},{10... | collective-permute-start | bytes 1179656 | tf_op jit(solution)/shard_map/ppermute | solution.py:32
  231.2 1.4 copy-start.1
  (3 other events, 2.8 us)

commit v2 on v0

v2 whole, which is shorter than its diff:
```python
import functools

import jax
import jax.numpy as jnp
from jax import lax
from jax.experimental import pallas as pl
from jax.experimental.pallas import tpu as pltpu
from jax.sharding import PartitionSpec as P

EXP_DEV = 4
DY_PARTS = 2
X_PARTS = 2
X_CHUNKS = 4
VMEM = 32 * 1024 * 1024
COST = 0.0


def cost(flops, size):
    return pl.CostEstimate(
        flops=int(COST * flops), bytes_accessed=int(COST * size), transcendentals=0
    )


def after(value, *deps):
    return lax.optimization_barrier((value, *deps))[0]


def swap(value, axis, bit):
    size = lax.axis_size(axis)
    return lax.ppermute(value, axis, [(i, i ^ bit) for i in range(size)])


def exchange(table, axis, bits):
    count = table.shape[0]
    for bit in bits:
        split = table.reshape(count // (2 * bit), 2, bit, table.shape[1])
        moved = swap(split[:, 1], axis, bit)
        table = jnp.stack([split[:, 0], moved], axis=1).reshape(table.shape)
    return table


def chip_sum(kept, sent):
    bit = 2
    if isinstance(sent, list):
        split = sent[0].shape[-1]
        halves = [
            chip_sum([k[:, i * split : (i + 1) * split] for k in kept], piece)
            for i, piece in enumerate(sent)
        ]
        return jnp.concatenate(halves, axis=1)
    while True:
        got = swap(sent, "dp", bit)
        kept = [kept[i] + got[i].astype(jnp.float32) for i in range(len(kept))]
        if len(kept) == 1:
            return kept[0]
        kept, sent = kept[0::2], jnp.stack(kept[1::2]).astype(jnp.bfloat16)
        bit *= 2


def slot_positions(table, capacity):
    tokens = table.shape[1]
    routed = table > 0
    earlier = (
        lax.broadcasted_iota(jnp.int32, (tokens, tokens), 0)
        < lax.broadcasted_iota(jnp.int32, (tokens, tokens), 1)
    )
    before = jnp.dot(
        jnp.where(routed, 1.0, 0.0).astype(jnp.bfloat16),
        jnp.where(earlier, 1.0, 0.0).astype(jnp.bfloat16),
        preferred_element_type=jnp.float32,
    ).astype(jnp.int32)
    return jnp.where(routed & (before < capacity), before, -1)


def place_kernel(blocks, peers, scaled, capacity, where, tables, *refs):
    rows = refs[:blocks]
    outs = refs[blocks : blocks + len(peers)]
    choices = refs[-1]
    tokens = tables.shape[2]
    cores = tables.shape[0] // blocks

    @pl.when(pl.program_id(0) == 0)
    def _():
        slot = lax.broadcasted_iota(jnp.int32, (capacity, tokens), 0)
        for s in range(tables.shape[0]):
            table = tables[s]
            position = slot_positions(table, capacity)
            value = table if scaled else jnp.where(table > 0, 1.0, 0.0)
            owner = lax.broadcasted_iota(jnp.int32, table.shape, 0)
            for n, k in enumerate(peers):
                mine = owner == (where[0] ^ k)
                wanted = jnp.sum(jnp.where(mine, position, 0), axis=0, keepdims=True)
                entry = jnp.sum(jnp.where(mine, value, 0.0), axis=0, keepdims=True)
                choices[s, n * capacity : (n + 1) * capacity, :] = jnp.where(
                    slot == wanted, entry, 0.0
                ).astype(jnp.bfloat16)

    for s in range(tables.shape[0]):
        first = (s % cores) * tokens
        placed = jnp.dot(
            choices[s],
            rows[s // cores][first : first + tokens, :],
            preferred_element_type=jnp.float32,
        ).astype(jnp.bfloat16)
        for n in range(len(peers)):
            outs[n][s * capacity : (s + 1) * capacity, :] = placed[
                n * capacity : (n + 1) * capacity, :
            ]


def place(where, tables, rows, maps, steps, width, peers, capacity, scaled):
    sources, owners, tokens = tables.shape
    out_shape = (sources * capacity, steps * width)
    return pl.pallas_call(
        functools.partial(place_kernel, len(rows), peers, scaled, capacity),
        grid_spec=pltpu.PrefetchScalarGridSpec(
            num_scalar_prefetch=1,
            grid=(steps,),
            in_specs=[pl.BlockSpec((sources, owners, tokens), lambda i, w: (0, 0, 0))]
            + [
                pl.BlockSpec((r.shape[0], width), functools.partial(lambda m, i, w: (0, m(i)), m))
                for r, m in zip(rows, maps)
            ],
            out_specs=[pl.BlockSpec((out_shape[0], width), lambda i, w: (0, i))] * len(peers),
            scratch_shapes=[pltpu.VMEM((sources, len(peers) * capacity, tokens), jnp.bfloat16)],
        ),
        out_shape=[jax.ShapeDtypeStruct(out_shape, jnp.bfloat16)] * len(peers),
        compiler_params=pltpu.CompilerParams(vmem_limit_bytes=VMEM),
        cost_estimate=cost(
            2 * len(peers) * out_shape[0] * out_shape[1] * tokens,
            2 * (len(peers) + 1) * out_shape[0] * out_shape[1],
        ),
        name="place",
    )(where, tables, *rows)


def down_kernel(count, hidden_t, *refs):
    dy = jnp.concatenate([ref[...] for ref in refs[:count]], axis=0)
    kept, sent = refs[count], refs[count + 1 :]
    middle = kept.shape[0]
    kept[...] = jnp.dot(hidden_t[:middle, :], dy, preferred_element_type=jnp.float32)
    other = jnp.dot(hidden_t[middle:, :], dy, preferred_element_type=jnp.float32)
    for n, out in enumerate(sent):

        @pl.when(pl.program_id(0) * len(sent) // pl.num_programs(0) == n)
        def _():
            out[...] = other.astype(jnp.bfloat16)


def down_step(hidden_t, near, far, pairs, share, first):
    hidden_width, slots = hidden_t.shape
    total = far[0].shape[1]
    width = share // 2
    steps = total // width
    column = lambda i: (0, i)
    middle = hidden_width // 2
    kept, *sent = pl.pallas_call(
        functools.partial(down_kernel, len(near) + len(far)),
        grid=(steps,),
        in_specs=[pl.BlockSpec((hidden_width, slots), lambda i: (0, 0))]
        + [pl.BlockSpec((piece.shape[0], width), lambda i: (0, 2 * first + i)) for piece in near]
        + [pl.BlockSpec((piece.shape[0], width), column) for piece in far],
        out_specs=[
            pl.BlockSpec((middle, width), column),
            pl.BlockSpec((middle, width), lambda i: (0, jnp.minimum(i, steps // 2 - 1))),
            pl.BlockSpec((middle, width), lambda i: (0, jnp.maximum(i - steps // 2, 0))),
        ],
        out_shape=[jax.ShapeDtypeStruct((middle, total), jnp.float32)]
        + [jax.ShapeDtypeStruct((middle, total // 2), jnp.bfloat16)] * 2,
        compiler_params=pltpu.CompilerParams(vmem_limit_bytes=VMEM),
        cost_estimate=cost(
            2 * slots * hidden_width * total, 2 * total * slots + 3 * total * hidden_width
        ),
        name="down_step",
    )(hidden_t, *near, *far)
    kept = kept.reshape(pairs, middle // pairs, total)
    sent = [piece.reshape(pairs, middle // pairs, total // 2) for piece in sent]
    return [kept[i] for i in range(pairs)], sent


def back_kernel(count, where, matrix, *refs):
    back = refs[-1]

    @pl.when(pl.program_id(0) == 0)
    def _():
        back[...] = jnp.zeros_like(back) if len(refs) == count + 1 else refs[count][...]

    dy = jnp.concatenate([ref[...] for ref in refs[:count]], axis=0)
    back[...] += lax.dot_general(
        dy, matrix[...], (((1,), (1,)), ((), ())), preferred_element_type=jnp.float32
    )


def back_step(where, matrix, near, far, share, first, back):
    hidden_width = matrix.shape[0]
    pieces = near + far
    total = far[0].shape[1]
    slots = sum(piece.shape[0] for piece in pieces)
    before = [] if back is None else [back]
    whole = pl.BlockSpec((slots, hidden_width), lambda i, w: (0, 0))
    return pl.pallas_call(
        functools.partial(back_kernel, len(pieces)),
        grid_spec=pltpu.PrefetchScalarGridSpec(
            num_scalar_prefetch=1,
            grid=(total // share,),
            in_specs=[pl.BlockSpec((hidden_width, share), lambda i, w: (0, w[1] % 2 + 2 * (first + i)))]
            + [pl.BlockSpec((piece.shape[0], share), lambda i, w: (0, first + i)) for piece in near]
            + [pl.BlockSpec((piece.shape[0], share), lambda i, w: (0, i)) for piece in far]
            + [whole] * len(before),
            out_specs=whole,
        ),
        out_shape=jax.ShapeDtypeStruct((slots, hidden_width), jnp.float32),
        compiler_params=pltpu.CompilerParams(vmem_limit_bytes=VMEM),
        cost_estimate=cost(
            2 * slots * hidden_width * total, 2 * total * (slots + hidden_width)
        ),
        name="back_step",
    )(where, matrix, *pieces, *before)


def up_kernel(count, grad_pre, *refs):
    even, odd = refs[:count], refs[count : 2 * count]
    kept, sent = refs[2 * count :]
    contract = (((0,), (0,)), ((), ()))
    for pieces, out in ((even, kept), (odd, sent)):
        x = jnp.concatenate([ref[...] for ref in pieces], axis=0)
        out[...] = lax.dot_general(
            x, grad_pre[...], contract, preferred_element_type=jnp.float32
        ).astype(out.dtype)


def up_step(grad_pre, pieces, chunk, per, chips):
    slots, hidden_width = grad_pre.shape
    width = pieces[0].shape[1] // (per * chips)
    rows = pieces[0].shape[0] // 2
    pairs = chips // 2
    pieces = pieces + pieces

    def specs(odd):
        out = []
        for n in range(len(pieces)):
            far = 2 * n // len(pieces)
            index = lambda i, far=far: (far, (2 * i + odd) * per + chunk)
            out.append(pl.BlockSpec((rows, width), index))
        return out

    kept, sent = pl.pallas_call(
        functools.partial(up_kernel, len(pieces)),
        grid=(pairs,),
        in_specs=[pl.BlockSpec((slots, hidden_width), lambda i: (0, 0))] + specs(0) + specs(1),
        out_specs=[pl.BlockSpec((width, hidden_width), lambda i: (i, 0))] * 2,
        out_shape=[
            jax.ShapeDtypeStruct((pairs * width, hidden_width), jnp.float32),
            jax.ShapeDtypeStruct((pairs * width, hidden_width), jnp.bfloat16),
        ],
        compiler_params=pltpu.CompilerParams(vmem_limit_bytes=VMEM),
        cost_estimate=cost(
            2 * slots * hidden_width * chips * width,
            2 * chips * width * slots + 3 * chips * width * hidden_width,
        ),
        name="up_step",
    )(grad_pre, *pieces, *pieces)
    kept = kept.reshape(pairs, width, hidden_width)
    return [kept[i] for i in range(pairs)], sent.reshape(pairs, width, hidden_width)


def pick(table, index):
    return lax.dynamic_index_in_dim(table, index, 0, keepdims=False)


def per_device(tokens, out_grad, probs, routes, saved_gate, saved_up, down_weight):
    owners = lax.axis_size("expert")
    groups = lax.axis_size("dp")
    me = lax.axis_index("expert")
    group = lax.axis_index("dp")
    where = jnp.stack([me, group]).astype(jnp.int32)
    half = owners // 2
    chips = groups // 2
    tok_count, model_width = tokens.shape
    slot_rows, hidden_width = saved_gate.shape
    capacity = slot_rows // owners
    share = model_width // groups
    peers = list(range(0, half, 2))

    core = group % 2
    def columns(rows, block, lo, hi):
        return lax.dynamic_slice_in_dim(rows, block * share + lo, hi - lo, 1)

    def both_cores(rows, blocks, lo, hi):
        mine = jnp.concatenate([columns(rows, b, lo, hi) for b in blocks], axis=1)
        other = jnp.concatenate([columns(rows, b ^ 1, lo, hi) for b in blocks], axis=1)
        return jnp.concatenate([mine, swap(other, "dp", 1)], axis=0)

    blocks = [2 * r + core for r in range(chips)]
    per_part = chips // DY_PARTS
    dy_own = both_cores(out_grad, [2 * r + core for r in range(chips)], 0, share)
    dy_parts = [
        dy_own[:, h * per_part * share : (h + 1) * per_part * share] for h in range(DY_PARTS)
    ]

    owner_ids = jnp.arange(owners, dtype=jnp.int32) * EXP_DEV
    named = routes.T[None, :, :] == owner_ids[:, None, None]
    table_own = jnp.sum(jnp.where(named, probs.T[None, :, :].astype(jnp.float32), 0.0), axis=1)
    tables_core = jnp.stack([table_own, swap(table_own, "dp", 1)])
    tables_next = swap(after(tables_core, dy_parts[0]), "expert", 1)
    tables_near = jnp.concatenate([tables_core, tables_next])
    tables_far = swap(tables_near, "expert", half)

    peers = list(range(0, half, 2))
    same = lambda i: i

    def spread(sent):
        return [sent[0]] + [swap(sent[n], "expert", peers[n]) for n in range(1, len(peers))]

    def place_rows(tables, rows, scaled, steps=None, width=None, index=same):
        width = width or share
        steps = steps or rows[0].shape[1] // width
        maps = [index] * len(rows)
        return place(where, tables, rows, maps, steps, width, peers, capacity, scaled)

    dy_next = swap(after(dy_own, tables_next), "expert", 1)
    dy_far0 = swap(dy_parts[0], "expert", half)
    dy_from_own = place_rows(tables_core, [after(dy_own, tables_next)], True)
    placed = dy_from_own[0]
    dy_from_own = spread(dy_from_own)
    dy_next, dy_far0, dy_from_own, tables_far, dy1 = lax.optimization_barrier(
        (dy_next, dy_far0, dy_from_own, tables_far, dy_parts[1])
    )

    dy_far1 = swap(dy1, "expert", half)
    dy_from_next = spread(place_rows(tables_next, [dy_next], True))
    dy_far_next0 = swap(dy_far0, "expert", 1)
    x_own = both_cores(tokens, [group ^ (2 * r) for r in range(chips)], 0, share)
    part_width = share // X_PARTS
    x_parts = [
        jnp.concatenate(
            [
                x_own[:, r * share + p * part_width : r * share + (p + 1) * part_width]
                for r in range(chips)
            ],
            axis=1,
        )
        for p in range(X_PARTS)
    ]
    order = me ^ jnp.arange(owners, dtype=jnp.int32)
    saved = jnp.stack([saved_gate, saved_up]).reshape(2, owners, capacity, hidden_width)[:, order]
    dy_far1, dy_from_next, dy_far_next0, x_parts, saved = lax.optimization_barrier(
        (dy_far1, dy_from_next, dy_far_next0, x_parts, saved)
    )
    dy_near = [piece for pair in zip(dy_from_own, dy_from_next) for piece in pair]

    x_far0 = swap(x_parts[0], "expert", half)
    dy_spread0 = spread(place_rows(tables_far, [dy_far0, dy_far_next0], True))
    dy_far_next1 = swap(dy_far1, "expert", 1)
    x_next0 = swap(x_parts[0], "expert", 1)
    saved = jnp.stack([after(saved, dy_far_next1), swap(saved, "dp", 1)], axis=2)
    saved = saved.reshape(2, 2 * slot_rows, hidden_width).astype(jnp.float32)
    gate_act = jax.nn.silu(saved[0])
    hidden = (gate_act * saved[1]).astype(jnp.bfloat16)
    block = hidden_width // groups
    hidden_t = hidden.T.reshape(groups, block, 2 * slot_rows)
    rows_order = [m for m in range(groups) if not m & 2] + [m for m in range(groups) if m & 2]
    hidden_t = jnp.concatenate([pick(hidden_t, group ^ m) for m in rows_order], axis=0)
    matrix = down_weight[0]
    x_far0, dy_spread0, dy_far_next1, x_next0, x_parts, hidden_t = lax.optimization_barrier(
        (x_far0, dy_spread0, dy_far_next1, x_next0, x_parts, hidden_t)
    )

    x_far1 = swap(x_parts[1], "expert", half)
    dy_spread1 = spread(place_rows(tables_far, [dy_far1, dy_far_next1], True))
    x_far_next0 = swap(x_far0, "expert", 1)
    x_next1 = swap(x_parts[1], "expert", 1)
    held = after(dy_near[0], dy_spread1[0])
    terms = down_step(hidden_t, [held] + dy_near[1:], dy_spread0, chips // 2, share, 0)
    terms_kept = terms[0][0]
    down = [chip_sum(*terms)]
    x_far1, dy_spread1, x_far_next0, x_next1, terms_kept = lax.optimization_barrier(
        (x_far1, dy_spread1, x_far_next0, x_next1, terms_kept)
    )

    width = share // X_CHUNKS
    per = X_CHUNKS // X_PARTS
    tables_all = jnp.concatenate([tables_near, tables_far])
    x_far_next1 = swap(x_far1, "expert", 1)
    rows = [x_parts[0], x_next0, x_far0, x_far_next0]
    x_spread0 = place_rows(tables_all, rows, False, chips, part_width)
    near = [after(dy_near[0], x_spread0[0], x_far_next1)] + dy_near[1:]
    x_spread0 = spread(x_spread0)
    terms = down_step(hidden_t, near, dy_spread1, chips // 2, share, per_part)
    near[0] = after(near[0], terms[0][0])
    down.append(chip_sum(*terms))
    back = back_step(where, matrix, near, dy_spread0, share, 0, None)
    back = back_step(where, matrix, near, dy_spread1, share, per_part, back)
    back = back.reshape(owners, 2, capacity, hidden_width)
    other = [swap(back[:, 1 - g].astype(jnp.bfloat16), "dp", 1) for g in range(2)]
    x_rows = [x_parts[1], x_next1, x_far1]
    x_far_next1, x_spread0 = lax.optimization_barrier((x_far_next1, x_spread0))
    x_spread1 = place_rows(
        tables_all, x_rows + [x_far_next1], False, chips, part_width
    )
    other[0] = after(other[0], x_spread1[0])
    back = jnp.stack([back[:, g] + other[g].astype(jnp.float32) for g in range(2)], axis=1)
    back = back.reshape(2 * slot_rows, hidden_width)
    grad_pre = (back * gate_act).astype(jnp.bfloat16)
    slot_grad = jnp.sum(
        (hidden.astype(jnp.float32) * back).reshape(owners, 2, capacity, hidden_width)[:, 0], axis=2
    )

    up_terms = [up_step(grad_pre, x_spread0, n, per, chips) for n in range(per)]
    up_parts = [chip_sum(*terms) for terms in up_terms]
    grad_pre = after(grad_pre, up_terms[-1][1])
    bits = [1 << n for n in range(owners.bit_length() - 1)]
    near_bits = [bit for bit in bits if bit in (1, half)]
    far_bits = [bit for bit in bits if bit not in (1, half)]
    returned = exchange(after(slot_grad, up_terms[-1][1]), "expert", near_bits)
    x_spread1 = spread(x_spread1)
    for n in range(per):
        grad_pre = after(grad_pre, up_parts[n], returned)
        up_terms.append(up_step(grad_pre, x_spread1, n, per, chips))
        grad_pre = after(grad_pre, up_terms[-1][1])
    up_parts += [chip_sum(*terms) for terms in up_terms[per:]]
    down_blocks = []
    for h in range(DY_PARTS):
        mine, other = down[h][:block], swap(after(down[h][block:], up_parts[0]), "dp", 1)
        for r in range(per_part):
            span = slice(r * share, (r + 1) * share)
            for c in range(2):
                down_blocks.append(jnp.where(core == c, mine[:, span], other[:, span]))
    down_share = jnp.concatenate(down_blocks, axis=1)
    returned = exchange(after(returned, up_parts[per]), "expert", far_bits)[order]
    position_own = slot_positions(table_own, capacity)
    chosen_own = (
        lax.broadcasted_iota(jnp.int32, (owners, capacity, tok_count), 1) == position_own[:, None, :]
    )
    token_grad = jnp.sum(jnp.where(chosen_own, returned[:, :, None], 0.0), axis=1)
    token_grad = jnp.where(
        position_own >= 0, token_grad / jnp.where(table_own > 0, table_own, 1.0), 0.0
    )
    prob_grad = jnp.sum(jnp.where(named, token_grad[:, None, :], 0.0), axis=0).T
    up_share = jnp.concatenate(up_parts, axis=0).astype(jnp.bfloat16)

    return down_share[None], up_share[None], prob_grad


def solution(mesh):
    in_specs = (
        P(("dp", "expert"), None),
        P(("dp", "expert"), None),
        P(("dp", "expert"), None),
        P(("dp", "expert"), None),
        P(("dp", "expert"), None),
        P(("dp", "expert"), None),
        P("expert", None, None),
    )
    out_specs = (P("expert", "dp", None), P("expert", "dp", None), P(("dp", "expert"), None))
    return jax.shard_map(
        per_device, mesh=mesh, in_specs=in_specs, out_specs=out_specs, check_vma=False
    )
```

time: 423 us -> 215 us (0.51)
  waiting for transfers between devices: 211 us -> 89 us
  blocking collectives: 98.9 us -> 0 us
  matrix products: 33.7 us -> 0.13 us
  Pallas kernels: 0 us -> 29.1 us
  starting transfers between devices: 16.8 us -> 41.6 us
  other arithmetic: 6.94 us -> 22.9 us
  between operations: 14.2 us -> 1.31 us
  local copies, waits for them, and re-layouts: 40.9 us -> 30.1 us
    reduce_scatter x2 -> x0, waiting for transfers between devices: 120 us -> none  [the longest x1 102 us: per_device(): lax.psum_scatter(lax.dot_general(column_block, scaled, (((0,), (0,)), (()...]
    all_to_all x1 -> x0, blocking collectives: 98.9 us -> none  [per_device(): lax.all_to_all(send_dy, 'expert', split_axis=0, concat_axis=0, tiled=True)]
    all_to_all x3 -> x0, waiting for transfers between devices: 90.5 us -> none  [the longest x1 84.1 us: per_device(): lax.all_to_all(send_x, 'expert', split_axis=0, concat_axis=0, tiled=True)]
    ppermute x0 -> x38, waiting for transfers between devices: none -> 89 us  [swap(): return lax.ppermute(value, axis, [(i, i ^ bit) for i in range(size)])]
    ppermute x0 -> x38, starting transfers between devices: none -> 41.6 us  [swap(): return lax.ppermute(value, axis, [(i, i ^ bit) for i in range(size)])]
    dot_general x4 -> x1, matrix products: 33.7 us -> 0.13 us  [slot_positions(): jnp.dot(jnp.where(routed, 1.0, 0.0).astype(jnp.bfloat16), jnp.where(earli...]
    pallas_call x0 -> x14, Pallas kernels: none -> 29.1 us  [the longest x6 14.4 us: place(): pl.pallas_call(functools.partial(place_kernel, len(rows), peers, scaled,...]
    gather x7 -> x2, local copies, waits for them, and re-layouts: 22.9 us -> 3.75 us  [the longest x1 3.2 us: per_device(): jnp.stack([saved_gate, saved_up]).reshape(2, owners, capacity, hidden_width)]
  transfers between devices with their start and end apart: 5 -> 38, of which waited for: 4 -> 19; matrix products, arithmetic and copies ran while one was open for 13% -> 18% of each run, Pallas kernels for 0% -> 13%
where the time goes in v2:
time: 215 us; the launch traced here: 214 us
  waiting for transfers between devices  89 us (41%)
  starting transfers between devices  41.6 us (19%)
  local copies, waits for them, and re-layouts  30.1 us (14%)
  Pallas kernels  29.1 us (14%)
  other arithmetic  22.9 us (11%)
    ppermute x38, waiting for transfers between devices, swap(): return lax.ppermute(value, axis, [(i, i ^ bit) for i in range(size)])  89 us
    ppermute x38, starting transfers between devices, swap(): return lax.ppermute(value, axis, [(i, i ^ bit) for i in range(size)])  41.6 us
    pallas_call x6, Pallas kernels, place(): pl.pallas_call(functools.partial(place_kernel, len(rows), peers, scaled,...  14.4 us
    unnamed x73, local copies, waits for them, and re-layouts  11.6 us
    pallas_call x2, Pallas kernels, down_step(): pl.pallas_call(functools.partial(down_kernel, len(near) + len(far)), grid...  5.91 us
    pallas_call x2, Pallas kernels, back_step(): pl.pallas_call(functools.partial(back_kernel, len(pieces)), grid_spec=plt...  4.73 us
  transfers between devices with their start and end apart: 38, of which 19 were waited for; matrix products, arithmetic and copies ran while one was open for 18% of the time, Pallas kernels for 13%

profile of v2, /device:TPU:0, one launch (start us, length us, event | category | flops | bytes accessed | tf_op | source)
XLA Modules:
  0.0 214.1 jit_solution(17054383190424696572)
XLA Ops:
  0.7 1.3 constant_dynamic-slice_fusion.7
  2.8 1.3 collective-permute-done.1
  5.2 2.9 %collective-permute-start.2 = (f32[2,8,128]{2,1,0:T(8,128)S(1)}, f32[2,8,128]{2,1,0:T(8,128)S(1)}, u32[]{:S(2)}, u32[]{:S(2)}) collective-permute-start(f32[2,8,128]{2,1,0:T(8,128)S(1)} %pad_maximum_fusion.14.tables), channel_id=1, source_target_pairs={{0,1},{1,0},{2,3},{3,2},{4,5},{5,4},{6,7},{7,6},{8,9},{9,8},{10,11... | collective-permute-start | bytes 24584 | tf_op jit(solution)/shard_map/ppermute | solution.py:30
  8.1 1.6 collective-permute-done.2.tables
  9.7 2.0 collective-permute-start.3
  11.8 2.0 constant_dynamic-slice_fusion.3
  13.8 2.6 %collective-permute-start.4 = (bf16[256,1024]{1,0:T(8,128)(2,1)}, bf16[256,1024]{1,0:T(8,128)(2,1)}, u32[]{:S(2)}, u32[]{:S(2)}) collective-permute-start(bf16[256,1024]{1,0:T(8,128)(2,1)} %get-tuple-element.172), channel_id=1, source_target_pairs={{0,4},{1,5},{2,6},{3,7},{4,0},{5,1},{6,2},{7,3},{8,12},{9,13},{10,... | collective-permute-start | bytes 1572872 | tf_op jit(solution)/shard_map/ppermute | solution.py:30
  16.4 2.1 place.6
  18.5 1.6 collective-permute-start.5
  20.9 2.7 %pad_maximum_fusion.1 = bf16[2,8,64,768]{3,2,1,0:T(8,128)(2,1)} fusion(bf16[1,8,64,768]{3,2,1,0:T(8,128)(2,1)} %bitcast.157, bf16[1,8,64,768]{3,2,1,0:T(8,128)(2,1)} %bitcast.158), kind=kLoop, calls=%fused_computation.28 | loop fusion | flops 786432 | bytes 3145728 | tf_op jit(solution)/shard_map/stack | solution.py:346
  23.9 3.2 %gather_fusion = bf16[8,2,64,768]{3,2,1,0:T(8,128)(2,1)} fusion(bf16[2,8,64,768]{3,2,1,0:T(8,128)(2,1)} %pad_maximum_fusion.1, s32[1024]{0:T(1024)S(1)} %pad_clamp_fusion), kind=kCustom, calls=%fused_computation | custom fusion | bytes 3145760 | tf_op jit(solution)/shard_map/gather | solution.py:346
  27.1 12.2 %collective-permute-done.6.tables = f32[4,8,128]{2,1,0:T(8,128)S(1)} collective-permute-done((f32[4,8,128]{2,1,0:T(8,128)S(1)}, f32[4,8,128]{2,1,0:T(8,128)S(1)}, u32[]{:S(2)}, u32[]{:S(2)}) %collective-permute-start.6) | collective-permute-done | bytes 16416 | tf_op jit(solution)/shard_map/ppermute | solution.py:30
  39.3 2.1 collective-permute-done.5.refs_2_
  41.4 1.4 place.7
  43.0 2.9 %collective-permute-start.7 = (bf16[256,1024]{1,0:T(8,128)(2,1)}, bf16[256,1024]{1,0:T(8,128)(2,1)}, u32[]{:S(2)}, u32[]{:S(2)}) collective-permute-start(bf16[256,1024]{1,0:T(8,128)(2,1)} %get-tuple-element.77), channel_id=1, source_target_pairs={{0,4},{1,5},{2,6},{3,7},{4,0},{5,1},{6,2},{7,3},{8,12},{9,13},{10,... | collective-permute-start | bytes 1572872 | tf_op jit(solution)/shard_map/ppermute | solution.py:30
  46.4 1.2 pad_maximum_fusion.5
  48.9 15.6 %collective-permute-done.8.refs_3_ = bf16[128,2048]{1,0:T(8,128)(2,1)S(1)} collective-permute-done((bf16[128,2048]{1,0:T(8,128)(2,1)S(1)}, bf16[128,2048]{1,0:T(8,128)(2,1)S(1)}, u32[]{:S(2)}, u32[]{:S(2)}) %collective-permute-start.8) | collective-permute-done | bytes 524320 | tf_op jit(solution)/shard_map/ppermute | solution.py:30
  64.5 4.0 %collective-permute-done.7.refs_0_ = bf16[256,1024]{1,0:T(8,128)(2,1)} collective-permute-done((bf16[256,1024]{1,0:T(8,128)(2,1)}, bf16[256,1024]{1,0:T(8,128)(2,1)}, u32[]{:S(2)}, u32[]{:S(2)}) %collective-permute-start.7) | collective-permute-done | bytes 524320 | tf_op jit(solution)/shard_map/ppermute | solution.py:30
  69.0 1.5 collective-permute-start.14
  70.5 3.0 %place.8 = (bf16[256,1024]{1,0:T(8,128)(2,1)S(1)}, bf16[256,1024]{1,0:T(8,128)(2,1)}) custom-call(s32[2]{0:T(128)S(1)} %pad_add_fusion.where, f32[4,8,128]{2,1,0:T(8,128)S(1)} %collective-permute-done.6.tables, bf16[256,1024]{1,0:T(8,128)(2,1)} %collective-permute-done.4.refs_0_, bf16[256,1024]{1,0:T(8,128)(2,1)S(1)} %collective-permute-done.9.refs_1_), custom_call_target="tpu_custom_call" | custom-call | tf_op jit(solution)/shard_map/place/pallas_call | solution.py:114
  73.4 3.0 %collective-permute-start.12 = (bf16[256,1024]{1,0:T(8,128)(2,1)}, bf16[256,1024]{1,0:T(8,128)(2,1)S(1)}, u32[]{:S(2)}, u32[]{:S(2)}) collective-permute-start(bf16[256,1024]{1,0:T(8,128)(2,1)} %get-tuple-element.86), channel_id=1, source_target_pairs={{0,2},{1,3},{2,0},{3,1},{4,6},{5,7},{6,4},{7,5},{8,10},{9,11},{10,... | collective-permute-start | bytes 1572872 | tf_op jit(solution)/shard_map/ppermute | solution.py:30
  76.4 7.1 %collective-permute-done.13.refs_1_ = bf16[256,1024]{1,0:T(8,128)(2,1)} collective-permute-done((bf16[256,1024]{1,0:T(8,128)(2,1)}, bf16[256,1024]{1,0:T(8,128)(2,1)}, u32[]{:S(2)}, u32[]{:S(2)}) %collective-permute-start.13) | collective-permute-done | bytes 524320 | tf_op jit(solution)/shard_map/ppermute | solution.py:30
  83.5 2.3 %maximum_convert_fusion = f32[2,8,2,64,768]{4,3,0,1,2:T(8,128)S(1)} fusion(bf16[2,8,1,64,768]{4,3,0,1,2:T(8,128)(2,1)} %bitcast.11, bf16[2,8,1,64,768]{4,3,0,1,2:T(8,128)(2,1)} %bitcast.10), kind=kLoop, calls=%fused_computation.5 | loop fusion | flops 3145728 | bytes 9437184 | tf_op jit(solution)/shard_map/convert_element_type | solution.py:357
  85.8 4.0 %slice_bitcast_fusion = (f32[8,2,64,768]{3,2,0,1:T(8,128)}, f32[8,2,64,768]{3,2,0,1:T(8,128)}, f32[1,8,2,64,768]{4,3,0,1,2:T(8,128)S(1)}, f32[1,8,2,64,768]{4,3,1,2,0:T(8,128)S(1)}) fusion(f32[2,8,2,64,768]{4,3,0,1,2:T(8,128)S(1)} %maximum_convert_fusion), kind=kLoop, calls=%fused_computation.17 | loop fusion | bytes 18874368 | tf_op jit(solution)/shard_map/squeeze | solution.py:358
  91.0 1.5 copy-done.28
  92.4 2.1 fusion.1
  94.5 2.6 %copy.44 = bf16[768,1024]{1,0:T(8,128)(2,1)} copy(bf16[768,1024]{0,1:T(8,128)(2,1)} %bitcast.153) | data formatting | bytes 3145728 | tf_op jit(solution)/shard_map/transpose | solution.py:361
  97.1 1.5 dynamic-slice_bitcast_fusion.3
  99.5 2.3 %place.9 = (bf16[256,1024]{1,0:T(8,128)(2,1)S(1)}, bf16[256,1024]{1,0:T(8,128)(2,1)S(1)}) custom-call(s32[2]{0:T(128)S(1)} %pad_add_fusion.where, f32[4,8,128]{2,1,0:T(8,128)S(1)} %collective-permute-done.6.tables, bf16[256,1024]{1,0:T(8,128)(2,1)} %collective-permute-done.7.refs_0_, bf16[256,1024]{1,0:T(8,128)(2,1)} %collective-permute-done.13.refs_1_), custom_call_target="tpu_custom_call" | custom-call | tf_op jit(solution)/shard_map/place/pallas_call | solution.py:114
  102.6 1.5 collective-permute-start.21
  104.1 2.7 %collective-permute-start.18 = (bf16[256,1024]{1,0:T(8,128)(2,1)S(1)}, bf16[256,1024]{1,0:T(8,128)(2,1)S(1)}, u32[]{:S(2)}, u32[]{:S(2)}) collective-permute-start(bf16[256,1024]{1,0:T(8,128)(2,1)S(1)} %copy-done.11), channel_id=1, source_target_pairs={{0,4},{1,5},{2,6},{3,7},{4,0},{5,1},{6,2},{7,3},{8,12},{9,13},{10,... | collective-permute-start | bytes 1572872 | tf_op jit(solution)/shard_map/ppermute | solution.py:30
  106.8 3.4 %down_step.2 = (f32[384,1024]{1,0:T(8,128)S(1)}, bf16[384,512]{1,0:T(8,128)(2,1)}, bf16[384,512]{1,0:T(8,128)(2,1)}) custom-call(bf16[768,1024]{1,0:T(8,128)(2,1)S(1)} %pad_maximum_fusion.2.hidden_t, bf16[128,2048]{1,0:T(8,128)(2,1)S(1)} %get-tuple-element.116.refs_0_, bf16[128,2048]{1,0:T(8,128)(2,1)S(1)} %get-tuple-element.96.refs_1_, ...), custom_call_target="tpu_custom_call" | custom-call | tf_op jit(solution)/shard_map/down_step/pallas_call | solution.py:157
  110.2 14.3 %collective-permute-done.19.refs_5_ = bf16[256,1024]{1,0:T(8,128)(2,1)S(1)} collective-permute-done((bf16[256,1024]{1,0:T(8,128)(2,1)S(1)}, bf16[256,1024]{1,0:T(8,128)(2,1)S(1)}, u32[]{:S(2)}, u32[]{:S(2)}) %collective-permute-start.19) | collective-permute-done | bytes 524320 | tf_op jit(solution)/shard_map/ppermute | solution.py:30
  124.5 2.2 %collective-permute-done.21.refs_1_ = bf16[256,1024]{1,0:T(8,128)(2,1)S(1)} collective-permute-done((bf16[256,1024]{1,0:T(8,128)(2,1)S(1)}, bf16[256,1024]{1,0:T(8,128)(2,1)S(1)}, u32[]{:S(2)}, u32[]{:S(2)}) %collective-permute-start.21) | collective-permute-done | bytes 524320 | tf_op jit(solution)/shard_map/ppermute | solution.py:30
  127.4 1.4 collective-permute-done.18.refs_2_
  129.4 1.5 collective-permute-start.17
  131.4 3.7 %place.10 = (bf16[512,1024]{1,0:T(8,128)(2,1)S(1)}, bf16[512,1024]{1,0:T(8,128)(2,1)}) custom-call(s32[2]{0:T(128)S(1)} %pad_add_fusion.where, f32[8,8,128]{2,1,0:T(8,128)S(1)} %pad_maximum_fusion.12.tables, bf16[256,1024]{1,0:T(8,128)(2,1)} %get-tuple-element.104.refs_0_, bf16[256,1024]{1,0:T(8,128)(2,1)} %collective-permute-done.14.refs_1_, ...), custom_call_target="tpu_custom_call" | custom-call | tf_op jit(solution)/shard_map/place/pallas_call | solution.py:114
  135.4 4.3 %collective-permute-done.22.refs_3_ = bf16[256,1024]{1,0:T(8,128)(2,1)S(1)} collective-permute-done((bf16[256,1024]{1,0:T(8,128)(2,1)S(1)}, bf16[256,1024]{1,0:T(8,128)(2,1)S(1)}, u32[]{:S(2)}, u32[]{:S(2)}) %collective-permute-start.22) | collective-permute-done | bytes 524320 | tf_op jit(solution)/shard_map/ppermute | solution.py:30
  139.6 1.2 copy-done.3
  141.9 2.5 %down_step.3 = (f32[384,1024]{1,0:T(8,128)S(1)}, bf16[384,512]{1,0:T(8,128)(2,1)S(1)}, bf16[384,512]{1,0:T(8,128)(2,1)S(1)}) custom-call(bf16[768,1024]{1,0:T(8,128)(2,1)S(1)} %pad_maximum_fusion.2.hidden_t, bf16[128,2048]{1,0:T(8,128)(2,1)S(1)} %get-tuple-element.116.refs_0_, bf16[128,2048]{1,0:T(8,128)(2,1)S(1)} %copy-done.3, ...), custom_call_target="tpu_custom_call" | custom-call | tf_op jit(solution)/shard_map/down_step/pallas_call | solution.py:157
  145.7 2.4 %back_step.2.refs_6_ = f32[1024,768]{1,0:T(8,128)S(1)} custom-call(s32[2]{0:T(128)S(1)} %pad_add_fusion.where, bf16[768,4096]{1,0:T(8,128)(2,1)S(1)} %bitcast.142, bf16[128,2048]{1,0:T(8,128)(2,1)S(1)} %get-tuple-element.116.refs_0_, bf16[128,2048]{1,0:T(8,128)(2,1)S(1)} %copy-done.4, bf16[128,2048]{1,0:T(8,128)(2,1)S(1)} %collective-permute-done.5.refs_2_, ...), custom_call_target="tpu_custom_call" | custom-call | tf_op jit(solution)/shard_map/back_step/pallas_call | solution.py:201
  148.1 2.4 %back_step.3 = f32[1024,768]{1,0:T(8,128)S(1)} custom-call(s32[2]{0:T(128)S(1)} %pad_add_fusion.where, bf16[768,4096]{1,0:T(8,128)(2,1)S(1)} %bitcast.143, bf16[128,2048]{1,0:T(8,128)(2,1)S(1)} %get-tuple-element.116.refs_0_, bf16[128,2048]{1,0:T(8,128)(2,1)S(1)} %copy-done.4, bf16[128,2048]{1,0:T(8,128)(2,1)S(1)} %collective-permute-done.5.refs_2_, ...), custom_call_target="tpu_custom_call" | custom-call | tf_op jit(solution)/shard_map/back_step/pallas_call | solution.py:201
  150.5 1.6 copy-done
  152.1 1.4 fusion.10
  154.1 2.5 %exponential_add_fusion = f32[8,2,64,768]{3,2,0,1:T(8,128)S(1)} fusion(f32[2,8,2,64,768]{4,3,0,1,2:T(8,128)} %copy-done.27), kind=kLoop, calls=%fused_computation.16 | loop fusion | flops 1572864 | bytes 6291456 | tf_op jit(solution)/shard_map/jit(silu)/add | solution.py:358
  156.7 1.5 convert_add_fusion.7
  158.2 1.6 collective-permute-start.29
  160.3 1.9 place.11
  162.2 1.5 collective-permute-start.34
  163.7 1.7 add_bitcast_fusion.1
  166.1 1.6 copy-done.29
  173.7 1.6 collective-permute-start.26
  175.6 2.4 %collective-permute-start.33 = (f32[1,4,64]{2,1,0:T(4,128)S(1)}, f32[1,4,64]{2,1,0:T(4,128)S(1)}, u32[]{:S(2)}, u32[]{:S(2)}) collective-permute-start(f32[1,4,64]{2,1,0:T(4,128)S(1)} %get-tuple-element.180), channel_id=1, source_target_pairs={{0,4},{1,5},{2,6},{3,7},{4,0},{5,1},{6,2},{7,3},{8,12},{9,13},{10,... | collective-permute-start | bytes 3080 | tf_op jit(solution)/shard_map/ppermute | solution.py:30
  178.9 1.6 collective-permute-start.31
  180.5 5.3 %collective-permute-done.33 = f32[1,4,64]{2,1,0:T(4,128)S(1)} collective-permute-done((f32[1,4,64]{2,1,0:T(4,128)S(1)}, f32[1,4,64]{2,1,0:T(4,128)S(1)}, u32[]{:S(2)}, u32[]{:S(2)}) %collective-permute-start.33) | collective-permute-done | bytes 1056 | tf_op jit(solution)/shard_map/ppermute | solution.py:30
  185.8 1.3 collective-permute-done.26
  188.3 1.6 collective-permute-start.35
  190.2 5.3 %collective-permute-done.31 = bf16[1,256,768]{2,1,0:T(8,128)(2,1)S(1)} collective-permute-done((bf16[1,256,768]{2,1,0:T(8,128)(2,1)S(1)}, bf16[1,256,768]{2,1,0:T(8,128)(2,1)S(1)}, u32[]{:S(2)}, u32[]{:S(2)}) %collective-permute-start.31) | collective-permute-done | bytes 393248 | tf_op jit(solution)/shard_map/ppermute | solution.py:30
  196.6 1.6 collective-permute-start.36
  198.2 5.7 %collective-permute-done.35 = bf16[1,256,768]{2,1,0:T(8,128)(2,1)S(1)} collective-permute-done((bf16[1,256,768]{2,1,0:T(8,128)(2,1)S(1)}, bf16[1,256,768]{2,1,0:T(8,128)(2,1)S(1)}, u32[]{:S(2)}, u32[]{:S(2)}) %collective-permute-start.35) | collective-permute-done | bytes 393248 | tf_op jit(solution)/shard_map/ppermute | solution.py:30
  204.0 1.5 collective-permute-start.37
  205.8 2.0 maximum_bitcast_fusion
  207.8 3.6 %collective-permute-done.36 = bf16[1,256,768]{2,1,0:T(8,128)(2,1)S(1)} collective-permute-done((bf16[1,256,768]{2,1,0:T(8,128)(2,1)S(1)}, bf16[1,256,768]{2,1,0:T(8,128)(2,1)S(1)}, u32[]{:S(2)}, u32[]{:S(2)}) %collective-permute-start.36) | collective-permute-done | bytes 393248 | tf_op jit(solution)/shard_map/ppermute | solution.py:30
  211.5 1.2 pad_maximum_fusion.3
  (159 shorter events, 26.2 us)
Async XLA Ops:
  2.0 2.1 collective-permute-start
  2.6 1.4 collective-permute-start.1
  5.2 4.5 %collective-permute-start.2 = (f32[2,8,128]{2,1,0:T(8,128)S(1)}, f32[2,8,128]{2,1,0:T(8,128)S(1)}, u32[]{:S(2)}, u32[]{:S(2)}) collective-permute-start(f32[2,8,128]{2,1,0:T(8,128)S(1)} %pad_maximum_fusion.14.tables), channel_id=1, source_target_pairs={{0,1},{1,0},{2,3},{3,2},{4,5},{5,4},{6,7},{7,6},{8,9},{9,8},{10,11... | collective-permute-start | bytes 24584 | tf_op jit(solution)/shard_map/ppermute | solution.py:30
  9.7 31.7 %collective-permute-start.3 = (bf16[256,2048]{1,0:T(8,128)(2,1)S(1)}, bf16[256,2048]{1,0:T(8,128)(2,1)S(1)}, u32[]{:S(2)}, u32[]{:S(2)}) collective-permute-start(bf16[256,2048]{1,0:T(8,128)(2,1)S(1)} %pad_maximum_fusion.4.refs_0_), channel_id=1, source_target_pairs={{0,1},{1,0},{2,3},{3,2},{4,5},{5,4},{6,7},{7,6},{8,9},{9,8},{10,11... | collective-permute-start | bytes 3145736 | tf_op jit(solution)/shard_map/ppermute | solution.py:30
  13.8 25.5 %collective-permute-start.4 = (bf16[256,1024]{1,0:T(8,128)(2,1)}, bf16[256,1024]{1,0:T(8,128)(2,1)}, u32[]{:S(2)}, u32[]{:S(2)}) collective-permute-start(bf16[256,1024]{1,0:T(8,128)(2,1)} %get-tuple-element.172), channel_id=1, source_target_pairs={{0,4},{1,5},{2,6},{3,7},{4,0},{5,1},{6,2},{7,3},{8,12},{9,13},{10,... | collective-permute-start | bytes 1572872 | tf_op jit(solution)/shard_map/ppermute | solution.py:30
  18.5 22.9 %collective-permute-start.5 = (bf16[128,2048]{1,0:T(8,128)(2,1)}, bf16[128,2048]{1,0:T(8,128)(2,1)S(1)}, u32[]{:S(2)}, u32[]{:S(2)}) collective-permute-start(bf16[128,2048]{1,0:T(8,128)(2,1)} %get-tuple-element.76), channel_id=1, source_target_pairs={{0,2},{1,3},{2,0},{3,1},{4,6},{5,7},{6,4},{7,5},{8,10},{9,11},{10,... | collective-permute-start | bytes 1572872 | tf_op jit(solution)/shard_map/ppermute | solution.py:30
  20.9 25.5 %collective-permute-start.10 = (bf16[128,2048]{1,0:T(8,128)(2,1)}, bf16[128,2048]{1,0:T(8,128)(2,1)}, u32[]{:S(2)}, u32[]{:S(2)}) collective-permute-start(bf16[128,2048]{1,0:T(8,128)(2,1)} %pad_maximum_fusion.9), channel_id=1, source_target_pairs={{0,8},{8,0},{16,24},{24,16},{1,9},{9,1},{17,25},{25,17},{2,10},{10... | collective-permute-start | bytes 1572872 | tf_op jit(solution)/shard_map/ppermute | solution.py:30
  23.6 15.7 %collective-permute-start.6 = (f32[4,8,128]{2,1,0:T(8,128)S(1)}, f32[4,8,128]{2,1,0:T(8,128)S(1)}, u32[]{:S(2)}, u32[]{:S(2)}) collective-permute-start(f32[4,8,128]{2,1,0:T(8,128)S(1)} %pad_maximum_fusion.13), channel_id=1, source_target_pairs={{0,4},{1,5},{2,6},{3,7},{4,0},{5,1},{6,2},{7,3},{8,12},{9,13},{10,... | collective-permute-start | bytes 49160 | tf_op jit(solution)/shard_map/ppermute | solution.py:30
  42.9 63.9 %copy-start.2 = (bf16[128,2048]{1,0:T(8,128)(2,1)}, bf16[128,2048]{1,0:T(8,128)(2,1)S(1)}, u32[]{:S(2)}) copy-start(bf16[128,2048]{1,0:T(8,128)(2,1)S(1)} %get-tuple-element.96.refs_1_) | copy-start | bytes 1572868
  42.9 21.6 %collective-permute-start.8 = (bf16[128,2048]{1,0:T(8,128)(2,1)S(1)}, bf16[128,2048]{1,0:T(8,128)(2,1)S(1)}, u32[]{:S(2)}, u32[]{:S(2)}) collective-permute-start(bf16[128,2048]{1,0:T(8,128)(2,1)S(1)} %get-tuple-element.80), channel_id=1, source_target_pairs={{0,2},{1,3},{2,0},{3,1},{4,6},{5,7},{6,4},{7,5},{8,10},{9,11},{10,... | collective-permute-start | bytes 1572872 | tf_op jit(solution)/shard_map/ppermute | solution.py:30
  43.0 25.5 %collective-permute-start.7 = (bf16[256,1024]{1,0:T(8,128)(2,1)}, bf16[256,1024]{1,0:T(8,128)(2,1)}, u32[]{:S(2)}, u32[]{:S(2)}) collective-permute-start(bf16[256,1024]{1,0:T(8,128)(2,1)} %get-tuple-element.77), channel_id=1, source_target_pairs={{0,4},{1,5},{2,6},{3,7},{4,0},{5,1},{6,2},{7,3},{8,12},{9,13},{10,... | collective-permute-start | bytes 1572872 | tf_op jit(solution)/shard_map/ppermute | solution.py:30
  45.9 22.6 %collective-permute-start.9 = (bf16[256,1024]{1,0:T(8,128)(2,1)}, bf16[256,1024]{1,0:T(8,128)(2,1)S(1)}, u32[]{:S(2)}, u32[]{:S(2)}) collective-permute-start(bf16[256,1024]{1,0:T(8,128)(2,1)} %collective-permute-done.4.refs_0_), channel_id=1, source_target_pairs={{0,1},{1,0},{2,3},{3,2},{4,5},{5,4},{6,7},{7,6},{8,9},{9,8},{10,11... | collective-permute-start | bytes 1572872 | tf_op jit(solution)/shard_map/ppermute | solution.py:30
  64.5 42.3 %copy-start.5 = (bf16[128,2048]{1,0:T(8,128)(2,1)}, bf16[128,2048]{1,0:T(8,128)(2,1)S(1)}, u32[]{:S(2)}) copy-start(bf16[128,2048]{1,0:T(8,128)(2,1)S(1)} %collective-permute-done.8.refs_3_) | copy-start | bytes 1572868
  68.4 15.0 %collective-permute-start.15 = (bf16[2,8,64,768]{3,2,0,1:T(8,128)(2,1)}, bf16[2,8,64,768]{3,2,0,1:T(8,128)(2,1)}, u32[]{:S(2)}, u32[]{:S(2)}) collective-permute-start(bf16[2,8,64,768]{3,2,0,1:T(8,128)(2,1)} %bitcast.9), channel_id=1, source_target_pairs={{0,8},{8,0},{16,24},{24,16},{1,9},{9,1},{17,25},{25,17},{2,10},{10... | collective-permute-start | bytes 4718600 | tf_op jit(solution)/shard_map/ppermute | solution.py:30
  68.5 15.0 %collective-permute-start.13 = (bf16[256,1024]{1,0:T(8,128)(2,1)}, bf16[256,1024]{1,0:T(8,128)(2,1)}, u32[]{:S(2)}, u32[]{:S(2)}) collective-permute-start(bf16[256,1024]{1,0:T(8,128)(2,1)} %collective-permute-done.7.refs_0_), channel_id=1, source_target_pairs={{0,1},{1,0},{2,3},{3,2},{4,5},{5,4},{6,7},{7,6},{8,9},{9,8},{10,11... | collective-permute-start | bytes 1572872 | tf_op jit(solution)/shard_map/ppermute | solution.py:30
  69.0 30.5 %collective-permute-start.14 = (bf16[256,1024]{1,0:T(8,128)(2,1)}, bf16[256,1024]{1,0:T(8,128)(2,1)}, u32[]{:S(2)}, u32[]{:S(2)}) collective-permute-start(bf16[256,1024]{1,0:T(8,128)(2,1)} %get-tuple-element.104.refs_0_), channel_id=1, source_target_pairs={{0,1},{1,0},{2,3},{3,2},{4,5},{5,4},{6,7},{7,6},{8,9},{9,8},{10,11... | collective-permute-start | bytes 1572872 | tf_op jit(solution)/shard_map/ppermute | solution.py:30
  70.5 29.1 %collective-permute-start.11 = (bf16[256,1024]{1,0:T(8,128)(2,1)}, bf16[256,1024]{1,0:T(8,128)(2,1)}, u32[]{:S(2)}, u32[]{:S(2)}) collective-permute-start(bf16[256,1024]{1,0:T(8,128)(2,1)} %get-tuple-element.104.refs_0_), channel_id=1, source_target_pairs={{0,4},{1,5},{2,6},{3,7},{4,0},{5,1},{6,2},{7,3},{8,12},{9,13},{10,... | collective-permute-start | bytes 1572872 | tf_op jit(solution)/shard_map/ppermute | solution.py:30
  73.4 33.3 %copy-start.7 = (bf16[256,1024]{1,0:T(8,128)(2,1)}, bf16[256,1024]{1,0:T(8,128)(2,1)S(1)}, u32[]{:S(2)}) copy-start(bf16[256,1024]{1,0:T(8,128)(2,1)S(1)} %get-tuple-element.99.refs_4_) | copy-start | bytes 1572868
  73.4 26.1 %collective-permute-start.12 = (bf16[256,1024]{1,0:T(8,128)(2,1)}, bf16[256,1024]{1,0:T(8,128)(2,1)S(1)}, u32[]{:S(2)}, u32[]{:S(2)}) collective-permute-start(bf16[256,1024]{1,0:T(8,128)(2,1)} %get-tuple-element.86), channel_id=1, source_target_pairs={{0,2},{1,3},{2,0},{3,1},{4,6},{5,7},{6,4},{7,5},{8,10},{9,11},{10,... | collective-permute-start | bytes 1572872 | tf_op jit(solution)/shard_map/ppermute | solution.py:30
  85.8 4.6 %copy-start.27 = (f32[2,8,2,64,768]{4,3,0,1,2:T(8,128)}, f32[2,8,2,64,768]{4,3,0,1,2:T(8,128)S(1)}, u32[]{:S(2)}) copy-start(f32[2,8,2,64,768]{4,3,0,1,2:T(8,128)S(1)} %maximum_convert_fusion) | copy-start | bytes 18874372
  97.1 5.5 %copy-start.11 = (bf16[256,1024]{1,0:T(8,128)(2,1)S(1)}, bf16[256,1024]{1,0:T(8,128)(2,1)}, u32[]{:S(2)}) copy-start(bf16[256,1024]{1,0:T(8,128)(2,1)} %get-tuple-element.107.refs_0_) | copy-start | bytes 1572868
  98.6 47.0 %slice-start = ((s8[6291456]{0:T(1024)(128)(4,1)}), s8[4194304]{0:T(1024)(128)(4,1)S(1)}, s32[]{:S(2)}) async-start(s8[6291456]{0:T(1024)(128)(4,1)} %bitcast.140), calls=%async_computation | async-start | bytes 8388608
  99.5 35.5 %copy-start.9 = (bf16[256,1024]{1,0:T(8,128)(2,1)}, bf16[256,1024]{1,0:T(8,128)(2,1)S(1)}, u32[]{:S(2)}) copy-start(bf16[256,1024]{1,0:T(8,128)(2,1)S(1)} %collective-permute-done.12.refs_5_) | copy-start | bytes 1572868
  101.9 22.6 %collective-permute-start.19 = (bf16[256,1024]{1,0:T(8,128)(2,1)S(1)}, bf16[256,1024]{1,0:T(8,128)(2,1)S(1)}, u32[]{:S(2)}, u32[]{:S(2)}) collective-permute-start(bf16[256,1024]{1,0:T(8,128)(2,1)S(1)} %get-tuple-element.108), channel_id=1, source_target_pairs={{0,2},{1,3},{2,0},{3,1},{4,6},{5,7},{6,4},{7,5},{8,10},{9,11},{10,... | collective-permute-start | bytes 1572872 | tf_op jit(solution)/shard_map/ppermute | solution.py:30
  102.1 22.4 %collective-permute-start.20 = (bf16[256,1024]{1,0:T(8,128)(2,1)}, bf16[256,1024]{1,0:T(8,128)(2,1)S(1)}, u32[]{:S(2)}, u32[]{:S(2)}) collective-permute-start(bf16[256,1024]{1,0:T(8,128)(2,1)} %collective-permute-done.11.refs_2_), channel_id=1, source_target_pairs={{0,1},{1,0},{2,3},{3,2},{4,5},{5,4},{6,7},{7,6},{8,9},{9,8},{10,11... | collective-permute-start | bytes 1572872 | tf_op jit(solution)/shard_map/ppermute | solution.py:30
  102.6 24.0 %collective-permute-start.21 = (bf16[256,1024]{1,0:T(8,128)(2,1)S(1)}, bf16[256,1024]{1,0:T(8,128)(2,1)S(1)}, u32[]{:S(2)}, u32[]{:S(2)}) collective-permute-start(bf16[256,1024]{1,0:T(8,128)(2,1)S(1)} %copy-done.11), channel_id=1, source_target_pairs={{0,1},{1,0},{2,3},{3,2},{4,5},{5,4},{6,7},{7,6},{8,9},{9,8},{10,11... | collective-permute-start | bytes 1572872 | tf_op jit(solution)/shard_map/ppermute | solution.py:30
  104.1 24.7 %collective-permute-start.18 = (bf16[256,1024]{1,0:T(8,128)(2,1)S(1)}, bf16[256,1024]{1,0:T(8,128)(2,1)S(1)}, u32[]{:S(2)}, u32[]{:S(2)}) collective-permute-start(bf16[256,1024]{1,0:T(8,128)(2,1)S(1)} %copy-done.11), channel_id=1, source_target_pairs={{0,4},{1,5},{2,6},{3,7},{4,0},{5,1},{6,2},{7,3},{8,12},{9,13},{10,... | collective-permute-start | bytes 1572872 | tf_op jit(solution)/shard_map/ppermute | solution.py:30
  106.8 38.9 %slice-start.1 = ((s8[6291456]{0:T(1024)(128)(4,1)}), s8[2097152]{0:T(1024)(128)(4,1)S(1)}, s32[]{:S(2)}) async-start(s8[6291456]{0:T(1024)(128)(4,1)} %bitcast.140), calls=%async_computation.1 | async-start | bytes 4194304
  110.2 29.5 %copy-start.15 = (f32[384,1024]{1,0:T(8,128)}, f32[384,1024]{1,0:T(8,128)S(1)}, u32[]{:S(2)}) copy-start(f32[384,1024]{1,0:T(8,128)S(1)} %get-tuple-element.101) | copy-start | bytes 4718596
  128.8 15.6 %copy-start.19 = (bf16[256,1024]{1,0:T(8,128)(2,1)}, bf16[256,1024]{1,0:T(8,128)(2,1)S(1)}, u32[]{:S(2)}) copy-start(bf16[256,1024]{1,0:T(8,128)(2,1)S(1)} %collective-permute-done.18.refs_2_) | copy-start | bytes 1572868
  128.8 10.8 %collective-permute-start.22 = (bf16[256,1024]{1,0:T(8,128)(2,1)S(1)}, bf16[256,1024]{1,0:T(8,128)(2,1)S(1)}, u32[]{:S(2)}, u32[]{:S(2)}) collective-permute-start(bf16[256,1024]{1,0:T(8,128)(2,1)S(1)} %collective-permute-done.18.refs_2_), channel_id=1, source_target_pairs={{0,1},{1,0},{2,3},{3,2},{4,5},{5,4},{6,7},{7,6},{8,9},{9,8},{10,11... | collective-permute-start | bytes 1572872 | tf_op jit(solution)/shard_map/ppermute | solution.py:30
  129.4 27.3 %collective-permute-start.17 = (bf16[1,384,512]{2,1,0:T(8,128)(2,1)}, bf16[1,384,512]{2,1,0:T(8,128)(2,1)}, u32[]{:S(2)}, u32[]{:S(2)}) collective-permute-start(bf16[1,384,512]{2,1,0:T(8,128)(2,1)} %bitcast.22), channel_id=1, source_target_pairs={{0,16},{8,24},{16,0},{24,8},{1,17},{9,25},{17,1},{25,9},{2,18},{10... | collective-permute-start | bytes 1179656 | tf_op jit(solution)/shard_map/ppermute | solution.py:30
  130.9 14.8 %copy-start.4 = (bf16[128,2048]{1,0:T(8,128)(2,1)S(1)}, bf16[128,2048]{1,0:T(8,128)(2,1)}, u32[]{:S(2)}) copy-start(bf16[128,2048]{1,0:T(8,128)(2,1)} %copy-done.2) | copy-start | bytes 1572868
  130.9 14.8 %copy-start.8 = (bf16[256,1024]{1,0:T(8,128)(2,1)S(1)}, bf16[256,1024]{1,0:T(8,128)(2,1)}, u32[]{:S(2)}) copy-start(bf16[256,1024]{1,0:T(8,128)(2,1)} %copy-done.7) | copy-start | bytes 1572868
  130.9 25.8 %collective-permute-start.16 = (bf16[1,384,512]{2,1,0:T(8,128)(2,1)}, bf16[1,384,512]{2,1,0:T(8,128)(2,1)}, u32[]{:S(2)}, u32[]{:S(2)}) collective-permute-start(bf16[1,384,512]{2,1,0:T(8,128)(2,1)} %bitcast.20), channel_id=1, source_target_pairs={{0,16},{8,24},{16,0},{24,8},{1,17},{9,25},{17,1},{25,9},{2,18},{10... | collective-permute-start | bytes 1179656 | tf_op jit(solution)/shard_map/ppermute | solution.py:30
  135.1 25.2 %collective-permute-start.24 = (bf16[512,1024]{1,0:T(8,128)(2,1)}, bf16[512,1024]{1,0:T(8,128)(2,1)S(1)}, u32[]{:S(2)}, u32[]{:S(2)}) collective-permute-start(bf16[512,1024]{1,0:T(8,128)(2,1)} %get-tuple-element.118), channel_id=1, source_target_pairs={{0,2},{1,3},{2,0},{3,1},{4,6},{5,7},{6,4},{7,5},{8,10},{9,11},{10,... | collective-permute-start | bytes 3145736 | tf_op jit(solution)/shard_map/ppermute | solution.py:30
  139.6 8.4 %copy-start.21 = (bf16[256,1024]{1,0:T(8,128)(2,1)}, bf16[256,1024]{1,0:T(8,128)(2,1)S(1)}, u32[]{:S(2)}) copy-start(bf16[256,1024]{1,0:T(8,128)(2,1)S(1)} %collective-permute-done.22.refs_3_) | copy-start | bytes 1572868
  141.9 3.7 %copy-start.10 = (bf16[256,1024]{1,0:T(8,128)(2,1)S(1)}, bf16[256,1024]{1,0:T(8,128)(2,1)}, u32[]{:S(2)}) copy-start(bf16[256,1024]{1,0:T(8,128)(2,1)} %copy-done.9) | copy-start | bytes 1572868
  145.6 2.4 %copy-start.23 = (bf16[384,512]{1,0:T(8,128)(2,1)}, bf16[384,512]{1,0:T(8,128)(2,1)S(1)}, u32[]{:S(2)}) copy-start(bf16[384,512]{1,0:T(8,128)(2,1)S(1)} %get-tuple-element.127) | copy-start | bytes 1179652
  145.6 2.4 %copy-start.25 = (bf16[384,512]{1,0:T(8,128)(2,1)}, bf16[384,512]{1,0:T(8,128)(2,1)S(1)}, u32[]{:S(2)}) copy-start(bf16[384,512]{1,0:T(8,128)(2,1)S(1)} %get-tuple-element.128) | copy-start | bytes 1179652
  153.5 10.3 %collective-permute-start.23 = (bf16[8,64,768]{2,1,0:T(8,128)(2,1)}, bf16[8,64,768]{2,1,0:T(8,128)(2,1)}, u32[]{:S(2)}, u32[]{:S(2)}) collective-permute-start(bf16[8,64,768]{2,1,0:T(8,128)(2,1)} %get-tuple-element.149), channel_id=1, source_target_pairs={{0,8},{8,0},{16,24},{24,16},{1,9},{9,1},{17,25},{25,17},{2,10},{10... | collective-permute-start | bytes 2359304 | tf_op jit(solution)/shard_map/ppermute | solution.py:30
  153.5 10.3 %collective-permute-start.25 = (bf16[8,64,768]{2,1,0:T(8,128)(2,1)}, bf16[8,64,768]{2,1,0:T(8,128)(2,1)}, u32[]{:S(2)}, u32[]{:S(2)}) collective-permute-start(bf16[8,64,768]{2,1,0:T(8,128)(2,1)} %get-tuple-element.150), channel_id=1, source_target_pairs={{0,8},{8,0},{16,24},{24,16},{1,9},{9,1},{17,25},{25,17},{2,10},{10... | collective-permute-start | bytes 2359304 | tf_op jit(solution)/shard_map/ppermute | solution.py:30
  154.1 2.5 %copy-start.16 = (f32[384,1024]{1,0:T(8,128)S(1)}, f32[384,1024]{1,0:T(8,128)}, u32[]{:S(2)}) copy-start(f32[384,1024]{1,0:T(8,128)} %copy-done.15) | copy-start | bytes 4718596
  154.1 4.1 %copy-start.26 = (bf16[384,512]{1,0:T(8,128)(2,1)S(1)}, bf16[384,512]{1,0:T(8,128)(2,1)}, u32[]{:S(2)}) copy-start(bf16[384,512]{1,0:T(8,128)(2,1)} %copy-done.25) | copy-start | bytes 1179652
  154.1 5.7 %copy-start.24 = (bf16[384,512]{1,0:T(8,128)(2,1)S(1)}, bf16[384,512]{1,0:T(8,128)(2,1)}, u32[]{:S(2)}) copy-start(bf16[384,512]{1,0:T(8,128)(2,1)} %copy-done.23) | copy-start | bytes 1179652
  154.1 6.2 %copy-start.18 = (bf16[256,1024]{1,0:T(8,128)(2,1)S(1)}, bf16[256,1024]{1,0:T(8,128)(2,1)}, u32[]{:S(2)}) copy-start(bf16[256,1024]{1,0:T(8,128)(2,1)} %copy-done.17) | copy-start | bytes 1572868
  154.1 6.2 %copy-start.20 = (bf16[256,1024]{1,0:T(8,128)(2,1)S(1)}, bf16[256,1024]{1,0:T(8,128)(2,1)}, u32[]{:S(2)}) copy-start(bf16[256,1024]{1,0:T(8,128)(2,1)} %copy-done.19) | copy-start | bytes 1572868
  154.1 6.2 %copy-start.22 = (bf16[256,1024]{1,0:T(8,128)(2,1)S(1)}, bf16[256,1024]{1,0:T(8,128)(2,1)}, u32[]{:S(2)}) copy-start(bf16[256,1024]{1,0:T(8,128)(2,1)} %copy-done.21) | copy-start | bytes 1572868
  156.6 3.7 %copy-start.12 = (bf16[256,1024]{1,0:T(8,128)(2,1)S(1)}, bf16[256,1024]{1,0:T(8,128)(2,1)}, u32[]{:S(2)}) copy-start(bf16[256,1024]{1,0:T(8,128)(2,1)} %get-tuple-element.107.refs_0_) | copy-start | bytes 1572868
  156.6 7.1 %copy-start.1 = (f32[1024,768]{1,0:T(8,128)S(1)}, f32[1024,768]{1,0:T(8,128)}, u32[]{:S(2)}) copy-start(f32[1024,768]{1,0:T(8,128)} %copy-done) | copy-start | bytes 9437188
  158.2 19.8 %collective-permute-start.29 = (bf16[1,384,512]{2,1,0:T(8,128)(2,1)S(1)}, bf16[1,384,512]{2,1,0:T(8,128)(2,1)S(1)}, u32[]{:S(2)}, u32[]{:S(2)}) collective-permute-start(bf16[1,384,512]{2,1,0:T(8,128)(2,1)S(1)} %bitcast.147), channel_id=1, source_target_pairs={{0,16},{8,24},{16,0},{24,8},{1,17},{9,25},{17,1},{25,9},{2,18},{10... | collective-permute-start | bytes 1179656 | tf_op jit(solution)/shard_map/ppermute | solution.py:30
  159.8 18.9 %collective-permute-start.28 = (bf16[1,384,512]{2,1,0:T(8,128)(2,1)S(1)}, bf16[1,384,512]{2,1,0:T(8,128)(2,1)S(1)}, u32[]{:S(2)}, u32[]{:S(2)}) collective-permute-start(bf16[1,384,512]{2,1,0:T(8,128)(2,1)S(1)} %bitcast.146), channel_id=1, source_target_pairs={{0,16},{8,24},{16,0},{24,8},{1,17},{9,25},{17,1},{25,9},{2,18},{10... | collective-permute-start | bytes 1179656 | tf_op jit(solution)/shard_map/ppermute | solution.py:30
  162.2 25.0 %collective-permute-start.34 = (bf16[512,1024]{1,0:T(8,128)(2,1)S(1)}, bf16[512,1024]{1,0:T(8,128)(2,1)S(1)}, u32[]{:S(2)}, u32[]{:S(2)}) collective-permute-start(bf16[512,1024]{1,0:T(8,128)(2,1)S(1)} %get-tuple-element.135), channel_id=1, source_target_pairs={{0,2},{1,3},{2,0},{3,1},{4,6},{5,7},{6,4},{7,5},{8,10},{9,11},{10,... | collective-permute-start | bytes 3145736 | tf_op jit(solution)/shard_map/ppermute | solution.py:30
  167.7 2.8 %copy-start.31 = (f32[8,2,64,768]{3,2,0,1:T(8,128)S(1)}, f32[8,2,64,768]{3,2,0,1:T(8,128)}, u32[]{:S(2)}) copy-start(f32[8,2,64,768]{3,2,0,1:T(8,128)} %get-tuple-element.144) | copy-start | bytes 9437188
  171.9 3.7 %collective-permute-start.32 = (f32[4,1,64]{2,0,1:T(4,128)S(1)}, f32[4,1,64]{2,0,1:T(4,128)S(1)}, u32[]{:S(2)}, u32[]{:S(2)}) collective-permute-start(f32[4,1,64]{2,0,1:T(4,128)S(1)} %bitcast.175), channel_id=1, source_target_pairs={{0,1},{1,0},{2,3},{3,2},{4,5},{5,4},{6,7},{7,6},{8,9},{9,8},{10,11... | collective-permute-start | bytes 3080 | tf_op jit(solution)/shard_map/ppermute | solution.py:30
  172.6 6.0 %copy-start.14 = (f32[384,1024]{1,0:T(8,128)S(1)}, f32[384,1024]{1,0:T(8,128)}, u32[]{:S(2)}) copy-start(f32[384,1024]{1,0:T(8,128)} %copy-done.13) | copy-start | bytes 4718596
  173.7 13.4 %collective-permute-start.26 = (bf16[1,256,768]{2,1,0:T(8,128)(2,1)S(1)}, bf16[1,256,768]{2,1,0:T(8,128)(2,1)S(1)}, u32[]{:S(2)}, u32[]{:S(2)}) collective-permute-start(bf16[1,256,768]{2,1,0:T(8,128)(2,1)S(1)} %bitcast.150), channel_id=1, source_target_pairs={{0,16},{8,24},{16,0},{24,8},{1,17},{9,25},{17,1},{25,9},{2,18},{10... | collective-permute-start | bytes 1179656 | tf_op jit(solution)/shard_map/ppermute | solution.py:30
  175.6 10.2 %collective-permute-start.33 = (f32[1,4,64]{2,1,0:T(4,128)S(1)}, f32[1,4,64]{2,1,0:T(4,128)S(1)}, u32[]{:S(2)}, u32[]{:S(2)}) collective-permute-start(f32[1,4,64]{2,1,0:T(4,128)S(1)} %get-tuple-element.180), channel_id=1, source_target_pairs={{0,4},{1,5},{2,6},{3,7},{4,0},{5,1},{6,2},{7,3},{8,12},{9,13},{10,... | collective-permute-start | bytes 3080 | tf_op jit(solution)/shard_map/ppermute | solution.py:30
  178.9 16.6 %collective-permute-start.31 = (bf16[1,256,768]{2,1,0:T(8,128)(2,1)S(1)}, bf16[1,256,768]{2,1,0:T(8,128)(2,1)S(1)}, u32[]{:S(2)}, u32[]{:S(2)}) collective-permute-start(bf16[1,256,768]{2,1,0:T(8,128)(2,1)S(1)} %bitcast.148), channel_id=1, source_target_pairs={{0,16},{8,24},{16,0},{24,8},{1,17},{9,25},{17,1},{25,9},{2,18},{10... | collective-permute-start | bytes 1179656 | tf_op jit(solution)/shard_map/ppermute | solution.py:30
  187.2 18.3 %collective-permute-start.27 = (f32[192,1024]{1,0:T(8,128)S(1)}, f32[192,1024]{1,0:T(8,128)S(1)}, u32[]{:S(2)}, u32[]{:S(2)}) collective-permute-start(f32[192,1024]{1,0:T(8,128)S(1)} %pad_maximum_fusion.7), channel_id=1, source_target_pairs={{0,8},{8,0},{16,24},{24,16},{1,9},{9,1},{17,25},{25,17},{2,10},{10... | collective-permute-start | bytes 2359304 | tf_op jit(solution)/shard_map/ppermute | solution.py:30
  188.3 15.6 %collective-permute-start.35 = (bf16[1,256,768]{2,1,0:T(8,128)(2,1)S(1)}, bf16[1,256,768]{2,1,0:T(8,128)(2,1)S(1)}, u32[]{:S(2)}, u32[]{:S(2)}) collective-permute-start(bf16[1,256,768]{2,1,0:T(8,128)(2,1)S(1)} %bitcast.151), channel_id=1, source_target_pairs={{0,16},{8,24},{16,0},{24,8},{1,17},{9,25},{17,1},{25,9},{2,18},{10... | collective-permute-start | bytes 1179656 | tf_op jit(solution)/shard_map/ppermute | solution.py:30
  189.9 15.7 %collective-permute-start.30 = (f32[192,1024]{1,0:T(8,128)S(1)}, f32[192,1024]{1,0:T(8,128)S(1)}, u32[]{:S(2)}, u32[]{:S(2)}) collective-permute-start(f32[192,1024]{1,0:T(8,128)S(1)} %pad_maximum_fusion.6), channel_id=1, source_target_pairs={{0,8},{8,0},{16,24},{24,16},{1,9},{9,1},{17,25},{25,17},{2,10},{10... | collective-permute-start | bytes 2359304 | tf_op jit(solution)/shard_map/ppermute | solution.py:30
  196.6 14.8 %collective-permute-start.36 = (bf16[1,256,768]{2,1,0:T(8,128)(2,1)S(1)}, bf16[1,256,768]{2,1,0:T(8,128)(2,1)S(1)}, u32[]{:S(2)}, u32[]{:S(2)}) collective-permute-start(bf16[1,256,768]{2,1,0:T(8,128)(2,1)S(1)} %bitcast.149), channel_id=1, source_target_pairs={{0,16},{8,24},{16,0},{24,8},{1,17},{9,25},{17,1},{25,9},{2,18},{10... | collective-permute-start | bytes 1179656 | tf_op jit(solution)/shard_map/ppermute | solution.py:30
  204.0 8.7 %collective-permute-start.37 = (f32[2,2,64]{2,1,0:T(2,128)S(1)}, f32[2,2,64]{2,1,0:T(2,128)S(1)}, u32[]{:S(2)}, u32[]{:S(2)}) collective-permute-start(f32[2,2,64]{2,1,0:T(2,128)S(1)} %get-tuple-element.178), channel_id=1, source_target_pairs={{0,2},{1,3},{2,0},{3,1},{4,6},{5,7},{6,4},{7,5},{8,10},{9,11},{10,... | collective-permute-start | bytes 3080 | tf_op jit(solution)/shard_map/ppermute | solution.py:30
  (10 other events, 15.3 us)

commit v3 on v2

--- a/solution.py
+++ b/solution.py
@@ -41,13 +41,6 @@
 
 def chip_sum(kept, sent):
     bit = 2
-    if isinstance(sent, list):
-        split = sent[0].shape[-1]
-        halves = [
-            chip_sum([k[:, i * split : (i + 1) * split] for k in kept], piece)
-            for i, piece in enumerate(sent)
-        ]
-        return jnp.concatenate(halves, axis=1)
     while True:
         got = swap(sent, "dp", bit)
         kept = [kept[i] + got[i].astype(jnp.float32) for i in range(len(kept))]
@@ -136,37 +129,30 @@
 
 def down_kernel(count, hidden_t, *refs):
     dy = jnp.concatenate([ref[...] for ref in refs[:count]], axis=0)
-    kept, sent = refs[count], refs[count + 1 :]
+    kept, sent = refs[count:]
     middle = kept.shape[0]
     kept[...] = jnp.dot(hidden_t[:middle, :], dy, preferred_element_type=jnp.float32)
-    other = jnp.dot(hidden_t[middle:, :], dy, preferred_element_type=jnp.float32)
-    for n, out in enumerate(sent):
-
-        @pl.when(pl.program_id(0) * len(sent) // pl.num_programs(0) == n)
-        def _():
-            out[...] = other.astype(jnp.bfloat16)
-
-
-def down_step(hidden_t, near, far, pairs, share, first):
+    sent[...] = jnp.dot(hidden_t[middle:, :], dy, preferred_element_type=jnp.float32).astype(
+        jnp.bfloat16
+    )
+
+
+def down_step(hidden_t, near, far, pairs, width, first):
     hidden_width, slots = hidden_t.shape
     total = far[0].shape[1]
-    width = share // 2
-    steps = total // width
     column = lambda i: (0, i)
     middle = hidden_width // 2
-    kept, *sent = pl.pallas_call(
+    kept, sent = pl.pallas_call(
         functools.partial(down_kernel, len(near) + len(far)),
-        grid=(steps,),
+        grid=(total // width,),
         in_specs=[pl.BlockSpec((hidden_width, slots), lambda i: (0, 0))]
-        + [pl.BlockSpec((piece.shape[0], width), lambda i: (0, 2 * first + i)) for piece in near]
+        + [pl.BlockSpec((piece.shape[0], width), lambda i: (0, first + i)) for piece in near]
         + [pl.BlockSpec((piece.shape[0], width), column) for piece in far],
-        out_specs=[
-            pl.BlockSpec((middle, width), column),
-            pl.BlockSpec((middle, width), lambda i: (0, jnp.minimum(i, steps // 2 - 1))),
-            pl.BlockSpec((middle, width), lambda i: (0, jnp.maximum(i - steps // 2, 0))),
+        out_specs=[pl.BlockSpec((middle, width), column)] * 2,
+        out_shape=[
+            jax.ShapeDtypeStruct((middle, total), jnp.float32),
+            jax.ShapeDtypeStruct((middle, total), jnp.bfloat16),
         ],
-        out_shape=[jax.ShapeDtypeStruct((middle, total), jnp.float32)]
-        + [jax.ShapeDtypeStruct((middle, total // 2), jnp.bfloat16)] * 2,
         compiler_params=pltpu.CompilerParams(vmem_limit_bytes=VMEM),
         cost_estimate=cost(
             2 * slots * hidden_width * total, 2 * total * slots + 3 * total * hidden_width
@@ -174,8 +160,7 @@
         name="down_step",
     )(hidden_t, *near, *far)
     kept = kept.reshape(pairs, middle // pairs, total)
-    sent = [piece.reshape(pairs, middle // pairs, total // 2) for piece in sent]
-    return [kept[i] for i in range(pairs)], sent
+    return [kept[i] for i in range(pairs)], sent.reshape(pairs, middle // pairs, total)
 
 
 def back_kernel(count, where, matrix, *refs):
@@ -330,7 +315,7 @@
     dy_far1 = swap(dy1, "expert", half)
     dy_from_next = spread(place_rows(tables_next, [dy_next], True))
     dy_far_next0 = swap(dy_far0, "expert", 1)
-    x_own = both_cores(tokens, [group ^ (2 * r) for r in range(chips)], 0, share)
+    x_own = both_cores(after(tokens, placed), [group ^ (2 * r) for r in range(chips)], 0, share)
     part_width = share // X_PARTS
     x_parts = [
         jnp.concatenate(
@@ -343,7 +328,7 @@
         for p in range(X_PARTS)
     ]
     order = me ^ jnp.arange(owners, dtype=jnp.int32)
-    saved = jnp.stack([saved_gate, saved_up]).reshape(2, owners, capacity, hidden_width)[:, order]
+    saved = jnp.stack([after(saved_gate, placed), saved_up]).reshape(2, owners, capacity, hidden_width)[:, order]
     dy_far1, dy_from_next, dy_far_next0, x_parts, saved = lax.optimization_barrier(
         (dy_far1, dy_from_next, dy_far_next0, x_parts, saved)
     )
@@ -384,7 +369,7 @@
     x_far_next1 = swap(x_far1, "expert", 1)
     rows = [x_parts[0], x_next0, x_far0, x_far_next0]
     x_spread0 = place_rows(tables_all, rows, False, chips, part_width)
-    near = [after(dy_near[0], x_spread0[0], x_far_next1)] + dy_near[1:]
+    near = [after(dy_near[0], x_spread0[0], x_far_next1, down[0])] + dy_near[1:]
     x_spread0 = spread(x_spread0)
     terms = down_step(hidden_t, near, dy_spread1, chips // 2, share, per_part)
     near[0] = after(near[0], terms[0][0])
@@ -398,7 +383,7 @@
     x_spread1 = place_rows(
         tables_all, x_rows + [x_far_next1], False, chips, part_width
     )
-    other[0] = after(other[0], x_spread1[0])
+    other[0] = after(other[0], x_spread1[0], down[1])
     back = jnp.stack([back[:, g] + other[g].astype(jnp.float32) for g in range(2)], axis=1)
     back = back.reshape(2 * slot_rows, hidden_width)
     grad_pre = (back * gate_act).astype(jnp.bfloat16)

time: 215 us -> 207 us (0.963)
  starting transfers between devices: 41.6 us -> 35.3 us
  local copies, waits for them, and re-layouts: 30.1 us -> 26.8 us
    ppermute x38 -> x36, starting transfers between devices: 41.6 us -> 35.3 us  [swap(): return lax.ppermute(value, axis, [(i, i ^ bit) for i in range(size)])]
    unnamed x73 -> x41, local copies, waits for them, and re-layouts: 11.6 us -> 7.19 us
    add x5, other arithmetic: 1.98 us -> 5.9 us  [chip_sum(): kept = [kept[i] + got[i].astype(jnp.float32) for i in range(len(kept))]]
    pallas_call x2, Pallas kernels: 5.91 us -> 3.59 us  [down_step(): pl.pallas_call(functools.partial(down_kernel, len(near) + len(far)), grid...]
    slice x0 -> x2, local copies, waits for them, and re-layouts: none -> 2.28 us  [per_device(): down[h][block:]]
    ppermute x38 -> x36, waiting for transfers between devices: 89 us -> 91.1 us  [swap(): return lax.ppermute(value, axis, [(i, i ^ bit) for i in range(size)])]
  transfers between devices with their start and end apart: 38 -> 36, of which waited for: 19 -> 18; matrix products, arithmetic and copies ran while one was open for 18% -> 20% of each run, Pallas kernels for 13% -> 11%
where the time goes in v3:
time: 207 us; the launch traced here: 206 us
  waiting for transfers between devices  91.1 us (44%)
  starting transfers between devices  35.3 us (17%)
  Pallas kernels  27.2 us (13%)
  local copies, waits for them, and re-layouts  26.8 us (13%)
  other arithmetic  24.4 us (12%)
    ppermute x36, waiting for transfers between devices, swap(): return lax.ppermute(value, axis, [(i, i ^ bit) for i in range(size)])  91.1 us
    ppermute x36, starting transfers between devices, swap(): return lax.ppermute(value, axis, [(i, i ^ bit) for i in range(size)])  35.3 us
    pallas_call x6, Pallas kernels, place(): pl.pallas_call(functools.partial(place_kernel, len(rows), peers, scaled,...  14 us
    unnamed x41, local copies, waits for them, and re-layouts  7.19 us
    add x5, other arithmetic, chip_sum(): kept = [kept[i] + got[i].astype(jnp.float32) for i in range(len(kept))]  5.9 us
    pallas_call x4, Pallas kernels, up_step(): pl.pallas_call(functools.partial(up_kernel, len(pieces)), grid=(pairs,),...  4.85 us
    pallas_call x2, Pallas kernels, back_step(): pl.pallas_call(functools.partial(back_kernel, len(pieces)), grid_spec=plt...  4.74 us
  transfers between devices with their start and end apart: 36, of which 18 were waited for; matrix products, arithmetic and copies ran while one was open for 20% of the time, Pallas kernels for 11%

profile of v3, /device:TPU:0, one launch (start us, length us, event | category | flops | bytes accessed | tf_op | source)
XLA Modules:
  0.0 206.1 jit_solution(10055059996628324943)
XLA Ops:
  0.7 1.3 constant_dynamic-slice_fusion.7
  2.8 1.3 collective-permute-done.1
  4.2 1.1 fusion.24
  5.3 2.9 %collective-permute-start.2 = (f32[2,8,128]{2,1,0:T(8,128)S(1)}, f32[2,8,128]{2,1,0:T(8,128)S(1)}, u32[]{:S(2)}, u32[]{:S(2)}) collective-permute-start(f32[2,8,128]{2,1,0:T(8,128)S(1)} %pad_maximum_fusion.12.tables), channel_id=1, source_target_pairs={{0,1},{1,0},{2,3},{3,2},{4,5},{5,4},{6,7},{7,6},{8,9},{9,8},{10,11... | collective-permute-start | bytes 24584 | tf_op jit(solution)/shard_map/ppermute | solution.py:30
  8.2 1.6 collective-permute-done.2.tables
  9.8 2.0 collective-permute-start.3
  11.9 2.6 %collective-permute-start.4 = (bf16[256,1024]{1,0:T(8,128)(2,1)}, bf16[256,1024]{1,0:T(8,128)(2,1)}, u32[]{:S(2)}, u32[]{:S(2)}) collective-permute-start(bf16[256,1024]{1,0:T(8,128)(2,1)} %get-tuple-element.168), channel_id=1, source_target_pairs={{0,4},{1,5},{2,6},{3,7},{4,0},{5,1},{6,2},{7,3},{8,12},{9,13},{10,... | collective-permute-start | bytes 1572872 | tf_op jit(solution)/shard_map/ppermute | solution.py:30
  14.5 2.1 %place.6 = (bf16[128,2048]{1,0:T(8,128)(2,1)S(1)}, bf16[128,2048]{1,0:T(8,128)(2,1)}) custom-call(s32[2]{0:T(128)S(1)} %pad_add_fusion.where, f32[2,8,128]{2,1,0:T(8,128)S(1)} %pad_maximum_fusion.12.tables, bf16[256,2048]{1,0:T(8,128)(2,1)S(1)} %pad_maximum_fusion.4.refs_0_), custom_call_target="tpu_custom_call" | custom-call | tf_op jit(solution)/shard_map/place/pallas_call | solution.py:107
  16.6 1.6 collective-permute-start.5
  18.2 2.0 constant_dynamic-slice_fusion.3
  21.4 2.7 %pad_maximum_fusion.1 = bf16[2,8,64,768]{3,2,1,0:T(8,128)(2,1)} fusion(bf16[1,8,64,768]{3,2,1,0:T(8,128)(2,1)} %bitcast.150, bf16[1,8,64,768]{3,2,1,0:T(8,128)(2,1)} %bitcast.151), kind=kLoop, calls=%fused_computation.28 | loop fusion | flops 786432 | bytes 3145728 | tf_op jit(solution)/shard_map/stack | solution.py:331
  24.0 3.2 %gather_fusion = bf16[8,2,64,768]{3,2,1,0:T(8,128)(2,1)} fusion(bf16[2,8,64,768]{3,2,1,0:T(8,128)(2,1)} %pad_maximum_fusion.1, s32[1024]{0:T(1024)S(1)} %pad_clamp_fusion), kind=kCustom, calls=%fused_computation | custom fusion | bytes 3145760 | tf_op jit(solution)/shard_map/gather | solution.py:331
  27.2 10.2 %collective-permute-done.6.tables = f32[4,8,128]{2,1,0:T(8,128)S(1)} collective-permute-done((f32[4,8,128]{2,1,0:T(8,128)S(1)}, f32[4,8,128]{2,1,0:T(8,128)S(1)}, u32[]{:S(2)}, u32[]{:S(2)}) %collective-permute-start.6) | collective-permute-done | bytes 16416 | tf_op jit(solution)/shard_map/ppermute | solution.py:30
  37.4 2.1 %collective-permute-done.5.refs_2_ = bf16[128,2048]{1,0:T(8,128)(2,1)S(1)} collective-permute-done((bf16[128,2048]{1,0:T(8,128)(2,1)}, bf16[128,2048]{1,0:T(8,128)(2,1)S(1)}, u32[]{:S(2)}, u32[]{:S(2)}) %collective-permute-start.5) | collective-permute-done | bytes 524320 | tf_op jit(solution)/shard_map/ppermute | solution.py:30
  39.5 1.4 place.7
  41.1 2.9 %collective-permute-start.7 = (bf16[256,1024]{1,0:T(8,128)(2,1)}, bf16[256,1024]{1,0:T(8,128)(2,1)}, u32[]{:S(2)}, u32[]{:S(2)}) collective-permute-start(bf16[256,1024]{1,0:T(8,128)(2,1)} %get-tuple-element.77), channel_id=1, source_target_pairs={{0,4},{1,5},{2,6},{3,7},{4,0},{5,1},{6,2},{7,3},{8,12},{9,13},{10,... | collective-permute-start | bytes 1572872 | tf_op jit(solution)/shard_map/ppermute | solution.py:30
  44.5 1.2 pad_maximum_fusion.5
  45.8 1.1 pad_maximum_fusion.8
  46.9 15.6 %collective-permute-done.8.refs_3_ = bf16[128,2048]{1,0:T(8,128)(2,1)S(1)} collective-permute-done((bf16[128,2048]{1,0:T(8,128)(2,1)S(1)}, bf16[128,2048]{1,0:T(8,128)(2,1)S(1)}, u32[]{:S(2)}, u32[]{:S(2)}) %collective-permute-start.8) | collective-permute-done | bytes 524320 | tf_op jit(solution)/shard_map/ppermute | solution.py:30
  62.5 4.0 %collective-permute-done.7.refs_0_ = bf16[256,1024]{1,0:T(8,128)(2,1)} collective-permute-done((bf16[256,1024]{1,0:T(8,128)(2,1)}, bf16[256,1024]{1,0:T(8,128)(2,1)}, u32[]{:S(2)}, u32[]{:S(2)}) %collective-permute-start.7) | collective-permute-done | bytes 524320 | tf_op jit(solution)/shard_map/ppermute | solution.py:30
  67.1 1.5 collective-permute-start.14
  68.6 2.9 %place.8 = (bf16[256,1024]{1,0:T(8,128)(2,1)S(1)}, bf16[256,1024]{1,0:T(8,128)(2,1)}) custom-call(s32[2]{0:T(128)S(1)} %pad_add_fusion.where, f32[4,8,128]{2,1,0:T(8,128)S(1)} %collective-permute-done.6.tables, bf16[256,1024]{1,0:T(8,128)(2,1)} %collective-permute-done.4.refs_0_, bf16[256,1024]{1,0:T(8,128)(2,1)S(1)} %collective-permute-done.9.refs_1_), custom_call_target="tpu_custom_call" | custom-call | tf_op jit(solution)/shard_map/place/pallas_call | solution.py:107
  71.5 3.0 %collective-permute-start.12 = (bf16[256,1024]{1,0:T(8,128)(2,1)}, bf16[256,1024]{1,0:T(8,128)(2,1)S(1)}, u32[]{:S(2)}, u32[]{:S(2)}) collective-permute-start(bf16[256,1024]{1,0:T(8,128)(2,1)} %get-tuple-element.88), channel_id=1, source_target_pairs={{0,2},{1,3},{2,0},{3,1},{4,6},{5,7},{6,4},{7,5},{8,10},{9,11},{10,... | collective-permute-start | bytes 1572872 | tf_op jit(solution)/shard_map/ppermute | solution.py:30
  74.5 7.1 %collective-permute-done.13.refs_1_ = bf16[256,1024]{1,0:T(8,128)(2,1)} collective-permute-done((bf16[256,1024]{1,0:T(8,128)(2,1)}, bf16[256,1024]{1,0:T(8,128)(2,1)}, u32[]{:S(2)}, u32[]{:S(2)}) %collective-permute-start.13) | collective-permute-done | bytes 524320 | tf_op jit(solution)/shard_map/ppermute | solution.py:30
  81.6 2.3 %maximum_convert_fusion = f32[2,8,2,64,768]{4,3,0,1,2:T(8,128)S(1)} fusion(bf16[2,8,1,64,768]{4,3,0,1,2:T(8,128)(2,1)} %bitcast.11, bf16[2,8,1,64,768]{4,3,0,1,2:T(8,128)(2,1)} %bitcast.10), kind=kLoop, calls=%fused_computation.5 | loop fusion | flops 3145728 | bytes 9437184 | tf_op jit(solution)/shard_map/convert_element_type | solution.py:342
  83.9 4.0 %slice_bitcast_fusion = (f32[8,2,64,768]{3,2,0,1:T(8,128)}, f32[8,2,64,768]{3,2,0,1:T(8,128)}, f32[1,8,2,64,768]{4,3,0,1,2:T(8,128)S(1)}, f32[1,8,2,64,768]{4,3,1,2,0:T(8,128)S(1)}) fusion(f32[2,8,2,64,768]{4,3,0,1,2:T(8,128)S(1)} %maximum_convert_fusion), kind=kLoop, calls=%fused_computation.17 | loop fusion | bytes 18874368 | tf_op jit(solution)/shard_map/squeeze | solution.py:343
  89.1 1.4 copy-done.6
  90.5 2.1 %fusion.1 = bf16[1024,768]{1,0:T(8,128)(2,1)} fusion(f32[1,8,2,64,768]{4,3,2,1,0:T(8,128)S(1)} %copy.43, f32[1,8,2,64,768]{4,3,2,1,0:T(8,128)S(1)} %copy.42), kind=kLoop, calls=%fused_computation.10 | loop fusion | flops 4718592 | bytes 7864320 | tf_op jit(solution)/shard_map/convert_element_type | solution.py:344
  92.6 2.6 %copy.44 = bf16[768,1024]{1,0:T(8,128)(2,1)} copy(bf16[768,1024]{0,1:T(8,128)(2,1)} %bitcast.146) | data formatting | bytes 3145728 | tf_op jit(solution)/shard_map/transpose | solution.py:346
  95.2 1.5 dynamic-slice_bitcast_fusion.3
  97.6 2.3 %place.9 = (bf16[256,1024]{1,0:T(8,128)(2,1)S(1)}, bf16[256,1024]{1,0:T(8,128)(2,1)S(1)}) custom-call(s32[2]{0:T(128)S(1)} %pad_add_fusion.where, f32[4,8,128]{2,1,0:T(8,128)S(1)} %collective-permute-done.6.tables, bf16[256,1024]{1,0:T(8,128)(2,1)} %collective-permute-done.7.refs_0_, bf16[256,1024]{1,0:T(8,128)(2,1)} %collective-permute-done.13.refs_1_), custom_call_target="tpu_custom_call" | custom-call | tf_op jit(solution)/shard_map/place/pallas_call | solution.py:107
  99.9 1.8 down_step.2
  101.7 1.6 collective-permute-start.16
  103.8 1.5 collective-permute-start.20
  105.3 2.3 %collective-permute-start.17 = (bf16[256,1024]{1,0:T(8,128)(2,1)S(1)}, bf16[256,1024]{1,0:T(8,128)(2,1)S(1)}, u32[]{:S(2)}, u32[]{:S(2)}) collective-permute-start(bf16[256,1024]{1,0:T(8,128)(2,1)S(1)} %copy-done.2), channel_id=1, source_target_pairs={{0,4},{1,5},{2,6},{3,7},{4,0},{5,1},{6,2},{7,3},{8,12},{9,13},{10,... | collective-permute-start | bytes 1572872 | tf_op jit(solution)/shard_map/ppermute | solution.py:30
  107.6 17.5 %collective-permute-done.18.refs_5_ = bf16[256,1024]{1,0:T(8,128)(2,1)S(1)} collective-permute-done((bf16[256,1024]{1,0:T(8,128)(2,1)S(1)}, bf16[256,1024]{1,0:T(8,128)(2,1)S(1)}, u32[]{:S(2)}, u32[]{:S(2)}) %collective-permute-start.18) | collective-permute-done | bytes 524320 | tf_op jit(solution)/shard_map/ppermute | solution.py:30
  125.0 2.3 %collective-permute-done.20.refs_1_ = bf16[256,1024]{1,0:T(8,128)(2,1)S(1)} collective-permute-done((bf16[256,1024]{1,0:T(8,128)(2,1)S(1)}, bf16[256,1024]{1,0:T(8,128)(2,1)S(1)}, u32[]{:S(2)}, u32[]{:S(2)}) %collective-permute-start.20) | collective-permute-done | bytes 524320 | tf_op jit(solution)/shard_map/ppermute | solution.py:30
  127.4 2.2 %collective-permute-done.17.refs_2_ = bf16[256,1024]{1,0:T(8,128)(2,1)S(1)} collective-permute-done((bf16[256,1024]{1,0:T(8,128)(2,1)S(1)}, bf16[256,1024]{1,0:T(8,128)(2,1)S(1)}, u32[]{:S(2)}, u32[]{:S(2)}) %collective-permute-start.17) | collective-permute-done | bytes 524320 | tf_op jit(solution)/shard_map/ppermute | solution.py:30
  130.1 3.1 %place.10 = (bf16[512,1024]{1,0:T(8,128)(2,1)S(1)}, bf16[512,1024]{1,0:T(8,128)(2,1)S(1)}) custom-call(s32[2]{0:T(128)S(1)} %pad_add_fusion.where, f32[8,8,128]{2,1,0:T(8,128)S(1)} %pad_maximum_fusion.10.tables, bf16[256,1024]{1,0:T(8,128)(2,1)} %get-tuple-element.105.refs_0_, bf16[256,1024]{1,0:T(8,128)(2,1)} %collective-permute-done.14.refs_1_, ...), custom_call_target="tpu_custom_call" | custom-call | tf_op jit(solution)/shard_map/place/pallas_call | solution.py:107
  133.3 1.5 convert_add_fusion.1
  134.8 4.4 %collective-permute-done.21.refs_3_ = bf16[256,1024]{1,0:T(8,128)(2,1)S(1)} collective-permute-done((bf16[256,1024]{1,0:T(8,128)(2,1)S(1)}, bf16[256,1024]{1,0:T(8,128)(2,1)S(1)}, u32[]{:S(2)}, u32[]{:S(2)}) %collective-permute-start.21) | collective-permute-done | bytes 524320 | tf_op jit(solution)/shard_map/ppermute | solution.py:30
  139.1 1.8 down_step.3
  141.5 2.4 %back_step.2.refs_6_ = f32[1024,768]{1,0:T(8,128)S(1)} custom-call(s32[2]{0:T(128)S(1)} %pad_add_fusion.where, bf16[768,4096]{1,0:T(8,128)(2,1)S(1)} %bitcast.134, bf16[128,2048]{1,0:T(8,128)(2,1)S(1)} %get-tuple-element.117.refs_0_, bf16[128,2048]{1,0:T(8,128)(2,1)S(1)} %get-tuple-element.98.refs_1_, bf16[128,2048]{1,0:T(8,128)(2,1)S(1)} %collective-permute-done.5.refs_2_, ...), custom_call_target="tpu_custom_call" | custom-call | tf_op jit(solution)/shard_map/back_step/pallas_call | solution.py:186
  143.9 2.4 %back_step.3 = f32[1024,768]{1,0:T(8,128)S(1)} custom-call(s32[2]{0:T(128)S(1)} %pad_add_fusion.where, bf16[768,4096]{1,0:T(8,128)(2,1)S(1)} %bitcast.135, bf16[128,2048]{1,0:T(8,128)(2,1)S(1)} %get-tuple-element.117.refs_0_, bf16[128,2048]{1,0:T(8,128)(2,1)S(1)} %get-tuple-element.98.refs_1_, bf16[128,2048]{1,0:T(8,128)(2,1)S(1)} %collective-permute-done.5.refs_2_, ...), custom_call_target="tpu_custom_call" | custom-call | tf_op jit(solution)/shard_map/back_step/pallas_call | solution.py:186
  147.5 6.3 %collective-permute-done.23.refs_1_.refs_3_.refs_5_.refs_7_ = bf16[512,1024]{1,0:T(8,128)(2,1)S(1)} collective-permute-done((bf16[512,1024]{1,0:T(8,128)(2,1)S(1)}, bf16[512,1024]{1,0:T(8,128)(2,1)S(1)}, u32[]{:S(2)}, u32[]{:S(2)}) %collective-permute-start.23) | collective-permute-done | bytes 1048608 | tf_op jit(solution)/shard_map/ppermute | solution.py:30
  153.7 2.2 %place.11 = (bf16[512,1024]{1,0:T(8,128)(2,1)S(1)}, bf16[512,1024]{1,0:T(8,128)(2,1)S(1)}) custom-call(s32[2]{0:T(128)S(1)} %pad_add_fusion.where, f32[8,8,128]{2,1,0:T(8,128)S(1)} %pad_maximum_fusion.10.tables, bf16[256,1024]{1,0:T(8,128)(2,1)S(1)} %copy-done.2, bf16[256,1024]{1,0:T(8,128)(2,1)S(1)} %collective-permute-done.20.refs_1_, ...), custom_call_target="tpu_custom_call" | custom-call | tf_op jit(solution)/shard_map/place/pallas_call | solution.py:107
  155.9 1.5 collective-permute-start.32
  157.4 1.5 convert_add_fusion
  159.9 1.6 copy-done.7
  162.4 1.2 copy-done.8
  163.5 1.4 copy-done.9
  166.3 1.6 collective-permute-start.30
  170.0 2.1 %collective-permute-start.31 = (f32[1,4,64]{2,1,0:T(4,128)S(1)}, f32[1,4,64]{2,1,0:T(4,128)S(1)}, u32[]{:S(2)}, u32[]{:S(2)}) collective-permute-start(f32[1,4,64]{2,1,0:T(4,128)S(1)} %get-tuple-element.176), channel_id=1, source_target_pairs={{0,4},{1,5},{2,6},{3,7},{4,0},{5,1},{6,2},{7,3},{8,12},{9,13},{10,... | collective-permute-start | bytes 3080 | tf_op jit(solution)/shard_map/ppermute | solution.py:30
  173.6 2.4 %collective-permute-done.31 = f32[1,4,64]{2,1,0:T(4,128)S(1)} collective-permute-done((f32[1,4,64]{2,1,0:T(4,128)S(1)}, f32[1,4,64]{2,1,0:T(4,128)S(1)}, u32[]{:S(2)}, u32[]{:S(2)}) %collective-permute-start.31) | collective-permute-done | bytes 1056 | tf_op jit(solution)/shard_map/ppermute | solution.py:30
  176.0 3.6 %collective-permute-done.26 = bf16[1,256,768]{2,1,0:T(8,128)(2,1)S(1)} collective-permute-done((bf16[1,256,768]{2,1,0:T(8,128)(2,1)S(1)}, bf16[1,256,768]{2,1,0:T(8,128)(2,1)S(1)}, u32[]{:S(2)}, u32[]{:S(2)}) %collective-permute-start.26) | collective-permute-done | bytes 393248 | tf_op jit(solution)/shard_map/ppermute | solution.py:30
  180.4 1.8 up_step.6
  183.8 1.3 slice.105
  185.5 1.1 convert_add_fusion.4
  187.6 1.6 collective-permute-start.34
  189.2 6.2 %collective-permute-done.33 = bf16[1,256,768]{2,1,0:T(8,128)(2,1)} collective-permute-done((bf16[1,256,768]{2,1,0:T(8,128)(2,1)}, bf16[1,256,768]{2,1,0:T(8,128)(2,1)}, u32[]{:S(2)}, u32[]{:S(2)}) %collective-permute-start.33) | collective-permute-done | bytes 393248 | tf_op jit(solution)/shard_map/ppermute | solution.py:30
  196.9 1.3 slice_select_fusion.3
  198.4 2.0 maximum_bitcast_fusion
  200.3 3.0 %collective-permute-done.34 = bf16[1,256,768]{2,1,0:T(8,128)(2,1)S(1)} collective-permute-done((bf16[1,256,768]{2,1,0:T(8,128)(2,1)S(1)}, bf16[1,256,768]{2,1,0:T(8,128)(2,1)S(1)}, u32[]{:S(2)}, u32[]{:S(2)}) %collective-permute-start.34) | collective-permute-done | bytes 393248 | tf_op jit(solution)/shard_map/ppermute | solution.py:30
  203.4 1.2 pad_maximum_fusion.3
  (124 shorter events, 22.0 us)
Async XLA Ops:
  0.6 1.9 copy-start.15
  0.6 1.9 copy-start.14
  2.0 2.1 %collective-permute-start = (bf16[128,2048]{1,0:T(8,128)(2,1)S(1)}, bf16[128,2048]{1,0:T(8,128)(2,1)S(1)}, u32[]{:S(2)}, u32[]{:S(2)}) collective-permute-start(bf16[128,2048]{1,0:T(8,128)(2,1)S(1)} %pad_maximum_fusion.6), channel_id=1, source_target_pairs={{0,8},{8,0},{16,24},{24,16},{1,9},{9,1},{17,25},{25,17},{2,10},{10... | collective-permute-start | bytes 1572872 | tf_op jit(solution)/shard_map/ppermute | solution.py:30
  2.6 1.4 collective-permute-start.1
  5.3 4.5 %collective-permute-start.2 = (f32[2,8,128]{2,1,0:T(8,128)S(1)}, f32[2,8,128]{2,1,0:T(8,128)S(1)}, u32[]{:S(2)}, u32[]{:S(2)}) collective-permute-start(f32[2,8,128]{2,1,0:T(8,128)S(1)} %pad_maximum_fusion.12.tables), channel_id=1, source_target_pairs={{0,1},{1,0},{2,3},{3,2},{4,5},{5,4},{6,7},{7,6},{8,9},{9,8},{10,11... | collective-permute-start | bytes 24584 | tf_op jit(solution)/shard_map/ppermute | solution.py:30
  9.8 29.7 %collective-permute-start.3 = (bf16[256,2048]{1,0:T(8,128)(2,1)S(1)}, bf16[256,2048]{1,0:T(8,128)(2,1)S(1)}, u32[]{:S(2)}, u32[]{:S(2)}) collective-permute-start(bf16[256,2048]{1,0:T(8,128)(2,1)S(1)} %pad_maximum_fusion.4.refs_0_), channel_id=1, source_target_pairs={{0,1},{1,0},{2,3},{3,2},{4,5},{5,4},{6,7},{7,6},{8,9},{9,8},{10,11... | collective-permute-start | bytes 3145736 | tf_op jit(solution)/shard_map/ppermute | solution.py:30
  11.9 25.5 %collective-permute-start.4 = (bf16[256,1024]{1,0:T(8,128)(2,1)}, bf16[256,1024]{1,0:T(8,128)(2,1)}, u32[]{:S(2)}, u32[]{:S(2)}) collective-permute-start(bf16[256,1024]{1,0:T(8,128)(2,1)} %get-tuple-element.168), channel_id=1, source_target_pairs={{0,4},{1,5},{2,6},{3,7},{4,0},{5,1},{6,2},{7,3},{8,12},{9,13},{10,... | collective-permute-start | bytes 1572872 | tf_op jit(solution)/shard_map/ppermute | solution.py:30
  16.6 23.0 %collective-permute-start.5 = (bf16[128,2048]{1,0:T(8,128)(2,1)}, bf16[128,2048]{1,0:T(8,128)(2,1)S(1)}, u32[]{:S(2)}, u32[]{:S(2)}) collective-permute-start(bf16[128,2048]{1,0:T(8,128)(2,1)} %get-tuple-element.76), channel_id=1, source_target_pairs={{0,2},{1,3},{2,0},{3,1},{4,6},{5,7},{6,4},{7,5},{8,10},{9,11},{10,... | collective-permute-start | bytes 1572872 | tf_op jit(solution)/shard_map/ppermute | solution.py:30
  21.0 23.6 %collective-permute-start.10 = (bf16[128,2048]{1,0:T(8,128)(2,1)}, bf16[128,2048]{1,0:T(8,128)(2,1)}, u32[]{:S(2)}, u32[]{:S(2)}) collective-permute-start(bf16[128,2048]{1,0:T(8,128)(2,1)} %pad_maximum_fusion.7), channel_id=1, source_target_pairs={{0,8},{8,0},{16,24},{24,16},{1,9},{9,1},{17,25},{25,17},{2,10},{10... | collective-permute-start | bytes 1572872 | tf_op jit(solution)/shard_map/ppermute | solution.py:30
  21.0 16.4 %collective-permute-start.6 = (f32[4,8,128]{2,1,0:T(8,128)S(1)}, f32[4,8,128]{2,1,0:T(8,128)S(1)}, u32[]{:S(2)}, u32[]{:S(2)}) collective-permute-start(f32[4,8,128]{2,1,0:T(8,128)S(1)} %pad_maximum_fusion.11), channel_id=1, source_target_pairs={{0,4},{1,5},{2,6},{3,7},{4,0},{5,1},{6,2},{7,3},{8,12},{9,13},{10,... | collective-permute-start | bytes 49160 | tf_op jit(solution)/shard_map/ppermute | solution.py:30
  41.0 21.6 %collective-permute-start.8 = (bf16[128,2048]{1,0:T(8,128)(2,1)S(1)}, bf16[128,2048]{1,0:T(8,128)(2,1)S(1)}, u32[]{:S(2)}, u32[]{:S(2)}) collective-permute-start(bf16[128,2048]{1,0:T(8,128)(2,1)S(1)} %get-tuple-element.80), channel_id=1, source_target_pairs={{0,2},{1,3},{2,0},{3,1},{4,6},{5,7},{6,4},{7,5},{8,10},{9,11},{10,... | collective-permute-start | bytes 1572872 | tf_op jit(solution)/shard_map/ppermute | solution.py:30
  41.1 25.5 %collective-permute-start.7 = (bf16[256,1024]{1,0:T(8,128)(2,1)}, bf16[256,1024]{1,0:T(8,128)(2,1)}, u32[]{:S(2)}, u32[]{:S(2)}) collective-permute-start(bf16[256,1024]{1,0:T(8,128)(2,1)} %get-tuple-element.77), channel_id=1, source_target_pairs={{0,4},{1,5},{2,6},{3,7},{4,0},{5,1},{6,2},{7,3},{8,12},{9,13},{10,... | collective-permute-start | bytes 1572872 | tf_op jit(solution)/shard_map/ppermute | solution.py:30
  44.0 22.6 %collective-permute-start.9 = (bf16[256,1024]{1,0:T(8,128)(2,1)}, bf16[256,1024]{1,0:T(8,128)(2,1)S(1)}, u32[]{:S(2)}, u32[]{:S(2)}) collective-permute-start(bf16[256,1024]{1,0:T(8,128)(2,1)} %collective-permute-done.4.refs_0_), channel_id=1, source_target_pairs={{0,1},{1,0},{2,3},{3,2},{4,5},{5,4},{6,7},{7,6},{8,9},{9,8},{10,11... | collective-permute-start | bytes 1572872 | tf_op jit(solution)/shard_map/ppermute | solution.py:30
  66.5 15.0 %collective-permute-start.15 = (bf16[2,8,64,768]{3,2,0,1:T(8,128)(2,1)}, bf16[2,8,64,768]{3,2,0,1:T(8,128)(2,1)}, u32[]{:S(2)}, u32[]{:S(2)}) collective-permute-start(bf16[2,8,64,768]{3,2,0,1:T(8,128)(2,1)} %bitcast.9), channel_id=1, source_target_pairs={{0,8},{8,0},{16,24},{24,16},{1,9},{9,1},{17,25},{25,17},{2,10},{10... | collective-permute-start | bytes 4718600 | tf_op jit(solution)/shard_map/ppermute | solution.py:30
  66.5 15.0 %collective-permute-start.13 = (bf16[256,1024]{1,0:T(8,128)(2,1)}, bf16[256,1024]{1,0:T(8,128)(2,1)}, u32[]{:S(2)}, u32[]{:S(2)}) collective-permute-start(bf16[256,1024]{1,0:T(8,128)(2,1)} %collective-permute-done.7.refs_0_), channel_id=1, source_target_pairs={{0,1},{1,0},{2,3},{3,2},{4,5},{5,4},{6,7},{7,6},{8,9},{9,8},{10,11... | collective-permute-start | bytes 1572872 | tf_op jit(solution)/shard_map/ppermute | solution.py:30
  67.1 30.5 %collective-permute-start.14 = (bf16[256,1024]{1,0:T(8,128)(2,1)}, bf16[256,1024]{1,0:T(8,128)(2,1)}, u32[]{:S(2)}, u32[]{:S(2)}) collective-permute-start(bf16[256,1024]{1,0:T(8,128)(2,1)} %get-tuple-element.105.refs_0_), channel_id=1, source_target_pairs={{0,1},{1,0},{2,3},{3,2},{4,5},{5,4},{6,7},{7,6},{8,9},{9,8},{10,11... | collective-permute-start | bytes 1572872 | tf_op jit(solution)/shard_map/ppermute | solution.py:30
  68.6 29.0 %collective-permute-start.11 = (bf16[256,1024]{1,0:T(8,128)(2,1)}, bf16[256,1024]{1,0:T(8,128)(2,1)}, u32[]{:S(2)}, u32[]{:S(2)}) collective-permute-start(bf16[256,1024]{1,0:T(8,128)(2,1)} %get-tuple-element.105.refs_0_), channel_id=1, source_target_pairs={{0,4},{1,5},{2,6},{3,7},{4,0},{5,1},{6,2},{7,3},{8,12},{9,13},{10,... | collective-permute-start | bytes 1572872 | tf_op jit(solution)/shard_map/ppermute | solution.py:30
  71.5 26.1 %collective-permute-start.12 = (bf16[256,1024]{1,0:T(8,128)(2,1)}, bf16[256,1024]{1,0:T(8,128)(2,1)S(1)}, u32[]{:S(2)}, u32[]{:S(2)}) collective-permute-start(bf16[256,1024]{1,0:T(8,128)(2,1)} %get-tuple-element.88), channel_id=1, source_target_pairs={{0,2},{1,3},{2,0},{3,1},{4,6},{5,7},{6,4},{7,5},{8,10},{9,11},{10,... | collective-permute-start | bytes 1572872 | tf_op jit(solution)/shard_map/ppermute | solution.py:30
  83.9 4.6 %copy-start.5 = (f32[2,8,2,64,768]{4,3,0,1,2:T(8,128)}, f32[2,8,2,64,768]{4,3,0,1,2:T(8,128)S(1)}, u32[]{:S(2)}) copy-start(f32[2,8,2,64,768]{4,3,0,1,2:T(8,128)S(1)} %maximum_convert_fusion) | copy-start | bytes 18874372
  88.8 1.8 copy-start.6
  96.8 7.0 %copy-start.2 = (bf16[256,1024]{1,0:T(8,128)(2,1)S(1)}, bf16[256,1024]{1,0:T(8,128)(2,1)}, u32[]{:S(2)}) copy-start(bf16[256,1024]{1,0:T(8,128)(2,1)} %get-tuple-element.108.refs_0_) | copy-start | bytes 1572868
  99.9 41.6 %slice-start = ((s8[6291456]{0:T(1024)(128)(4,1)}), s8[4194304]{0:T(1024)(128)(4,1)S(1)}, s32[]{:S(2)}) async-start(s8[6291456]{0:T(1024)(128)(4,1)} %bitcast.132), calls=%async_computation | async-start | bytes 8388608
  101.7 31.6 %collective-permute-start.16 = (bf16[1,384,1024]{2,1,0:T(8,128)(2,1)S(1)}, bf16[1,384,1024]{2,1,0:T(8,128)(2,1)S(1)}, u32[]{:S(2)}, u32[]{:S(2)}) collective-permute-start(bf16[1,384,1024]{2,1,0:T(8,128)(2,1)S(1)} %bitcast.138), channel_id=1, source_target_pairs={{0,16},{8,24},{16,0},{24,8},{1,17},{9,25},{17,1},{25,9},{2,18},{10... | collective-permute-start | bytes 2359304 | tf_op jit(solution)/shard_map/ppermute | solution.py:30
  103.3 21.7 %collective-permute-start.18 = (bf16[256,1024]{1,0:T(8,128)(2,1)S(1)}, bf16[256,1024]{1,0:T(8,128)(2,1)S(1)}, u32[]{:S(2)}, u32[]{:S(2)}) collective-permute-start(bf16[256,1024]{1,0:T(8,128)(2,1)S(1)} %get-tuple-element.109), channel_id=1, source_target_pairs={{0,2},{1,3},{2,0},{3,1},{4,6},{5,7},{6,4},{7,5},{8,10},{9,11},{10,... | collective-permute-start | bytes 1572872 | tf_op jit(solution)/shard_map/ppermute | solution.py:30
  103.3 21.7 %collective-permute-start.19 = (bf16[256,1024]{1,0:T(8,128)(2,1)}, bf16[256,1024]{1,0:T(8,128)(2,1)S(1)}, u32[]{:S(2)}, u32[]{:S(2)}) collective-permute-start(bf16[256,1024]{1,0:T(8,128)(2,1)} %collective-permute-done.11.refs_2_), channel_id=1, source_target_pairs={{0,1},{1,0},{2,3},{3,2},{4,5},{5,4},{6,7},{7,6},{8,9},{9,8},{10,11... | collective-permute-start | bytes 1572872 | tf_op jit(solution)/shard_map/ppermute | solution.py:30
  103.8 23.6 %collective-permute-start.20 = (bf16[256,1024]{1,0:T(8,128)(2,1)S(1)}, bf16[256,1024]{1,0:T(8,128)(2,1)S(1)}, u32[]{:S(2)}, u32[]{:S(2)}) collective-permute-start(bf16[256,1024]{1,0:T(8,128)(2,1)S(1)} %copy-done.2), channel_id=1, source_target_pairs={{0,1},{1,0},{2,3},{3,2},{4,5},{5,4},{6,7},{7,6},{8,9},{9,8},{10,11... | collective-permute-start | bytes 1572872 | tf_op jit(solution)/shard_map/ppermute | solution.py:30
  105.3 24.3 %collective-permute-start.17 = (bf16[256,1024]{1,0:T(8,128)(2,1)S(1)}, bf16[256,1024]{1,0:T(8,128)(2,1)S(1)}, u32[]{:S(2)}, u32[]{:S(2)}) collective-permute-start(bf16[256,1024]{1,0:T(8,128)(2,1)S(1)} %copy-done.2), channel_id=1, source_target_pairs={{0,4},{1,5},{2,6},{3,7},{4,0},{5,1},{6,2},{7,3},{8,12},{9,13},{10,... | collective-permute-start | bytes 1572872 | tf_op jit(solution)/shard_map/ppermute | solution.py:30
  129.6 9.5 %collective-permute-start.21 = (bf16[256,1024]{1,0:T(8,128)(2,1)S(1)}, bf16[256,1024]{1,0:T(8,128)(2,1)S(1)}, u32[]{:S(2)}, u32[]{:S(2)}) collective-permute-start(bf16[256,1024]{1,0:T(8,128)(2,1)S(1)} %collective-permute-done.17.refs_2_), channel_id=1, source_target_pairs={{0,1},{1,0},{2,3},{3,2},{4,5},{5,4},{6,7},{7,6},{8,9},{9,8},{10,11... | collective-permute-start | bytes 1572872 | tf_op jit(solution)/shard_map/ppermute | solution.py:30
  133.2 8.3 %slice-start.1 = ((s8[6291456]{0:T(1024)(128)(4,1)}), s8[2097152]{0:T(1024)(128)(4,1)S(1)}, s32[]{:S(2)}) async-start(s8[6291456]{0:T(1024)(128)(4,1)} %bitcast.132), calls=%async_computation.1 | async-start | bytes 4194304
  133.2 20.5 %collective-permute-start.23 = (bf16[512,1024]{1,0:T(8,128)(2,1)S(1)}, bf16[512,1024]{1,0:T(8,128)(2,1)S(1)}, u32[]{:S(2)}, u32[]{:S(2)}) collective-permute-start(bf16[512,1024]{1,0:T(8,128)(2,1)S(1)} %get-tuple-element.119), channel_id=1, source_target_pairs={{0,2},{1,3},{2,0},{3,1},{4,6},{5,7},{6,4},{7,5},{8,10},{9,11},{10,... | collective-permute-start | bytes 3145736 | tf_op jit(solution)/shard_map/ppermute | solution.py:30
  140.9 16.5 %collective-permute-start.24 = (bf16[1,384,1024]{2,1,0:T(8,128)(2,1)S(1)}, bf16[1,384,1024]{2,1,0:T(8,128)(2,1)S(1)}, u32[]{:S(2)}, u32[]{:S(2)}) collective-permute-start(bf16[1,384,1024]{2,1,0:T(8,128)(2,1)S(1)} %bitcast.139), channel_id=1, source_target_pairs={{0,16},{8,24},{16,0},{24,8},{1,17},{9,25},{17,1},{25,9},{2,18},{10... | collective-permute-start | bytes 2359304 | tf_op jit(solution)/shard_map/ppermute | solution.py:30
  141.5 5.5 %slice-start.2 = ((s8[6291456]{0:T(1024)(128)(4,1)}), s8[4194304]{0:T(1024)(128)(4,1)S(1)}, s32[]{:S(2)}) async-start(s8[6291456]{0:T(1024)(128)(4,1)} %bitcast.143), calls=%async_computation.2 | async-start | bytes 8388608
  143.9 3.2 %slice-start.3 = ((s8[6291456]{0:T(1024)(128)(4,1)}), s8[2097152]{0:T(1024)(128)(4,1)S(1)}, s32[]{:S(2)}) async-start(s8[6291456]{0:T(1024)(128)(4,1)} %bitcast.143), calls=%async_computation.3 | async-start | bytes 4194304
  146.5 12.4 %collective-permute-start.22 = (bf16[8,64,768]{2,1,0:T(8,128)(2,1)S(1)}, bf16[8,64,768]{2,1,0:T(8,128)(2,1)S(1)}, u32[]{:S(2)}, u32[]{:S(2)}) collective-permute-start(bf16[8,64,768]{2,1,0:T(8,128)(2,1)S(1)} %get-tuple-element.149), channel_id=1, source_target_pairs={{0,8},{8,0},{16,24},{24,16},{1,9},{9,1},{17,25},{25,17},{2,10},{10... | collective-permute-start | bytes 2359304 | tf_op jit(solution)/shard_map/ppermute | solution.py:30
  146.5 12.4 %collective-permute-start.25 = (bf16[8,64,768]{2,1,0:T(8,128)(2,1)S(1)}, bf16[8,64,768]{2,1,0:T(8,128)(2,1)S(1)}, u32[]{:S(2)}, u32[]{:S(2)}) collective-permute-start(bf16[8,64,768]{2,1,0:T(8,128)(2,1)S(1)} %get-tuple-element.150), channel_id=1, source_target_pairs={{0,8},{8,0},{16,24},{24,16},{1,9},{9,1},{17,25},{25,17},{2,10},{10... | collective-permute-start | bytes 2359304 | tf_op jit(solution)/shard_map/ppermute | solution.py:30
  155.9 24.5 %collective-permute-start.32 = (bf16[512,1024]{1,0:T(8,128)(2,1)S(1)}, bf16[512,1024]{1,0:T(8,128)(2,1)S(1)}, u32[]{:S(2)}, u32[]{:S(2)}) collective-permute-start(bf16[512,1024]{1,0:T(8,128)(2,1)S(1)} %get-tuple-element.135), channel_id=1, source_target_pairs={{0,2},{1,3},{2,0},{3,1},{4,6},{5,7},{6,4},{7,5},{8,10},{9,11},{10,... | collective-permute-start | bytes 3145736 | tf_op jit(solution)/shard_map/ppermute | solution.py:30
  159.6 1.9 copy-start.7
  161.5 2.0 copy-start.8
  161.5 3.4 %copy-start.9 = (f32[8,2,64,768]{3,2,0,1:T(8,128)S(1)}, f32[8,2,64,768]{3,2,0,1:T(8,128)}, u32[]{:S(2)}) copy-start(f32[8,2,64,768]{3,2,0,1:T(8,128)} %get-tuple-element.144) | copy-start | bytes 9437188
  162.3 18.1 %copy-start = (bf16[1024,768]{1,0:T(8,128)(2,1)}, bf16[1024,768]{1,0:T(8,128)(2,1)S(1)}, u32[]{:S(2)}) copy-start(bf16[1024,768]{1,0:T(8,128)(2,1)S(1)} %fusion.grad_pre) | copy-start | bytes 4718596
  166.3 5.8 %copy-start.10 = (f32[384,1024]{1,0:T(8,128)S(1)}, f32[384,1024]{1,0:T(8,128)}, u32[]{:S(2)}) copy-start(f32[384,1024]{1,0:T(8,128)} %convert_add_fusion.1) | copy-start | bytes 4718596
  166.3 3.7 %collective-permute-start.30 = (f32[4,1,64]{2,0,1:T(4,128)S(1)}, f32[4,1,64]{2,0,1:T(4,128)S(1)}, u32[]{:S(2)}, u32[]{:S(2)}) collective-permute-start(f32[4,1,64]{2,0,1:T(4,128)S(1)} %bitcast.167), channel_id=1, source_target_pairs={{0,1},{1,0},{2,3},{3,2},{4,5},{5,4},{6,7},{7,6},{8,9},{9,8},{10,11... | collective-permute-start | bytes 3080 | tf_op jit(solution)/shard_map/ppermute | solution.py:30
  168.9 10.7 %collective-permute-start.26 = (bf16[1,256,768]{2,1,0:T(8,128)(2,1)S(1)}, bf16[1,256,768]{2,1,0:T(8,128)(2,1)S(1)}, u32[]{:S(2)}, u32[]{:S(2)}) collective-permute-start(bf16[1,256,768]{2,1,0:T(8,128)(2,1)S(1)} %bitcast.142), channel_id=1, source_target_pairs={{0,16},{8,24},{16,0},{24,8},{1,17},{9,25},{17,1},{25,9},{2,18},{10... | collective-permute-start | bytes 1179656 | tf_op jit(solution)/shard_map/ppermute | solution.py:30
  170.0 6.0 %collective-permute-start.31 = (f32[1,4,64]{2,1,0:T(4,128)S(1)}, f32[1,4,64]{2,1,0:T(4,128)S(1)}, u32[]{:S(2)}, u32[]{:S(2)}) collective-permute-start(f32[1,4,64]{2,1,0:T(4,128)S(1)} %get-tuple-element.176), channel_id=1, source_target_pairs={{0,4},{1,5},{2,6},{3,7},{4,0},{5,1},{6,2},{7,3},{8,12},{9,13},{10,... | collective-permute-start | bytes 3080 | tf_op jit(solution)/shard_map/ppermute | solution.py:30
  173.1 12.4 %collective-permute-start.29 = (bf16[1,256,768]{2,1,0:T(8,128)(2,1)S(1)}, bf16[1,256,768]{2,1,0:T(8,128)(2,1)}, u32[]{:S(2)}, u32[]{:S(2)}) collective-permute-start(bf16[1,256,768]{2,1,0:T(8,128)(2,1)S(1)} %bitcast.140), channel_id=1, source_target_pairs={{0,16},{8,24},{16,0},{24,8},{1,17},{9,25},{17,1},{25,9},{2,18},{10... | collective-permute-start | bytes 1179656 | tf_op jit(solution)/shard_map/ppermute | solution.py:30
  180.4 16.4 %collective-permute-start.27 = (f32[192,1024]{1,0:T(8,128)}, f32[192,1024]{1,0:T(8,128)}, u32[]{:S(2)}, u32[]{:S(2)}) collective-permute-start(f32[192,1024]{1,0:T(8,128)} %slice.101), channel_id=1, source_target_pairs={{0,8},{8,0},{16,24},{24,16},{1,9},{9,1},{17,25},{25,17},{2,10},{10... | collective-permute-start | bytes 2359304 | tf_op jit(solution)/shard_map/ppermute | solution.py:30
  182.2 1.0 copy-start.3
  183.2 12.2 %collective-permute-start.33 = (bf16[1,256,768]{2,1,0:T(8,128)(2,1)}, bf16[1,256,768]{2,1,0:T(8,128)(2,1)}, u32[]{:S(2)}, u32[]{:S(2)}) collective-permute-start(bf16[1,256,768]{2,1,0:T(8,128)(2,1)} %bitcast.47), channel_id=1, source_target_pairs={{0,16},{8,24},{16,0},{24,8},{1,17},{9,25},{17,1},{25,9},{2,18},{10... | collective-permute-start | bytes 1179656 | tf_op jit(solution)/shard_map/ppermute | solution.py:30
  183.8 2.7 %copy-start.1 = (bf16[1024,768]{1,0:T(8,128)(2,1)S(1)}, bf16[1024,768]{1,0:T(8,128)(2,1)}, u32[]{:S(2)}) copy-start(bf16[1024,768]{1,0:T(8,128)(2,1)} %copy-done) | copy-start | bytes 4718596
  185.2 13.0 %collective-permute-start.28 = (f32[192,1024]{1,0:T(8,128)S(1)}, f32[192,1024]{1,0:T(8,128)S(1)}, u32[]{:S(2)}, u32[]{:S(2)}) collective-permute-start(f32[192,1024]{1,0:T(8,128)S(1)} %slice.105), channel_id=1, source_target_pairs={{0,8},{8,0},{16,24},{24,16},{1,9},{9,1},{17,25},{25,17},{2,10},{10... | collective-permute-start | bytes 2359304 | tf_op jit(solution)/shard_map/ppermute | solution.py:30
  186.6 8.9 %copy-start.4 = (f32[256,768]{1,0:T(8,128)S(1)}, f32[256,768]{1,0:T(8,128)}, u32[]{:S(2)}) copy-start(f32[256,768]{1,0:T(8,128)} %copy-done.3) | copy-start | bytes 2359300
  186.6 10.3 %copy-start.11 = (f32[384,1024]{1,0:T(8,128)S(1)}, f32[384,1024]{1,0:T(8,128)}, u32[]{:S(2)}) copy-start(f32[384,1024]{1,0:T(8,128)} %convert_add_fusion.1) | copy-start | bytes 4718596
  187.6 10.6 %copy-start.12 = (f32[384,1024]{1,0:T(8,128)S(1)}, f32[384,1024]{1,0:T(8,128)}, u32[]{:S(2)}) copy-start(f32[384,1024]{1,0:T(8,128)} %convert_add_fusion) | copy-start | bytes 4718596
  187.6 15.7 %collective-permute-start.34 = (bf16[1,256,768]{2,1,0:T(8,128)(2,1)S(1)}, bf16[1,256,768]{2,1,0:T(8,128)(2,1)S(1)}, u32[]{:S(2)}, u32[]{:S(2)}) collective-permute-start(bf16[1,256,768]{2,1,0:T(8,128)(2,1)S(1)} %bitcast.141), channel_id=1, source_target_pairs={{0,16},{8,24},{16,0},{24,8},{1,17},{9,25},{17,1},{25,9},{2,18},{10... | collective-permute-start | bytes 1179656 | tf_op jit(solution)/shard_map/ppermute | solution.py:30
  196.5 8.2 %collective-permute-start.35 = (f32[2,2,64]{2,1,0:T(2,128)S(1)}, f32[2,2,64]{2,1,0:T(2,128)S(1)}, u32[]{:S(2)}, u32[]{:S(2)}) collective-permute-start(f32[2,2,64]{2,1,0:T(2,128)S(1)} %get-tuple-element.174), channel_id=1, source_target_pairs={{0,2},{1,3},{2,0},{3,1},{4,6},{5,7},{6,4},{7,5},{8,10},{9,11},{10,... | collective-permute-start | bytes 3080 | tf_op jit(solution)/shard_map/ppermute | solution.py:30
  198.4 5.1 %copy-start.13 = (bf16[256,768]{1,0:T(8,128)(2,1)S(1)}, bf16[256,768]{1,0:T(8,128)(2,1)}, u32[]{:S(2)}) copy-start(bf16[256,768]{1,0:T(8,128)(2,1)} %convert_add_fusion.5) | copy-start | bytes 1179652

commit v4 on v3

--- a/solution.py
+++ b/solution.py
@@ -39,10 +39,12 @@
     return table
 
 
-def chip_sum(kept, sent):
+def chip_sum(kept, sent, raw=None):
     bit = 2
     while True:
         got = swap(sent, "dp", bit)
+        if raw is not None:
+            raw.append(got)
         kept = [kept[i] + got[i].astype(jnp.float32) for i in range(len(kept))]
         if len(kept) == 1:
             return kept[0]
@@ -65,58 +67,69 @@
     return jnp.where(routed & (before < capacity), before, -1)
 
 
-def place_kernel(blocks, peers, scaled, capacity, where, tables, *refs):
-    rows = refs[:blocks]
-    outs = refs[blocks : blocks + len(peers)]
-    choices = refs[-1]
-    tokens = tables.shape[2]
-    cores = tables.shape[0] // blocks
-
-    @pl.when(pl.program_id(0) == 0)
-    def _():
-        slot = lax.broadcasted_iota(jnp.int32, (capacity, tokens), 0)
-        for s in range(tables.shape[0]):
-            table = tables[s]
-            position = slot_positions(table, capacity)
-            value = table if scaled else jnp.where(table > 0, 1.0, 0.0)
-            owner = lax.broadcasted_iota(jnp.int32, table.shape, 0)
-            for n, k in enumerate(peers):
-                mine = owner == (where[0] ^ k)
-                wanted = jnp.sum(jnp.where(mine, position, 0), axis=0, keepdims=True)
-                entry = jnp.sum(jnp.where(mine, value, 0.0), axis=0, keepdims=True)
-                choices[s, n * capacity : (n + 1) * capacity, :] = jnp.where(
-                    slot == wanted, entry, 0.0
+def choose_kernel(peers, capacity, where, tables, *outs):
+    sources, owners, tokens = tables.shape
+    slot = lax.broadcasted_iota(jnp.int32, (capacity, tokens), 0)
+    owner = lax.broadcasted_iota(jnp.int32, (owners, tokens), 0)
+    for s in range(sources):
+        table = tables[s]
+        position = slot_positions(table, capacity)
+        for n, k in enumerate(peers):
+            mine = owner == (where[0] ^ k)
+            wanted = jnp.sum(jnp.where(mine, position, 0), axis=0, keepdims=True)
+            entry = jnp.sum(jnp.where(mine, table, 0.0), axis=0, keepdims=True)
+            for out, value in zip(outs, (entry, jnp.ones_like(entry))):
+                out[s, n * capacity : (n + 1) * capacity, :] = jnp.where(
+                    slot == wanted, value, 0.0
                 ).astype(jnp.bfloat16)
 
-    for s in range(tables.shape[0]):
-        first = (s % cores) * tokens
-        placed = jnp.dot(
-            choices[s],
-            rows[s // cores][first : first + tokens, :],
-            preferred_element_type=jnp.float32,
-        ).astype(jnp.bfloat16)
-        for n in range(len(peers)):
-            outs[n][s * capacity : (s + 1) * capacity, :] = placed[
-                n * capacity : (n + 1) * capacity, :
-            ]
-
-
-def place(where, tables, rows, maps, steps, width, peers, capacity, scaled):
+
+def choose(where, tables, peers, capacity):
     sources, owners, tokens = tables.shape
-    out_shape = (sources * capacity, steps * width)
+    out = jax.ShapeDtypeStruct((sources, len(peers) * capacity, tokens), jnp.bfloat16)
     return pl.pallas_call(
-        functools.partial(place_kernel, len(rows), peers, scaled, capacity),
-        grid_spec=pltpu.PrefetchScalarGridSpec(
-            num_scalar_prefetch=1,
-            grid=(steps,),
-            in_specs=[pl.BlockSpec((sources, owners, tokens), lambda i, w: (0, 0, 0))]
-            + [
-                pl.BlockSpec((r.shape[0], width), functools.partial(lambda m, i, w: (0, m(i)), m))
-                for r, m in zip(rows, maps)
-            ],
-            out_specs=[pl.BlockSpec((out_shape[0], width), lambda i, w: (0, i))] * len(peers),
-            scratch_shapes=[pltpu.VMEM((sources, len(peers) * capacity, tokens), jnp.bfloat16)],
-        ),
+        functools.partial(choose_kernel, peers, capacity),
+        in_specs=[
+            pl.BlockSpec(memory_space=pltpu.SMEM),
+            pl.BlockSpec(memory_space=pltpu.VMEM),
+        ],
+        out_specs=[pl.BlockSpec(memory_space=pltpu.VMEM)] * 2,
+        out_shape=[out] * 2,
+        compiler_params=pltpu.CompilerParams(vmem_limit_bytes=VMEM),
+        cost_estimate=cost(0, 0),
+        name="choose",
+    )(where, tables)
+
+
+def place_kernel(blocks, peers, capacity, *refs):
+    choices, rows, outs = refs[:blocks], refs[blocks : 2 * blocks], refs[2 * blocks :]
+    cores, _, tokens = choices[0].shape
+    for b in range(blocks):
+        for c in range(cores):
+            first = (b * cores + c) * capacity
+            placed = jnp.dot(
+                choices[b][c],
+                rows[b][c * tokens : (c + 1) * tokens, :],
+                preferred_element_type=jnp.float32,
+            ).astype(jnp.bfloat16)
+            for n in range(len(peers)):
+                outs[n][first : first + capacity, :] = placed[n * capacity : (n + 1) * capacity, :]
+
+
+def place(choices, rows, index, steps, width, peers, capacity):
+    blocks = len(rows)
+    cores = 2
+    _, chosen, tokens = choices[0][0].shape
+    out_shape = (blocks * cores * capacity, steps * width)
+    return pl.pallas_call(
+        functools.partial(place_kernel, blocks, peers, capacity),
+        grid=(steps,),
+        in_specs=[
+            pl.BlockSpec((cores, chosen, tokens), functools.partial(lambda o, i: (o, 0, 0), o))
+            for _, o in choices
+        ]
+        + [pl.BlockSpec((r.shape[0], width), lambda i: (0, index(i))) for r in rows],
+        out_specs=[pl.BlockSpec((out_shape[0], width), lambda i: (0, i))] * len(peers),
         out_shape=[jax.ShapeDtypeStruct(out_shape, jnp.bfloat16)] * len(peers),
         compiler_params=pltpu.CompilerParams(vmem_limit_bytes=VMEM),
         cost_estimate=cost(
@@ -124,7 +137,7 @@
             2 * (len(peers) + 1) * out_shape[0] * out_shape[1],
         ),
         name="place",
-    )(where, tables, *rows)
+    )(*[array for array, _ in choices], *rows)
 
 
 def down_kernel(count, hidden_t, *refs):
@@ -297,15 +310,16 @@
     def spread(sent):
         return [sent[0]] + [swap(sent[n], "expert", peers[n]) for n in range(1, len(peers))]
 
-    def place_rows(tables, rows, scaled, steps=None, width=None, index=same):
+    def place_rows(choices, rows, steps=None, width=None, index=same):
         width = width or share
         steps = steps or rows[0].shape[1] // width
-        maps = [index] * len(rows)
-        return place(where, tables, rows, maps, steps, width, peers, capacity, scaled)
+        return place(choices, rows, index, steps, width, peers, capacity)
+
+    scaled_near, plain_near = choose(where, tables_near, peers, capacity)
 
     dy_next = swap(after(dy_own, tables_next), "expert", 1)
     dy_far0 = swap(dy_parts[0], "expert", half)
-    dy_from_own = place_rows(tables_core, [after(dy_own, tables_next)], True)
+    dy_from_own = place_rows([(scaled_near, 0)], [dy_own])
     placed = dy_from_own[0]
     dy_from_own = spread(dy_from_own)
     dy_next, dy_far0, dy_from_own, tables_far, dy1 = lax.optimization_barrier(
@@ -313,7 +327,7 @@
     )
 
     dy_far1 = swap(dy1, "expert", half)
-    dy_from_next = spread(place_rows(tables_next, [dy_next], True))
+    dy_from_next = spread(place_rows([(scaled_near, 1)], [dy_next]))
     dy_far_next0 = swap(dy_far0, "expert", 1)
     x_own = both_cores(after(tokens, placed), [group ^ (2 * r) for r in range(chips)], 0, share)
     part_width = share // X_PARTS
@@ -329,13 +343,14 @@
     ]
     order = me ^ jnp.arange(owners, dtype=jnp.int32)
     saved = jnp.stack([after(saved_gate, placed), saved_up]).reshape(2, owners, capacity, hidden_width)[:, order]
-    dy_far1, dy_from_next, dy_far_next0, x_parts, saved = lax.optimization_barrier(
-        (dy_far1, dy_from_next, dy_far_next0, x_parts, saved)
+    scaled_far, plain_far = choose(where, after(tables_far, dy_from_next[0]), peers, capacity)
+    dy_far1, dy_from_next, dy_far_next0, x_parts, saved, scaled_far = lax.optimization_barrier(
+        (dy_far1, dy_from_next, dy_far_next0, x_parts, saved, scaled_far)
     )
     dy_near = [piece for pair in zip(dy_from_own, dy_from_next) for piece in pair]
 
     x_far0 = swap(x_parts[0], "expert", half)
-    dy_spread0 = spread(place_rows(tables_far, [dy_far0, dy_far_next0], True))
+    dy_spread0 = spread(place_rows([(scaled_far, 0), (scaled_far, 1)], [dy_far0, dy_far_next0]))
     dy_far_next1 = swap(dy_far1, "expert", 1)
     x_next0 = swap(x_parts[0], "expert", 1)
     saved = jnp.stack([after(saved, dy_far_next1), swap(saved, "dp", 1)], axis=2)
@@ -352,7 +367,7 @@
     )
 
     x_far1 = swap(x_parts[1], "expert", half)
-    dy_spread1 = spread(place_rows(tables_far, [dy_far1, dy_far_next1], True))
+    dy_spread1 = spread(place_rows([(scaled_far, 0), (scaled_far, 1)], [dy_far1, dy_far_next1]))
     x_far_next0 = swap(x_far0, "expert", 1)
     x_next1 = swap(x_parts[1], "expert", 1)
     held = after(dy_near[0], dy_spread1[0])
@@ -365,15 +380,16 @@
 
     width = share // X_CHUNKS
     per = X_CHUNKS // X_PARTS
-    tables_all = jnp.concatenate([tables_near, tables_far])
+    plain = [(plain_near, 0), (plain_near, 1), (plain_far, 0), (plain_far, 1)]
     x_far_next1 = swap(x_far1, "expert", 1)
     rows = [x_parts[0], x_next0, x_far0, x_far_next0]
-    x_spread0 = place_rows(tables_all, rows, False, chips, part_width)
+    x_spread0 = place_rows(plain, rows, chips, part_width)
     near = [after(dy_near[0], x_spread0[0], x_far_next1, down[0])] + dy_near[1:]
     x_spread0 = spread(x_spread0)
     terms = down_step(hidden_t, near, dy_spread1, chips // 2, share, per_part)
     near[0] = after(near[0], terms[0][0])
-    down.append(chip_sum(*terms))
+    raw = []
+    down.append(chip_sum(*terms, raw))
     back = back_step(where, matrix, near, dy_spread0, share, 0, None)
     back = back_step(where, matrix, near, dy_spread1, share, per_part, back)
     back = back.reshape(owners, 2, capacity, hidden_width)
@@ -381,9 +397,9 @@
     x_rows = [x_parts[1], x_next1, x_far1]
     x_far_next1, x_spread0 = lax.optimization_barrier((x_far_next1, x_spread0))
     x_spread1 = place_rows(
-        tables_all, x_rows + [x_far_next1], False, chips, part_width
-    )
-    other[0] = after(other[0], x_spread1[0], down[1])
+        plain, x_rows + [x_far_next1], chips, part_width
+    )
+    other[0] = after(other[0], x_spread1[0], raw[-1])
     back = jnp.stack([back[:, g] + other[g].astype(jnp.float32) for g in range(2)], axis=1)
     back = back.reshape(2 * slot_rows, hidden_width)
     grad_pre = (back * gate_act).astype(jnp.bfloat16)
@@ -400,7 +416,7 @@
     returned = exchange(after(slot_grad, up_terms[-1][1]), "expert", near_bits)
     x_spread1 = spread(x_spread1)
     for n in range(per):
-        grad_pre = after(grad_pre, up_parts[n], returned)
+        grad_pre = after(grad_pre, up_parts[n])
         up_terms.append(up_step(grad_pre, x_spread1, n, per, chips))
         grad_pre = after(grad_pre, up_terms[-1][1])
     up_parts += [chip_sum(*terms) for terms in up_terms[per:]]

time: 207 us -> 200 us (0.966)
  waiting for transfers between devices: 91.1 us -> 81 us
  starting transfers between devices: 35.3 us -> 43.6 us
  other arithmetic: 24.4 us -> 20.7 us
  Pallas kernels: 27.2 us -> 24.9 us
    ppermute x36, waiting for transfers between devices: 91.1 us -> 81 us  [swap(): return lax.ppermute(value, axis, [(i, i ^ bit) for i in range(size)])]
    ppermute x36, starting transfers between devices: 35.3 us -> 43.6 us  [swap(): return lax.ppermute(value, axis, [(i, i ^ bit) for i in range(size)])]
    add x5, other arithmetic: 5.9 us -> 3.21 us  [chip_sum(): kept = [kept[i] + got[i].astype(jnp.float32) for i in range(len(kept))]]
    pallas_call x6 -> x8, Pallas kernels: 14 us -> 11.7 us  [the longest x6 10.3 us: place(): pl.pallas_call(functools.partial(place_kernel, blocks, peers, capacity),...]
    unnamed x41 -> x51, local copies, waits for them, and re-layouts: 7.19 us -> 8.74 us
  transfers between devices with their start and end apart: 36 -> 36, of which waited for: 18 -> 15; matrix products, arithmetic and copies ran while one was open for 20% -> 18% of each run, Pallas kernels for 11% -> 11%
where the time goes in v4:
time: 200 us; the launch traced here: 199 us
  waiting for transfers between devices  81 us (40%)
  starting transfers between devices  43.6 us (22%)
  local copies, waits for them, and re-layouts  27.6 us (14%)
  Pallas kernels  24.9 us (12%)
  other arithmetic  20.7 us (10%)
    ppermute x36, waiting for transfers between devices, swap(): return lax.ppermute(value, axis, [(i, i ^ bit) for i in range(size)])  81 us
    ppermute x36, starting transfers between devices, swap(): return lax.ppermute(value, axis, [(i, i ^ bit) for i in range(size)])  43.6 us
    pallas_call x6, Pallas kernels, place(): pl.pallas_call(functools.partial(place_kernel, blocks, peers, capacity),...  10.3 us
    unnamed x51, local copies, waits for them, and re-layouts  8.74 us
    pallas_call x4, Pallas kernels, up_step(): pl.pallas_call(functools.partial(up_kernel, len(pieces)), grid=(pairs,),...  4.86 us
    pallas_call x2, Pallas kernels, back_step(): pl.pallas_call(functools.partial(back_kernel, len(pieces)), grid_spec=plt...  4.76 us
  transfers between devices with their start and end apart: 36, of which 15 were waited for; matrix products, arithmetic and copies ran while one was open for 18% of the time, Pallas kernels for 11%

profile of v4, /device:TPU:0, one launch (start us, length us, event | category | flops | bytes accessed | tf_op | source)
XLA Modules:
  0.0 199.2 jit_solution(17827009776780982891)
XLA Ops:
  0.7 1.3 constant_dynamic-slice_fusion.7
  2.8 1.3 collective-permute-done.1
  4.2 1.1 fusion.24
  5.2 2.9 %collective-permute-start.2 = (f32[2,8,128]{2,1,0:T(8,128)S(1)}, f32[2,8,128]{2,1,0:T(8,128)S(1)}, u32[]{:S(2)}, u32[]{:S(2)}) collective-permute-start(f32[2,8,128]{2,1,0:T(8,128)S(1)} %pad_maximum_fusion.11), channel_id=1, source_target_pairs={{0,1},{1,0},{2,3},{3,2},{4,5},{5,4},{6,7},{7,6},{8,9},{9,8},{10,11... | collective-permute-start | bytes 24584 | tf_op jit(solution)/shard_map/ppermute | solution.py:30
  8.1 1.6 collective-permute-done.2
  9.7 2.0 %collective-permute-start.3 = (bf16[256,2048]{1,0:T(8,128)(2,1)S(1)}, bf16[256,2048]{1,0:T(8,128)(2,1)S(1)}, u32[]{:S(2)}, u32[]{:S(2)}) collective-permute-start(bf16[256,2048]{1,0:T(8,128)(2,1)S(1)} %pad_maximum_fusion.4.refs_1_), channel_id=1, source_target_pairs={{0,1},{1,0},{2,3},{3,2},{4,5},{5,4},{6,7},{7,6},{8,9},{9,8},{10,11... | collective-permute-start | bytes 3145736 | tf_op jit(solution)/shard_map/ppermute | solution.py:30
  11.8 2.6 %collective-permute-start.4 = (bf16[256,1024]{1,0:T(8,128)(2,1)}, bf16[256,1024]{1,0:T(8,128)(2,1)}, u32[]{:S(2)}, u32[]{:S(2)}) collective-permute-start(bf16[256,1024]{1,0:T(8,128)(2,1)} %get-tuple-element.180), channel_id=1, source_target_pairs={{0,4},{1,5},{2,6},{3,7},{4,0},{5,1},{6,2},{7,3},{8,12},{9,13},{10,... | collective-permute-start | bytes 1572872 | tf_op jit(solution)/shard_map/ppermute | solution.py:30
  15.2 1.4 place.6
  16.6 1.6 collective-permute-start.5
  18.2 2.1 %constant_dynamic-slice_fusion.3 = (bf16[128,1024]{1,0:T(8,128)(2,1)}, bf16[128,1024]{1,0:T(8,128)(2,1)S(1)}, bf16[128,1024]{1,0:T(8,128)(2,1)S(1)}, bf16[128,1024]{1,0:T(8,128)(2,1)}) fusion(bf16[128,4096]{1,0:T(8,128)(2,1)} %param.7, s32[]{:T(128)S(6)} %select_n.115, s32[]{:T(128)S(6)} %select_n.118, s32[]{:T(128)S(6)} %select_n.117, s32[]{:T(128)S(6)} %select_n.116), kind=kLoop, calls=%fused_computation.84 | loop fusion | bytes 2097168 | tf_op jit(solution)/shard_map/dynamic_slice | solution.py:285
  21.5 2.7 %pad_maximum_fusion.1 = bf16[2,8,64,768]{3,2,1,0:T(8,128)(2,1)} fusion(bf16[1,8,64,768]{3,2,1,0:T(8,128)(2,1)} %bitcast.150, bf16[1,8,64,768]{3,2,1,0:T(8,128)(2,1)} %bitcast.151), kind=kLoop, calls=%fused_computation.28 | loop fusion | flops 786432 | bytes 3145728 | tf_op jit(solution)/shard_map/stack | solution.py:345
  24.2 3.2 %gather_fusion = bf16[8,2,64,768]{3,2,1,0:T(8,128)(2,1)} fusion(bf16[2,8,64,768]{3,2,1,0:T(8,128)(2,1)} %pad_maximum_fusion.1, s32[1024]{0:T(1024)S(1)} %pad_clamp_fusion), kind=kCustom, calls=%fused_computation | custom fusion | bytes 3145760 | tf_op jit(solution)/shard_map/gather | solution.py:345
  27.4 10.0 %collective-permute-done.6.tables = f32[4,8,128]{2,1,0:T(8,128)S(1)} collective-permute-done((f32[4,8,128]{2,1,0:T(8,128)S(1)}, f32[4,8,128]{2,1,0:T(8,128)S(1)}, u32[]{:S(2)}, u32[]{:S(2)}) %collective-permute-start.6) | collective-permute-done | bytes 16416 | tf_op jit(solution)/shard_map/ppermute | solution.py:30
  37.4 2.2 %collective-permute-done.5.refs_2_ = bf16[128,2048]{1,0:T(8,128)(2,1)S(1)} collective-permute-done((bf16[128,2048]{1,0:T(8,128)(2,1)}, bf16[128,2048]{1,0:T(8,128)(2,1)S(1)}, u32[]{:S(2)}, u32[]{:S(2)}) %collective-permute-start.5) | collective-permute-done | bytes 524320 | tf_op jit(solution)/shard_map/ppermute | solution.py:30
  41.4 2.4 %collective-permute-start.8 = (bf16[128,2048]{1,0:T(8,128)(2,1)S(1)}, bf16[128,2048]{1,0:T(8,128)(2,1)S(1)}, u32[]{:S(2)}, u32[]{:S(2)}) collective-permute-start(bf16[128,2048]{1,0:T(8,128)(2,1)S(1)} %get-tuple-element.87), channel_id=1, source_target_pairs={{0,2},{1,3},{2,0},{3,1},{4,6},{5,7},{6,4},{7,5},{8,10},{9,11},{10,... | collective-permute-start | bytes 1572872 | tf_op jit(solution)/shard_map/ppermute | solution.py:30
  43.8 1.3 pad_maximum_fusion.5
  45.2 1.1 pad_maximum_fusion.8
  47.1 15.8 %collective-permute-done.7.refs_2_ = bf16[256,1024]{1,0:T(8,128)(2,1)} collective-permute-done((bf16[256,1024]{1,0:T(8,128)(2,1)}, bf16[256,1024]{1,0:T(8,128)(2,1)}, u32[]{:S(2)}, u32[]{:S(2)}) %collective-permute-start.7) | collective-permute-done | bytes 524320 | tf_op jit(solution)/shard_map/ppermute | solution.py:30
  63.6 1.4 collective-permute-start.13
  65.7 1.7 collective-permute-start.11
  67.4 1.0 copy-done.7
  68.4 2.3 %place.8 = (bf16[256,1024]{1,0:T(8,128)(2,1)S(1)}, bf16[256,1024]{1,0:T(8,128)(2,1)}) custom-call(bf16[4,128,128]{2,1,0:T(8,128)(2,1)S(1)} %get-tuple-element.95.refs_0_.refs_1_, bf16[4,128,128]{2,1,0:T(8,128)(2,1)S(1)} %get-tuple-element.95.refs_0_.refs_1_, bf16[256,1024]{1,0:T(8,128)(2,1)} %collective-permute-done.4.refs_2_, bf16[256,1024]{1,0:T(8,128)(2,1)S(1)} %copy-done.7), custom_call_target="tpu_custom_call" | custom-call | tf_op jit(solution)/shard_map/place/pallas_call | solution.py:124
  70.7 2.5 %collective-permute-start.12 = (bf16[256,1024]{1,0:T(8,128)(2,1)}, bf16[256,1024]{1,0:T(8,128)(2,1)S(1)}, u32[]{:S(2)}, u32[]{:S(2)}) collective-permute-start(bf16[256,1024]{1,0:T(8,128)(2,1)} %get-tuple-element.98), channel_id=1, source_target_pairs={{0,2},{1,3},{2,0},{3,1},{4,6},{5,7},{6,4},{7,5},{8,10},{9,11},{10,... | collective-permute-start | bytes 1572872 | tf_op jit(solution)/shard_map/ppermute | solution.py:30
  73.2 5.5 %collective-permute-done.13.refs_3_ = bf16[256,1024]{1,0:T(8,128)(2,1)} collective-permute-done((bf16[256,1024]{1,0:T(8,128)(2,1)}, bf16[256,1024]{1,0:T(8,128)(2,1)}, u32[]{:S(2)}, u32[]{:S(2)}) %collective-permute-start.13) | collective-permute-done | bytes 524320 | tf_op jit(solution)/shard_map/ppermute | solution.py:30
  78.7 2.3 %maximum_convert_fusion = f32[2,8,2,64,768]{4,3,0,1,2:T(8,128)S(1)} fusion(bf16[2,8,1,64,768]{4,3,0,1,2:T(8,128)(2,1)} %bitcast.11, bf16[2,8,1,64,768]{4,3,0,1,2:T(8,128)(2,1)} %bitcast.10), kind=kLoop, calls=%fused_computation.5 | loop fusion | flops 3145728 | bytes 9437184 | tf_op jit(solution)/shard_map/convert_element_type | solution.py:357
  81.0 4.0 %slice_bitcast_fusion = (f32[8,2,64,768]{3,2,0,1:T(8,128)}, f32[8,2,64,768]{3,2,0,1:T(8,128)}, f32[1,8,2,64,768]{4,3,0,1,2:T(8,128)S(1)}, f32[1,8,2,64,768]{4,3,1,2,0:T(8,128)S(1)}) fusion(f32[2,8,2,64,768]{4,3,0,1,2:T(8,128)S(1)} %maximum_convert_fusion), kind=kLoop, calls=%fused_computation.17 | loop fusion | bytes 18874368 | tf_op jit(solution)/shard_map/squeeze | solution.py:358
  86.2 1.5 copy-done.12
  87.7 2.1 %fusion.1 = bf16[1024,768]{1,0:T(8,128)(2,1)} fusion(f32[1,8,2,64,768]{4,3,2,1,0:T(8,128)S(1)} %copy.43, f32[1,8,2,64,768]{4,3,2,1,0:T(8,128)S(1)} %copy.42), kind=kLoop, calls=%fused_computation.10 | loop fusion | flops 4718592 | bytes 7864320 | tf_op jit(solution)/shard_map/convert_element_type | solution.py:359
  89.8 2.6 %copy.44 = bf16[768,1024]{1,0:T(8,128)(2,1)} copy(bf16[768,1024]{0,1:T(8,128)(2,1)} %bitcast.146) | data formatting | bytes 3145728 | tf_op jit(solution)/shard_map/transpose | solution.py:361
  92.3 1.5 dynamic-slice_bitcast_fusion.3
  94.0 1.3 collective-permute-done.12.refs_5_
  95.3 1.6 place.9
  96.9 1.8 down_step.2
  98.7 1.6 collective-permute-start.16
  100.3 1.5 collective-permute-start.19
  102.3 3.1 %collective-permute-start.17 = (bf16[256,1024]{1,0:T(8,128)(2,1)S(1)}, bf16[256,1024]{1,0:T(8,128)(2,1)S(1)}, u32[]{:S(2)}, u32[]{:S(2)}) collective-permute-start(bf16[256,1024]{1,0:T(8,128)(2,1)S(1)} %copy-done.2), channel_id=1, source_target_pairs={{0,4},{1,5},{2,6},{3,7},{4,0},{5,1},{6,2},{7,3},{8,12},{9,13},{10,... | collective-permute-start | bytes 1572872 | tf_op jit(solution)/shard_map/ppermute | solution.py:30
  105.4 17.1 %collective-permute-done.18.refs_5_ = bf16[256,1024]{1,0:T(8,128)(2,1)S(1)} collective-permute-done((bf16[256,1024]{1,0:T(8,128)(2,1)S(1)}, bf16[256,1024]{1,0:T(8,128)(2,1)S(1)}, u32[]{:S(2)}, u32[]{:S(2)}) %collective-permute-start.18) | collective-permute-done | bytes 524320 | tf_op jit(solution)/shard_map/ppermute | solution.py:30
  122.5 1.9 collective-permute-done.20.refs_5_
  124.4 2.5 %collective-permute-done.17.refs_6_ = bf16[256,1024]{1,0:T(8,128)(2,1)S(1)} collective-permute-done((bf16[256,1024]{1,0:T(8,128)(2,1)S(1)}, bf16[256,1024]{1,0:T(8,128)(2,1)S(1)}, u32[]{:S(2)}, u32[]{:S(2)}) %collective-permute-start.17) | collective-permute-done | bytes 524320 | tf_op jit(solution)/shard_map/ppermute | solution.py:30
  126.9 1.4 collective-permute-start.21
  128.3 2.3 %place.10 = (bf16[512,1024]{1,0:T(8,128)(2,1)S(1)}, bf16[512,1024]{1,0:T(8,128)(2,1)S(1)}) custom-call(bf16[4,128,128]{2,1,0:T(8,128)(2,1)S(1)} %get-tuple-element.115.refs_0_.refs_1_, bf16[4,128,128]{2,1,0:T(8,128)(2,1)S(1)} %get-tuple-element.115.refs_0_.refs_1_, bf16[4,128,128]{2,1,0:T(8,128)(2,1)S(1)} %get-tuple-element.116.refs_2_.refs_3_, ...), custom_call_target="tpu_custom_call" | custom-call | tf_op jit(solution)/shard_map/place/pallas_call | solution.py:124
  130.7 1.5 convert_add_fusion.1
  132.2 3.9 %collective-permute-done.21.refs_7_ = bf16[256,1024]{1,0:T(8,128)(2,1)S(1)} collective-permute-done((bf16[256,1024]{1,0:T(8,128)(2,1)S(1)}, bf16[256,1024]{1,0:T(8,128)(2,1)S(1)}, u32[]{:S(2)}, u32[]{:S(2)}) %collective-permute-start.21) | collective-permute-done | bytes 524320 | tf_op jit(solution)/shard_map/ppermute | solution.py:30
  136.1 1.8 down_step.3
  137.9 1.1 copy-done.3
  139.6 2.4 %back_step.2.refs_6_ = f32[1024,768]{1,0:T(8,128)S(1)} custom-call(s32[2]{0:T(128)S(1)} %copy-done.10, bf16[768,4096]{1,0:T(8,128)(2,1)S(1)} %bitcast.134, bf16[128,2048]{1,0:T(8,128)(2,1)S(1)} %get-tuple-element.129.refs_0_, bf16[128,2048]{1,0:T(8,128)(2,1)S(1)} %get-tuple-element.108.refs_1_, bf16[128,2048]{1,0:T(8,128)(2,1)S(1)} %collective-permute-done.5.refs_2_, ...), custom_call_target="tpu_custom_call" | custom-call | tf_op jit(solution)/shard_map/back_step/pallas_call | solution.py:199
  142.0 2.4 %back_step.3 = f32[1024,768]{1,0:T(8,128)S(1)} custom-call(s32[2]{0:T(128)S(1)} %copy-done.10, bf16[768,4096]{1,0:T(8,128)(2,1)S(1)} %bitcast.135, bf16[128,2048]{1,0:T(8,128)(2,1)S(1)} %get-tuple-element.129.refs_0_, bf16[128,2048]{1,0:T(8,128)(2,1)S(1)} %get-tuple-element.108.refs_1_, bf16[128,2048]{1,0:T(8,128)(2,1)S(1)} %collective-permute-done.5.refs_2_, ...), custom_call_target="tpu_custom_call" | custom-call | tf_op jit(solution)/shard_map/back_step/pallas_call | solution.py:199
  145.6 5.4 %collective-permute-done.23.refs_1_.refs_3_.refs_5_.refs_7_ = bf16[512,1024]{1,0:T(8,128)(2,1)S(1)} collective-permute-done((bf16[512,1024]{1,0:T(8,128)(2,1)S(1)}, bf16[512,1024]{1,0:T(8,128)(2,1)S(1)}, u32[]{:S(2)}, u32[]{:S(2)}) %collective-permute-start.23) | collective-permute-done | bytes 1048608 | tf_op jit(solution)/shard_map/ppermute | solution.py:30
  151.0 1.9 place.11
  152.9 1.6 collective-permute-start.30
  156.0 1.6 copy-done.13
  159.6 1.8 up_step.4
  161.5 1.4 copy-done.15
  164.6 1.3 slice.101
  165.9 1.6 collective-permute-start.29
  167.6 4.4 %collective-permute-start.34 = (f32[1,4,64]{2,1,0:T(4,128)S(1)}, f32[1,4,64]{2,1,0:T(4,128)S(1)}, u32[]{:S(2)}, u32[]{:S(2)}) collective-permute-start(f32[1,4,64]{2,1,0:T(4,128)S(1)} %get-tuple-element.188), channel_id=1, source_target_pairs={{0,4},{1,5},{2,6},{3,7},{4,0},{5,1},{6,2},{7,3},{8,12},{9,13},{10,... | collective-permute-start | bytes 3080 | tf_op jit(solution)/shard_map/ppermute | solution.py:30
  172.0 4.4 %collective-permute-done.26 = bf16[1,256,768]{2,1,0:T(8,128)(2,1)} collective-permute-done((bf16[1,256,768]{2,1,0:T(8,128)(2,1)}, bf16[1,256,768]{2,1,0:T(8,128)(2,1)}, u32[]{:S(2)}, u32[]{:S(2)}) %collective-permute-start.26) | collective-permute-done | bytes 393248 | tf_op jit(solution)/shard_map/ppermute | solution.py:30
  176.3 1.3 convert_add_fusion.5
  180.3 2.9 %collective-permute-done.29 = bf16[1,256,768]{2,1,0:T(8,128)(2,1)S(1)} collective-permute-done((bf16[1,256,768]{2,1,0:T(8,128)(2,1)S(1)}, bf16[1,256,768]{2,1,0:T(8,128)(2,1)S(1)}, u32[]{:S(2)}, u32[]{:S(2)}) %collective-permute-start.29) | collective-permute-done | bytes 393248 | tf_op jit(solution)/shard_map/ppermute | solution.py:30
  184.3 1.2 collective-permute-start.32
  185.5 5.2 %collective-permute-done.31 = bf16[1,256,768]{2,1,0:T(8,128)(2,1)S(1)} collective-permute-done((bf16[1,256,768]{2,1,0:T(8,128)(2,1)S(1)}, bf16[1,256,768]{2,1,0:T(8,128)(2,1)S(1)}, u32[]{:S(2)}, u32[]{:S(2)}) %collective-permute-start.31) | collective-permute-done | bytes 393248 | tf_op jit(solution)/shard_map/ppermute | solution.py:30
  190.8 3.3 %collective-permute-start.35 = (f32[2,2,64]{2,1,0:T(2,128)S(1)}, f32[2,2,64]{2,1,0:T(2,128)S(1)}, u32[]{:S(2)}, u32[]{:S(2)}) collective-permute-start(f32[2,2,64]{2,1,0:T(2,128)S(1)} %get-tuple-element.186), channel_id=1, source_target_pairs={{0,2},{1,3},{2,0},{3,1},{4,6},{5,7},{6,4},{7,5},{8,10},{9,11},{10,... | collective-permute-start | bytes 3080 | tf_op jit(solution)/shard_map/ppermute | solution.py:30
  194.4 2.0 maximum_bitcast_fusion
  196.5 1.2 pad_maximum_fusion.3
  (135 shorter events, 21.5 us)
Async XLA Ops:
  0.6 1.9 copy-start.20
  0.6 1.9 copy-start.19
  2.0 2.1 %collective-permute-start = (bf16[128,2048]{1,0:T(8,128)(2,1)S(1)}, bf16[128,2048]{1,0:T(8,128)(2,1)S(1)}, u32[]{:S(2)}, u32[]{:S(2)}) collective-permute-start(bf16[128,2048]{1,0:T(8,128)(2,1)S(1)} %pad_maximum_fusion.6), channel_id=1, source_target_pairs={{0,8},{8,0},{16,24},{24,16},{1,9},{9,1},{17,25},{25,17},{2,10},{10... | collective-permute-start | bytes 1572872 | tf_op jit(solution)/shard_map/ppermute | solution.py:30
  2.6 1.4 collective-permute-start.1
  5.2 4.5 %collective-permute-start.2 = (f32[2,8,128]{2,1,0:T(8,128)S(1)}, f32[2,8,128]{2,1,0:T(8,128)S(1)}, u32[]{:S(2)}, u32[]{:S(2)}) collective-permute-start(f32[2,8,128]{2,1,0:T(8,128)S(1)} %pad_maximum_fusion.11), channel_id=1, source_target_pairs={{0,1},{1,0},{2,3},{3,2},{4,5},{5,4},{6,7},{7,6},{8,9},{9,8},{10,11... | collective-permute-start | bytes 24584 | tf_op jit(solution)/shard_map/ppermute | solution.py:30
  9.7 29.8 %collective-permute-start.3 = (bf16[256,2048]{1,0:T(8,128)(2,1)S(1)}, bf16[256,2048]{1,0:T(8,128)(2,1)S(1)}, u32[]{:S(2)}, u32[]{:S(2)}) collective-permute-start(bf16[256,2048]{1,0:T(8,128)(2,1)S(1)} %pad_maximum_fusion.4.refs_1_), channel_id=1, source_target_pairs={{0,1},{1,0},{2,3},{3,2},{4,5},{5,4},{6,7},{7,6},{8,9},{9,8},{10,11... | collective-permute-start | bytes 3145736 | tf_op jit(solution)/shard_map/ppermute | solution.py:30
  11.8 3.4 %copy-start.8 = (s32[2]{0:T(128)}, s32[2]{0:T(128)S(1)}, u32[]{:S(2)}) copy-start(s32[2]{0:T(128)S(1)} %pad_add_fusion.where) | copy-start | bytes 28
  11.8 25.5 %collective-permute-start.4 = (bf16[256,1024]{1,0:T(8,128)(2,1)}, bf16[256,1024]{1,0:T(8,128)(2,1)}, u32[]{:S(2)}, u32[]{:S(2)}) collective-permute-start(bf16[256,1024]{1,0:T(8,128)(2,1)} %get-tuple-element.180), channel_id=1, source_target_pairs={{0,4},{1,5},{2,6},{3,7},{4,0},{5,1},{6,2},{7,3},{8,12},{9,13},{10,... | collective-permute-start | bytes 1572872 | tf_op jit(solution)/shard_map/ppermute | solution.py:30
  16.6 22.9 %collective-permute-start.5 = (bf16[128,2048]{1,0:T(8,128)(2,1)}, bf16[128,2048]{1,0:T(8,128)(2,1)S(1)}, u32[]{:S(2)}, u32[]{:S(2)}) collective-permute-start(bf16[128,2048]{1,0:T(8,128)(2,1)} %get-tuple-element.83), channel_id=1, source_target_pairs={{0,2},{1,3},{2,0},{3,1},{4,6},{5,7},{6,4},{7,5},{8,10},{9,11},{10,... | collective-permute-start | bytes 1572872 | tf_op jit(solution)/shard_map/ppermute | solution.py:30
  21.1 22.7 %collective-permute-start.10 = (bf16[128,2048]{1,0:T(8,128)(2,1)}, bf16[128,2048]{1,0:T(8,128)(2,1)}, u32[]{:S(2)}, u32[]{:S(2)}) collective-permute-start(bf16[128,2048]{1,0:T(8,128)(2,1)} %pad_maximum_fusion.7), channel_id=1, source_target_pairs={{0,8},{8,0},{16,24},{24,16},{1,9},{9,1},{17,25},{25,17},{2,10},{10... | collective-permute-start | bytes 1572872 | tf_op jit(solution)/shard_map/ppermute | solution.py:30
  21.1 16.3 %collective-permute-start.6 = (f32[4,8,128]{2,1,0:T(8,128)S(1)}, f32[4,8,128]{2,1,0:T(8,128)S(1)}, u32[]{:S(2)}, u32[]{:S(2)}) collective-permute-start(f32[4,8,128]{2,1,0:T(8,128)S(1)} %pad_maximum_fusion.10.tables), channel_id=1, source_target_pairs={{0,4},{1,5},{2,6},{3,7},{4,0},{5,1},{6,2},{7,3},{8,12},{9,13},{10,... | collective-permute-start | bytes 49160 | tf_op jit(solution)/shard_map/ppermute | solution.py:30
  39.6 23.3 %collective-permute-start.7 = (bf16[256,1024]{1,0:T(8,128)(2,1)}, bf16[256,1024]{1,0:T(8,128)(2,1)}, u32[]{:S(2)}, u32[]{:S(2)}) collective-permute-start(bf16[256,1024]{1,0:T(8,128)(2,1)} %get-tuple-element.84), channel_id=1, source_target_pairs={{0,4},{1,5},{2,6},{3,7},{4,0},{5,1},{6,2},{7,3},{8,12},{9,13},{10,... | collective-permute-start | bytes 1572872 | tf_op jit(solution)/shard_map/ppermute | solution.py:30
  40.1 22.7 %collective-permute-start.9 = (bf16[256,1024]{1,0:T(8,128)(2,1)}, bf16[256,1024]{1,0:T(8,128)(2,1)S(1)}, u32[]{:S(2)}, u32[]{:S(2)}) collective-permute-start(bf16[256,1024]{1,0:T(8,128)(2,1)} %collective-permute-done.4.refs_2_), channel_id=1, source_target_pairs={{0,1},{1,0},{2,3},{3,2},{4,5},{5,4},{6,7},{7,6},{8,9},{9,8},{10,11... | collective-permute-start | bytes 1572872 | tf_op jit(solution)/shard_map/ppermute | solution.py:30
  41.4 22.3 %collective-permute-start.8 = (bf16[128,2048]{1,0:T(8,128)(2,1)S(1)}, bf16[128,2048]{1,0:T(8,128)(2,1)S(1)}, u32[]{:S(2)}, u32[]{:S(2)}) collective-permute-start(bf16[128,2048]{1,0:T(8,128)(2,1)S(1)} %get-tuple-element.87), channel_id=1, source_target_pairs={{0,2},{1,3},{2,0},{3,1},{4,6},{5,7},{6,4},{7,5},{8,10},{9,11},{10,... | collective-permute-start | bytes 1572872 | tf_op jit(solution)/shard_map/ppermute | solution.py:30
  43.8 2.5 %copy-start.9 = (s32[2]{0:T(128)S(1)}, s32[2]{0:T(128)}, u32[]{:S(2)}) copy-start(s32[2]{0:T(128)} %copy-done.8) | copy-start | bytes 28
  62.8 0.8 copy-start.6
  63.6 15.0 %collective-permute-start.15 = (bf16[2,8,64,768]{3,2,0,1:T(8,128)(2,1)}, bf16[2,8,64,768]{3,2,0,1:T(8,128)(2,1)}, u32[]{:S(2)}, u32[]{:S(2)}) collective-permute-start(bf16[2,8,64,768]{3,2,0,1:T(8,128)(2,1)} %bitcast.9), channel_id=1, source_target_pairs={{0,8},{8,0},{16,24},{24,16},{1,9},{9,1},{17,25},{25,17},{2,10},{10... | collective-permute-start | bytes 4718600 | tf_op jit(solution)/shard_map/ppermute | solution.py:30
  63.6 15.0 %collective-permute-start.13 = (bf16[256,1024]{1,0:T(8,128)(2,1)}, bf16[256,1024]{1,0:T(8,128)(2,1)}, u32[]{:S(2)}, u32[]{:S(2)}) collective-permute-start(bf16[256,1024]{1,0:T(8,128)(2,1)} %collective-permute-done.7.refs_2_), channel_id=1, source_target_pairs={{0,1},{1,0},{2,3},{3,2},{4,5},{5,4},{6,7},{7,6},{8,9},{9,8},{10,11... | collective-permute-start | bytes 1572872 | tf_op jit(solution)/shard_map/ppermute | solution.py:30
  65.0 30.2 %collective-permute-start.14 = (bf16[256,1024]{1,0:T(8,128)(2,1)}, bf16[256,1024]{1,0:T(8,128)(2,1)}, u32[]{:S(2)}, u32[]{:S(2)}) collective-permute-start(bf16[256,1024]{1,0:T(8,128)(2,1)} %get-tuple-element.117.refs_4_), channel_id=1, source_target_pairs={{0,1},{1,0},{2,3},{3,2},{4,5},{5,4},{6,7},{7,6},{8,9},{9,8},{10,11... | collective-permute-start | bytes 1572872 | tf_op jit(solution)/shard_map/ppermute | solution.py:30
  65.7 29.6 %collective-permute-start.11 = (bf16[256,1024]{1,0:T(8,128)(2,1)}, bf16[256,1024]{1,0:T(8,128)(2,1)}, u32[]{:S(2)}, u32[]{:S(2)}) collective-permute-start(bf16[256,1024]{1,0:T(8,128)(2,1)} %get-tuple-element.117.refs_4_), channel_id=1, source_target_pairs={{0,4},{1,5},{2,6},{3,7},{4,0},{5,1},{6,2},{7,3},{8,12},{9,13},{10,... | collective-permute-start | bytes 1572872 | tf_op jit(solution)/shard_map/ppermute | solution.py:30
  67.4 1.0 copy-start.7
  70.7 24.5 %collective-permute-start.12 = (bf16[256,1024]{1,0:T(8,128)(2,1)}, bf16[256,1024]{1,0:T(8,128)(2,1)S(1)}, u32[]{:S(2)}, u32[]{:S(2)}) collective-permute-start(bf16[256,1024]{1,0:T(8,128)(2,1)} %get-tuple-element.98), channel_id=1, source_target_pairs={{0,2},{1,3},{2,0},{3,1},{4,6},{5,7},{6,4},{7,5},{8,10},{9,11},{10,... | collective-permute-start | bytes 1572872 | tf_op jit(solution)/shard_map/ppermute | solution.py:30
  81.0 4.6 %copy-start.11 = (f32[2,8,2,64,768]{4,3,0,1,2:T(8,128)}, f32[2,8,2,64,768]{4,3,0,1,2:T(8,128)S(1)}, u32[]{:S(2)}) copy-start(f32[2,8,2,64,768]{4,3,0,1,2:T(8,128)S(1)} %maximum_convert_fusion) | copy-start | bytes 18874372
  85.9 1.8 copy-start.12
  93.9 7.8 %copy-start.2 = (bf16[256,1024]{1,0:T(8,128)(2,1)S(1)}, bf16[256,1024]{1,0:T(8,128)(2,1)}, u32[]{:S(2)}) copy-start(bf16[256,1024]{1,0:T(8,128)(2,1)} %get-tuple-element.120.refs_4_) | copy-start | bytes 1572868
  96.9 42.7 %slice-start = ((s8[6291456]{0:T(1024)(128)(4,1)}), s8[4194304]{0:T(1024)(128)(4,1)S(1)}, s32[]{:S(2)}) async-start(s8[6291456]{0:T(1024)(128)(4,1)} %bitcast.132), calls=%async_computation | async-start | bytes 8388608
  98.7 32.0 %collective-permute-start.16 = (bf16[1,384,1024]{2,1,0:T(8,128)(2,1)S(1)}, bf16[1,384,1024]{2,1,0:T(8,128)(2,1)S(1)}, u32[]{:S(2)}, u32[]{:S(2)}) collective-permute-start(bf16[1,384,1024]{2,1,0:T(8,128)(2,1)S(1)} %bitcast.138), channel_id=1, source_target_pairs={{0,16},{8,24},{16,0},{24,8},{1,17},{9,25},{17,1},{25,9},{2,18},{10... | collective-permute-start | bytes 2359304 | tf_op jit(solution)/shard_map/ppermute | solution.py:30
  100.3 22.2 %collective-permute-start.18 = (bf16[256,1024]{1,0:T(8,128)(2,1)S(1)}, bf16[256,1024]{1,0:T(8,128)(2,1)S(1)}, u32[]{:S(2)}, u32[]{:S(2)}) collective-permute-start(bf16[256,1024]{1,0:T(8,128)(2,1)S(1)} %get-tuple-element.121), channel_id=1, source_target_pairs={{0,2},{1,3},{2,0},{3,1},{4,6},{5,7},{6,4},{7,5},{8,10},{9,11},{10,... | collective-permute-start | bytes 1572872 | tf_op jit(solution)/shard_map/ppermute | solution.py:30
  100.3 22.2 %collective-permute-start.19 = (bf16[256,1024]{1,0:T(8,128)(2,1)}, bf16[256,1024]{1,0:T(8,128)(2,1)S(1)}, u32[]{:S(2)}, u32[]{:S(2)}) collective-permute-start(bf16[256,1024]{1,0:T(8,128)(2,1)} %collective-permute-done.11.refs_6_), channel_id=1, source_target_pairs={{0,1},{1,0},{2,3},{3,2},{4,5},{5,4},{6,7},{7,6},{8,9},{9,8},{10,11... | collective-permute-start | bytes 1572872 | tf_op jit(solution)/shard_map/ppermute | solution.py:30
  101.8 22.6 %collective-permute-start.20 = (bf16[256,1024]{1,0:T(8,128)(2,1)S(1)}, bf16[256,1024]{1,0:T(8,128)(2,1)S(1)}, u32[]{:S(2)}, u32[]{:S(2)}) collective-permute-start(bf16[256,1024]{1,0:T(8,128)(2,1)S(1)} %copy-done.2), channel_id=1, source_target_pairs={{0,1},{1,0},{2,3},{3,2},{4,5},{5,4},{6,7},{7,6},{8,9},{9,8},{10,11... | collective-permute-start | bytes 1572872 | tf_op jit(solution)/shard_map/ppermute | solution.py:30
  102.3 24.6 %collective-permute-start.17 = (bf16[256,1024]{1,0:T(8,128)(2,1)S(1)}, bf16[256,1024]{1,0:T(8,128)(2,1)S(1)}, u32[]{:S(2)}, u32[]{:S(2)}) collective-permute-start(bf16[256,1024]{1,0:T(8,128)(2,1)S(1)} %copy-done.2), channel_id=1, source_target_pairs={{0,4},{1,5},{2,6},{3,7},{4,0},{5,1},{6,2},{7,3},{8,12},{9,13},{10,... | collective-permute-start | bytes 1572872 | tf_op jit(solution)/shard_map/ppermute | solution.py:30
  126.9 9.2 %collective-permute-start.21 = (bf16[256,1024]{1,0:T(8,128)(2,1)S(1)}, bf16[256,1024]{1,0:T(8,128)(2,1)S(1)}, u32[]{:S(2)}, u32[]{:S(2)}) collective-permute-start(bf16[256,1024]{1,0:T(8,128)(2,1)S(1)} %collective-permute-done.17.refs_6_), channel_id=1, source_target_pairs={{0,1},{1,0},{2,3},{3,2},{4,5},{5,4},{6,7},{7,6},{8,9},{9,8},{10,11... | collective-permute-start | bytes 1572872 | tf_op jit(solution)/shard_map/ppermute | solution.py:30
  130.6 9.0 %slice-start.1 = ((s8[6291456]{0:T(1024)(128)(4,1)}), s8[2097152]{0:T(1024)(128)(4,1)S(1)}, s32[]{:S(2)}) async-start(s8[6291456]{0:T(1024)(128)(4,1)} %bitcast.132), calls=%async_computation.1 | async-start | bytes 4194304
  130.6 20.4 %collective-permute-start.23 = (bf16[512,1024]{1,0:T(8,128)(2,1)S(1)}, bf16[512,1024]{1,0:T(8,128)(2,1)S(1)}, u32[]{:S(2)}, u32[]{:S(2)}) collective-permute-start(bf16[512,1024]{1,0:T(8,128)(2,1)S(1)} %get-tuple-element.131), channel_id=1, source_target_pairs={{0,2},{1,3},{2,0},{3,1},{4,6},{5,7},{6,4},{7,5},{8,10},{9,11},{10,... | collective-permute-start | bytes 3145736 | tf_op jit(solution)/shard_map/ppermute | solution.py:30
  132.2 7.4 %copy-start.10 = (s32[2]{0:T(128)S(1)}, s32[2]{0:T(128)}, u32[]{:S(2)}) copy-start(s32[2]{0:T(128)} %copy-done.8) | copy-start | bytes 28
  137.9 1.1 copy-start.3
  139.0 15.5 %collective-permute-start.24 = (bf16[1,384,1024]{2,1,0:T(8,128)(2,1)S(1)}, bf16[1,384,1024]{2,1,0:T(8,128)(2,1)S(1)}, u32[]{:S(2)}, u32[]{:S(2)}) collective-permute-start(bf16[1,384,1024]{2,1,0:T(8,128)(2,1)S(1)} %bitcast.139), channel_id=1, source_target_pairs={{0,16},{8,24},{16,0},{24,8},{1,17},{9,25},{17,1},{25,9},{2,18},{10... | collective-permute-start | bytes 2359304 | tf_op jit(solution)/shard_map/ppermute | solution.py:30
  139.6 5.6 %slice-start.2 = ((s8[6291456]{0:T(1024)(128)(4,1)}), s8[4194304]{0:T(1024)(128)(4,1)S(1)}, s32[]{:S(2)}) async-start(s8[6291456]{0:T(1024)(128)(4,1)} %bitcast.143), calls=%async_computation.2 | async-start | bytes 8388608
  141.9 3.2 %slice-start.3 = ((s8[6291456]{0:T(1024)(128)(4,1)}), s8[2097152]{0:T(1024)(128)(4,1)S(1)}, s32[]{:S(2)}) async-start(s8[6291456]{0:T(1024)(128)(4,1)} %bitcast.143), calls=%async_computation.3 | async-start | bytes 4194304
  144.6 10.0 %collective-permute-start.22 = (bf16[8,64,768]{2,1,0:T(8,128)(2,1)S(1)}, bf16[8,64,768]{2,1,0:T(8,128)(2,1)S(1)}, u32[]{:S(2)}, u32[]{:S(2)}) collective-permute-start(bf16[8,64,768]{2,1,0:T(8,128)(2,1)S(1)} %get-tuple-element.161), channel_id=1, source_target_pairs={{0,8},{8,0},{16,24},{24,16},{1,9},{9,1},{17,25},{25,17},{2,10},{10... | collective-permute-start | bytes 2359304 | tf_op jit(solution)/shard_map/ppermute | solution.py:30
  144.6 9.9 %collective-permute-start.25 = (bf16[8,64,768]{2,1,0:T(8,128)(2,1)S(1)}, bf16[8,64,768]{2,1,0:T(8,128)(2,1)S(1)}, u32[]{:S(2)}, u32[]{:S(2)}) collective-permute-start(bf16[8,64,768]{2,1,0:T(8,128)(2,1)S(1)} %get-tuple-element.162), channel_id=1, source_target_pairs={{0,8},{8,0},{16,24},{24,16},{1,9},{9,1},{17,25},{25,17},{2,10},{10... | collective-permute-start | bytes 2359304 | tf_op jit(solution)/shard_map/ppermute | solution.py:30
  152.9 24.8 %collective-permute-start.30 = (bf16[512,1024]{1,0:T(8,128)(2,1)}, bf16[512,1024]{1,0:T(8,128)(2,1)S(1)}, u32[]{:S(2)}, u32[]{:S(2)}) collective-permute-start(bf16[512,1024]{1,0:T(8,128)(2,1)} %get-tuple-element.146), channel_id=1, source_target_pairs={{0,2},{1,3},{2,0},{3,1},{4,6},{5,7},{6,4},{7,5},{8,10},{9,11},{10,... | collective-permute-start | bytes 3145736 | tf_op jit(solution)/shard_map/ppermute | solution.py:30
  154.5 0.9 copy-start.17
  155.7 1.9 copy-start.13
  158.4 1.2 copy-start
  159.6 1.9 copy-start.14
  159.6 3.3 %copy-start.15 = (f32[8,2,64,768]{3,2,0,1:T(8,128)S(1)}, f32[8,2,64,768]{3,2,0,1:T(8,128)}, u32[]{:S(2)}) copy-start(f32[8,2,64,768]{3,2,0,1:T(8,128)} %get-tuple-element.156) | copy-start | bytes 9437188
  161.4 1.8 copy-start.5
  163.2 4.3 %collective-permute-start.33 = (f32[4,1,64]{2,0,1:T(4,128)S(1)}, f32[4,1,64]{2,0,1:T(4,128)S(1)}, u32[]{:S(2)}, u32[]{:S(2)}) collective-permute-start(f32[4,1,64]{2,0,1:T(4,128)S(1)} %bitcast.166), channel_id=1, source_target_pairs={{0,1},{1,0},{2,3},{3,2},{4,5},{5,4},{6,7},{7,6},{8,9},{9,8},{10,11... | collective-permute-start | bytes 3080 | tf_op jit(solution)/shard_map/ppermute | solution.py:30
  164.0 12.4 %collective-permute-start.26 = (bf16[1,256,768]{2,1,0:T(8,128)(2,1)}, bf16[1,256,768]{2,1,0:T(8,128)(2,1)}, u32[]{:S(2)}, u32[]{:S(2)}) collective-permute-start(bf16[1,256,768]{2,1,0:T(8,128)(2,1)} %bitcast.30), channel_id=1, source_target_pairs={{0,16},{8,24},{16,0},{24,8},{1,17},{9,25},{17,1},{25,9},{2,18},{10... | collective-permute-start | bytes 1179656 | tf_op jit(solution)/shard_map/ppermute | solution.py:30
  164.6 13.1 %copy-start.1 = (bf16[1024,768]{1,0:T(8,128)(2,1)S(1)}, bf16[1024,768]{1,0:T(8,128)(2,1)}, u32[]{:S(2)}) copy-start(bf16[1024,768]{1,0:T(8,128)(2,1)} %copy-done) | copy-start | bytes 4718596
  165.9 17.3 %collective-permute-start.29 = (bf16[1,256,768]{2,1,0:T(8,128)(2,1)S(1)}, bf16[1,256,768]{2,1,0:T(8,128)(2,1)S(1)}, u32[]{:S(2)}, u32[]{:S(2)}) collective-permute-start(bf16[1,256,768]{2,1,0:T(8,128)(2,1)S(1)} %bitcast.140), channel_id=1, source_target_pairs={{0,16},{8,24},{16,0},{24,8},{1,17},{9,25},{17,1},{25,9},{2,18},{10... | collective-permute-start | bytes 1179656 | tf_op jit(solution)/shard_map/ppermute | solution.py:30
  167.6 12.2 %collective-permute-start.34 = (f32[1,4,64]{2,1,0:T(4,128)S(1)}, f32[1,4,64]{2,1,0:T(4,128)S(1)}, u32[]{:S(2)}, u32[]{:S(2)}) collective-permute-start(f32[1,4,64]{2,1,0:T(4,128)S(1)} %get-tuple-element.188), channel_id=1, source_target_pairs={{0,4},{1,5},{2,6},{3,7},{4,0},{5,1},{6,2},{7,3},{8,12},{9,13},{10,... | collective-permute-start | bytes 3080 | tf_op jit(solution)/shard_map/ppermute | solution.py:30
  177.7 1.6 copy-start.4
  177.7 1.6 copy-start.18
  178.7 12.0 %collective-permute-start.31 = (bf16[1,256,768]{2,1,0:T(8,128)(2,1)S(1)}, bf16[1,256,768]{2,1,0:T(8,128)(2,1)S(1)}, u32[]{:S(2)}, u32[]{:S(2)}) collective-permute-start(bf16[1,256,768]{2,1,0:T(8,128)(2,1)S(1)} %bitcast.142), channel_id=1, source_target_pairs={{0,16},{8,24},{16,0},{24,8},{1,17},{9,25},{17,1},{25,9},{2,18},{10... | collective-permute-start | bytes 1179656 | tf_op jit(solution)/shard_map/ppermute | solution.py:30
  179.7 14.4 %collective-permute-start.27 = (f32[192,1024]{1,0:T(8,128)S(1)}, f32[192,1024]{1,0:T(8,128)S(1)}, u32[]{:S(2)}, u32[]{:S(2)}) collective-permute-start(f32[192,1024]{1,0:T(8,128)S(1)} %slice.101), channel_id=1, source_target_pairs={{0,8},{8,0},{16,24},{24,16},{1,9},{9,1},{17,25},{25,17},{2,10},{10... | collective-permute-start | bytes 2359304 | tf_op jit(solution)/shard_map/ppermute | solution.py:30
  179.8 14.5 %collective-permute-start.28 = (f32[192,1024]{1,0:T(8,128)S(1)}, f32[192,1024]{1,0:T(8,128)S(1)}, u32[]{:S(2)}, u32[]{:S(2)}) collective-permute-start(f32[192,1024]{1,0:T(8,128)S(1)} %slice.105), channel_id=1, source_target_pairs={{0,8},{8,0},{16,24},{24,16},{1,9},{9,1},{17,25},{25,17},{2,10},{10... | collective-permute-start | bytes 2359304 | tf_op jit(solution)/shard_map/ppermute | solution.py:30
  183.3 10.8 %copy-start.16 = (f32[384,1024]{1,0:T(8,128)S(1)}, f32[384,1024]{1,0:T(8,128)}, u32[]{:S(2)}) copy-start(f32[384,1024]{1,0:T(8,128)} %convert_add_fusion.1) | copy-start | bytes 4718596
  184.3 12.1 %collective-permute-start.32 = (bf16[1,256,768]{2,1,0:T(8,128)(2,1)S(1)}, bf16[1,256,768]{2,1,0:T(8,128)(2,1)S(1)}, u32[]{:S(2)}, u32[]{:S(2)}) collective-permute-start(bf16[1,256,768]{2,1,0:T(8,128)(2,1)S(1)} %bitcast.141), channel_id=1, source_target_pairs={{0,16},{8,24},{16,0},{24,8},{1,17},{9,25},{17,1},{25,9},{2,18},{10... | collective-permute-start | bytes 1179656 | tf_op jit(solution)/shard_map/ppermute | solution.py:30
  190.8 7.0 %collective-permute-start.35 = (f32[2,2,64]{2,1,0:T(2,128)S(1)}, f32[2,2,64]{2,1,0:T(2,128)S(1)}, u32[]{:S(2)}, u32[]{:S(2)}) collective-permute-start(f32[2,2,64]{2,1,0:T(2,128)S(1)} %get-tuple-element.186), channel_id=1, source_target_pairs={{0,2},{1,3},{2,0},{3,1},{4,6},{5,7},{6,4},{7,5},{8,10},{9,11},{10,... | collective-permute-start | bytes 3080 | tf_op jit(solution)/shard_map/ppermute | solution.py:30

commit v5 on v4

--- a/solution.py
+++ b/solution.py
@@ -428,7 +428,7 @@
             for c in range(2):
                 down_blocks.append(jnp.where(core == c, mine[:, span], other[:, span]))
     down_share = jnp.concatenate(down_blocks, axis=1)
-    returned = exchange(after(returned, up_parts[per]), "expert", far_bits)[order]
+    returned = exchange(after(returned, up_terms[per][1]), "expert", far_bits)[order]
     position_own = slot_positions(table_own, capacity)
     chosen_own = (
         lax.broadcasted_iota(jnp.int32, (owners, capacity, tok_count), 1) == position_own[:, None, :]

time: 200 us -> 214 us (1.070)
  local copies, waits for them, and re-layouts: 27.6 us -> 33.8 us
  waiting for transfers between devices: 81 us -> 86 us
  other arithmetic: 20.7 us -> 25.1 us
    ppermute x36, waiting for transfers between devices: 81 us -> 86 us  [swap(): return lax.ppermute(value, axis, [(i, i ^ bit) for i in range(size)])]
    unnamed x51 -> x87, local copies, waits for them, and re-layouts: 8.74 us -> 13 us
    select_n x2, other arithmetic: 0.37 us -> 2.79 us  [per_device(): down_blocks.append(jnp.where(core == c, mine[:, span], other[:, span]))]
  transfers between devices with their start and end apart: 36 -> 36, of which waited for: 15 -> 15; matrix products, arithmetic and copies ran while one was open for 18% -> 19% of each run, Pallas kernels for 11% -> 10%
where the time goes in v5:
time: 214 us; the launch traced here: 213 us
  waiting for transfers between devices  86 us (40%)
  starting transfers between devices  41.9 us (20%)
  local copies, waits for them, and re-layouts  33.8 us (16%)
  other arithmetic  25.1 us (12%)
  Pallas kernels  25.1 us (12%)
    ppermute x36, waiting for transfers between devices, swap(): return lax.ppermute(value, axis, [(i, i ^ bit) for i in range(size)])  86 us
    ppermute x36, starting transfers between devices, swap(): return lax.ppermute(value, axis, [(i, i ^ bit) for i in range(size)])  41.9 us
    unnamed x87, local copies, waits for them, and re-layouts  13 us
    pallas_call x6, Pallas kernels, place(): pl.pallas_call(functools.partial(place_kernel, blocks, peers, capacity),...  10.4 us
    pallas_call x4, Pallas kernels, up_step(): pl.pallas_call(functools.partial(up_kernel, len(pieces)), grid=(pairs,),...  4.85 us
    pallas_call x2, Pallas kernels, back_step(): pl.pallas_call(functools.partial(back_kernel, len(pieces)), grid_spec=plt...  4.75 us
  transfers between devices with their start and end apart: 36, of which 15 were waited for; matrix products, arithmetic and copies ran while one was open for 19% of the time, Pallas kernels for 10%

profile of v5, /device:TPU:0, one launch (start us, length us, event | category | flops | bytes accessed | tf_op | source)
XLA Modules:
  0.0 213.3 jit_solution(9494473892324264171)
XLA Ops:
  0.7 1.3 constant_dynamic-slice_fusion.7
  2.8 1.3 collective-permute-done.1
  5.2 2.9 %collective-permute-start.2 = (f32[2,8,128]{2,1,0:T(8,128)S(1)}, f32[2,8,128]{2,1,0:T(8,128)S(1)}, u32[]{:S(2)}, u32[]{:S(2)}) collective-permute-start(f32[2,8,128]{2,1,0:T(8,128)S(1)} %pad_maximum_fusion.11), channel_id=1, source_target_pairs={{0,1},{1,0},{2,3},{3,2},{4,5},{5,4},{6,7},{7,6},{8,9},{9,8},{10,11... | collective-permute-start | bytes 24584 | tf_op jit(solution)/shard_map/ppermute | solution.py:30
  8.1 1.6 collective-permute-done.2
  9.7 2.0 collective-permute-start.3
  11.8 2.6 %collective-permute-start.4 = (bf16[256,1024]{1,0:T(8,128)(2,1)}, bf16[256,1024]{1,0:T(8,128)(2,1)}, u32[]{:S(2)}, u32[]{:S(2)}) collective-permute-start(bf16[256,1024]{1,0:T(8,128)(2,1)} %get-tuple-element.180), channel_id=1, source_target_pairs={{0,4},{1,5},{2,6},{3,7},{4,0},{5,1},{6,2},{7,3},{8,12},{9,13},{10,... | collective-permute-start | bytes 1572872 | tf_op jit(solution)/shard_map/ppermute | solution.py:30
  15.2 1.4 place.6
  16.6 1.6 collective-permute-start.5
  18.2 2.1 constant_dynamic-slice_fusion.3
  21.5 2.7 %pad_maximum_fusion.1 = bf16[2,8,64,768]{3,2,1,0:T(8,128)(2,1)} fusion(bf16[1,8,64,768]{3,2,1,0:T(8,128)(2,1)} %bitcast.148, bf16[1,8,64,768]{3,2,1,0:T(8,128)(2,1)} %bitcast.149), kind=kLoop, calls=%fused_computation.28 | loop fusion | flops 786432 | bytes 3145728 | tf_op jit(solution)/shard_map/stack | solution.py:345
  24.2 3.2 %gather_fusion = bf16[8,2,64,768]{3,2,1,0:T(8,128)(2,1)} fusion(bf16[2,8,64,768]{3,2,1,0:T(8,128)(2,1)} %pad_maximum_fusion.1, s32[1024]{0:T(1024)S(1)} %pad_clamp_fusion), kind=kCustom, calls=%fused_computation | custom fusion | bytes 3145760 | tf_op jit(solution)/shard_map/gather | solution.py:345
  27.4 10.0 %collective-permute-done.6.tables = f32[4,8,128]{2,1,0:T(8,128)S(1)} collective-permute-done((f32[4,8,128]{2,1,0:T(8,128)S(1)}, f32[4,8,128]{2,1,0:T(8,128)S(1)}, u32[]{:S(2)}, u32[]{:S(2)}) %collective-permute-start.6) | collective-permute-done | bytes 16416 | tf_op jit(solution)/shard_map/ppermute | solution.py:30
  37.3 2.2 %collective-permute-done.5.refs_2_ = bf16[128,2048]{1,0:T(8,128)(2,1)S(1)} collective-permute-done((bf16[128,2048]{1,0:T(8,128)(2,1)}, bf16[128,2048]{1,0:T(8,128)(2,1)S(1)}, u32[]{:S(2)}, u32[]{:S(2)}) %collective-permute-start.5) | collective-permute-done | bytes 524320 | tf_op jit(solution)/shard_map/ppermute | solution.py:30
  41.3 2.5 %collective-permute-start.8 = (bf16[128,2048]{1,0:T(8,128)(2,1)S(1)}, bf16[128,2048]{1,0:T(8,128)(2,1)S(1)}, u32[]{:S(2)}, u32[]{:S(2)}) collective-permute-start(bf16[128,2048]{1,0:T(8,128)(2,1)S(1)} %get-tuple-element.87), channel_id=1, source_target_pairs={{0,2},{1,3},{2,0},{3,1},{4,6},{5,7},{6,4},{7,5},{8,10},{9,11},{10,... | collective-permute-start | bytes 1572872 | tf_op jit(solution)/shard_map/ppermute | solution.py:30
  43.8 1.3 pad_maximum_fusion.5
  45.2 1.1 pad_maximum_fusion.8
  47.0 15.8 %collective-permute-done.7.refs_2_ = bf16[256,1024]{1,0:T(8,128)(2,1)} collective-permute-done((bf16[256,1024]{1,0:T(8,128)(2,1)}, bf16[256,1024]{1,0:T(8,128)(2,1)}, u32[]{:S(2)}, u32[]{:S(2)}) %collective-permute-start.7) | collective-permute-done | bytes 524320 | tf_op jit(solution)/shard_map/ppermute | solution.py:30
  63.6 1.4 collective-permute-start.13
  65.7 1.7 collective-permute-start.11
  68.4 2.3 %place.8 = (bf16[256,1024]{1,0:T(8,128)(2,1)S(1)}, bf16[256,1024]{1,0:T(8,128)(2,1)}) custom-call(bf16[4,128,128]{2,1,0:T(8,128)(2,1)S(1)} %get-tuple-element.95.refs_0_.refs_1_, bf16[4,128,128]{2,1,0:T(8,128)(2,1)S(1)} %get-tuple-element.95.refs_0_.refs_1_, bf16[256,1024]{1,0:T(8,128)(2,1)} %collective-permute-done.4.refs_2_, bf16[256,1024]{1,0:T(8,128)(2,1)S(1)} %copy-done.16), custom_call_target="tpu_custom_call" | custom-call | tf_op jit(solution)/shard_map/place/pallas_call | solution.py:124
  70.7 2.5 %collective-permute-start.12 = (bf16[256,1024]{1,0:T(8,128)(2,1)}, bf16[256,1024]{1,0:T(8,128)(2,1)S(1)}, u32[]{:S(2)}, u32[]{:S(2)}) collective-permute-start(bf16[256,1024]{1,0:T(8,128)(2,1)} %get-tuple-element.98), channel_id=1, source_target_pairs={{0,2},{1,3},{2,0},{3,1},{4,6},{5,7},{6,4},{7,5},{8,10},{9,11},{10,... | collective-permute-start | bytes 1572872 | tf_op jit(solution)/shard_map/ppermute | solution.py:30
  73.2 5.5 %collective-permute-done.13.refs_3_ = bf16[256,1024]{1,0:T(8,128)(2,1)} collective-permute-done((bf16[256,1024]{1,0:T(8,128)(2,1)}, bf16[256,1024]{1,0:T(8,128)(2,1)}, u32[]{:S(2)}, u32[]{:S(2)}) %collective-permute-start.13) | collective-permute-done | bytes 524320 | tf_op jit(solution)/shard_map/ppermute | solution.py:30
  78.7 2.3 %maximum_convert_fusion = f32[2,8,2,64,768]{4,3,0,1,2:T(8,128)S(1)} fusion(bf16[2,8,1,64,768]{4,3,0,1,2:T(8,128)(2,1)} %bitcast.11, bf16[2,8,1,64,768]{4,3,0,1,2:T(8,128)(2,1)} %bitcast.10), kind=kLoop, calls=%fused_computation.5 | loop fusion | flops 3145728 | bytes 9437184 | tf_op jit(solution)/shard_map/convert_element_type | solution.py:357
  81.0 4.0 %slice_bitcast_fusion = (f32[8,2,64,768]{3,2,0,1:T(8,128)}, f32[8,2,64,768]{3,2,0,1:T(8,128)}, f32[1,8,2,64,768]{4,3,0,1,2:T(8,128)S(1)}, f32[1,8,2,64,768]{4,3,1,2,0:T(8,128)S(1)}) fusion(f32[2,8,2,64,768]{4,3,0,1,2:T(8,128)S(1)} %maximum_convert_fusion), kind=kLoop, calls=%fused_computation.17 | loop fusion | bytes 18874368 | tf_op jit(solution)/shard_map/squeeze | solution.py:358
  86.2 1.5 copy-done.21
  87.7 2.1 fusion.1
  89.8 2.6 %copy.44 = bf16[768,1024]{1,0:T(8,128)(2,1)} copy(bf16[768,1024]{0,1:T(8,128)(2,1)} %bitcast.145) | data formatting | bytes 3145728 | tf_op jit(solution)/shard_map/transpose | solution.py:361
  92.4 1.5 dynamic-slice_bitcast_fusion.3
  94.1 1.2 collective-permute-done.12.refs_5_
  95.3 1.8 place.9
  97.1 1.8 down_step.2
  98.9 1.6 collective-permute-start.16
  100.5 1.5 collective-permute-start.19
  102.5 3.1 %collective-permute-start.17 = (bf16[256,1024]{1,0:T(8,128)(2,1)S(1)}, bf16[256,1024]{1,0:T(8,128)(2,1)S(1)}, u32[]{:S(2)}, u32[]{:S(2)}) collective-permute-start(bf16[256,1024]{1,0:T(8,128)(2,1)S(1)} %copy-done.8), channel_id=1, source_target_pairs={{0,4},{1,5},{2,6},{3,7},{4,0},{5,1},{6,2},{7,3},{8,12},{9,13},{10,... | collective-permute-start | bytes 1572872 | tf_op jit(solution)/shard_map/ppermute | solution.py:30
  105.6 17.1 %collective-permute-done.18.refs_5_ = bf16[256,1024]{1,0:T(8,128)(2,1)S(1)} collective-permute-done((bf16[256,1024]{1,0:T(8,128)(2,1)S(1)}, bf16[256,1024]{1,0:T(8,128)(2,1)S(1)}, u32[]{:S(2)}, u32[]{:S(2)}) %collective-permute-start.18) | collective-permute-done | bytes 524320 | tf_op jit(solution)/shard_map/ppermute | solution.py:30
  122.7 1.9 collective-permute-done.20.refs_5_
  124.6 2.6 %collective-permute-done.17.refs_6_ = bf16[256,1024]{1,0:T(8,128)(2,1)S(1)} collective-permute-done((bf16[256,1024]{1,0:T(8,128)(2,1)S(1)}, bf16[256,1024]{1,0:T(8,128)(2,1)S(1)}, u32[]{:S(2)}, u32[]{:S(2)}) %collective-permute-start.17) | collective-permute-done | bytes 524320 | tf_op jit(solution)/shard_map/ppermute | solution.py:30
  127.2 1.4 collective-permute-start.21
  128.6 2.3 %place.10 = (bf16[512,1024]{1,0:T(8,128)(2,1)S(1)}, bf16[512,1024]{1,0:T(8,128)(2,1)S(1)}) custom-call(bf16[4,128,128]{2,1,0:T(8,128)(2,1)S(1)} %get-tuple-element.115.refs_0_.refs_1_, bf16[4,128,128]{2,1,0:T(8,128)(2,1)S(1)} %get-tuple-element.115.refs_0_.refs_1_, bf16[4,128,128]{2,1,0:T(8,128)(2,1)S(1)} %get-tuple-element.116.refs_2_.refs_3_, ...), custom_call_target="tpu_custom_call" | custom-call | tf_op jit(solution)/shard_map/place/pallas_call | solution.py:124
  131.0 1.5 convert_add_fusion.1
  132.5 3.9 %collective-permute-done.21.refs_7_ = bf16[256,1024]{1,0:T(8,128)(2,1)S(1)} collective-permute-done((bf16[256,1024]{1,0:T(8,128)(2,1)S(1)}, bf16[256,1024]{1,0:T(8,128)(2,1)S(1)}, u32[]{:S(2)}, u32[]{:S(2)}) %collective-permute-start.21) | collective-permute-done | bytes 524320 | tf_op jit(solution)/shard_map/ppermute | solution.py:30
  136.4 1.8 down_step.3
  138.8 2.4 %back_step.2.refs_6_ = f32[1024,768]{1,0:T(8,128)S(1)} custom-call(s32[2]{0:T(128)S(1)} %copy-done.19, bf16[768,4096]{1,0:T(8,128)(2,1)S(1)} %bitcast.133, bf16[128,2048]{1,0:T(8,128)(2,1)S(1)} %get-tuple-element.129.refs_0_, bf16[128,2048]{1,0:T(8,128)(2,1)S(1)} %get-tuple-element.108.refs_1_, bf16[128,2048]{1,0:T(8,128)(2,1)S(1)} %collective-permute-done.5.refs_2_, ...), custom_call_target="tpu_custom_call" | custom-call | tf_op jit(solution)/shard_map/back_step/pallas_call | solution.py:199
  141.2 2.4 %back_step.3 = f32[1024,768]{1,0:T(8,128)S(1)} custom-call(s32[2]{0:T(128)S(1)} %copy-done.19, bf16[768,4096]{1,0:T(8,128)(2,1)S(1)} %bitcast.134, bf16[128,2048]{1,0:T(8,128)(2,1)S(1)} %get-tuple-element.129.refs_0_, bf16[128,2048]{1,0:T(8,128)(2,1)S(1)} %get-tuple-element.108.refs_1_, bf16[128,2048]{1,0:T(8,128)(2,1)S(1)} %collective-permute-done.5.refs_2_, ...), custom_call_target="tpu_custom_call" | custom-call | tf_op jit(solution)/shard_map/back_step/pallas_call | solution.py:199
  144.7 6.5 %collective-permute-done.23.refs_1_.refs_3_.refs_5_.refs_7_ = bf16[512,1024]{1,0:T(8,128)(2,1)S(1)} collective-permute-done((bf16[512,1024]{1,0:T(8,128)(2,1)S(1)}, bf16[512,1024]{1,0:T(8,128)(2,1)S(1)}, u32[]{:S(2)}, u32[]{:S(2)}) %collective-permute-start.23) | collective-permute-done | bytes 1048608 | tf_op jit(solution)/shard_map/ppermute | solution.py:30
  151.2 1.9 place.11
  153.1 1.7 collective-permute-start.30
  156.4 1.6 copy-done.22
  158.8 1.2 copy-done.23
  160.0 1.4 copy-done.24
  164.5 2.1 %slice.101 = f32[192,1024]{1,0:T(8,128)} slice(f32[384,1024]{1,0:T(8,128)} %convert_add_fusion.1), slice={[192:384], [0:1024]} | slice | bytes 1572864 | tf_op jit(solution)/shard_map/slice | solution.py:425
  166.7 1.2 copy-done.1
  167.9 1.4 copy-done.3
  170.9 1.5 collective-permute-start.26
  173.1 3.5 %collective-permute-start.34 = (f32[1,4,64]{2,1,0:T(4,128)S(1)}, f32[1,4,64]{2,1,0:T(4,128)S(1)}, u32[]{:S(2)}, u32[]{:S(2)}) collective-permute-start(f32[1,4,64]{2,1,0:T(4,128)S(1)} %get-tuple-element.188), channel_id=1, source_target_pairs={{0,4},{1,5},{2,6},{3,7},{4,0},{5,1},{6,2},{7,3},{8,12},{9,13},{10,... | collective-permute-start | bytes 3080 | tf_op jit(solution)/shard_map/ppermute | solution.py:30
  178.2 7.1 %collective-permute-done.26 = bf16[1,256,768]{2,1,0:T(8,128)(2,1)S(1)} collective-permute-done((bf16[1,256,768]{2,1,0:T(8,128)(2,1)S(1)}, bf16[1,256,768]{2,1,0:T(8,128)(2,1)S(1)}, u32[]{:S(2)}, u32[]{:S(2)}) %collective-permute-start.26) | collective-permute-done | bytes 393248 | tf_op jit(solution)/shard_map/ppermute | solution.py:30
  186.6 1.8 up_step.6
  188.4 2.3 %collective-permute-start.35 = (f32[2,2,64]{2,1,0:T(2,128)S(1)}, f32[2,2,64]{2,1,0:T(2,128)S(1)}, u32[]{:S(2)}, u32[]{:S(2)}) collective-permute-start(f32[2,2,64]{2,1,0:T(2,128)S(1)} %get-tuple-element.186), channel_id=1, source_target_pairs={{0,2},{1,3},{2,0},{3,1},{4,6},{5,7},{6,4},{7,5},{8,10},{9,11},{10,... | collective-permute-start | bytes 3080 | tf_op jit(solution)/shard_map/ppermute | solution.py:30
  193.9 1.5 collective-permute-start.32
  197.0 1.5 slice_select_fusion.3
  198.6 1.3 slice_select_fusion.1
  199.8 2.0 maximum_bitcast_fusion
  201.8 9.1 %collective-permute-done.32 = bf16[1,256,768]{2,1,0:T(8,128)(2,1)S(1)} collective-permute-done((bf16[1,256,768]{2,1,0:T(8,128)(2,1)S(1)}, bf16[1,256,768]{2,1,0:T(8,128)(2,1)S(1)}, u32[]{:S(2)}, u32[]{:S(2)}) %collective-permute-start.32) | collective-permute-done | bytes 393248 | tf_op jit(solution)/shard_map/ppermute | solution.py:30
  212.1 1.2 pad_maximum_fusion.3
  (171 shorter events, 29.4 us)
Async XLA Ops:
  2.0 2.1 collective-permute-start
  2.7 11.8 %copy-start.31 = (f32[8,128]{1,0:T(8,128)}, f32[8,128]{1,0:T(8,128)S(1)}, u32[]{:S(2)}) copy-start(f32[8,128]{1,0:T(8,128)S(1)} %fusion.15) | copy-start | bytes 12292
  2.7 1.4 collective-permute-start.1
  5.2 4.5 %collective-permute-start.2 = (f32[2,8,128]{2,1,0:T(8,128)S(1)}, f32[2,8,128]{2,1,0:T(8,128)S(1)}, u32[]{:S(2)}, u32[]{:S(2)}) collective-permute-start(f32[2,8,128]{2,1,0:T(8,128)S(1)} %pad_maximum_fusion.11), channel_id=1, source_target_pairs={{0,1},{1,0},{2,3},{3,2},{4,5},{5,4},{6,7},{7,6},{8,9},{9,8},{10,11... | collective-permute-start | bytes 24584 | tf_op jit(solution)/shard_map/ppermute | solution.py:30
  9.7 29.8 %collective-permute-start.3 = (bf16[256,2048]{1,0:T(8,128)(2,1)S(1)}, bf16[256,2048]{1,0:T(8,128)(2,1)S(1)}, u32[]{:S(2)}, u32[]{:S(2)}) collective-permute-start(bf16[256,2048]{1,0:T(8,128)(2,1)S(1)} %pad_maximum_fusion.4.refs_1_), channel_id=1, source_target_pairs={{0,1},{1,0},{2,3},{3,2},{4,5},{5,4},{6,7},{7,6},{8,9},{9,8},{10,11... | collective-permute-start | bytes 3145736 | tf_op jit(solution)/shard_map/ppermute | solution.py:30
  11.8 3.4 %copy-start.17 = (s32[2]{0:T(128)}, s32[2]{0:T(128)S(1)}, u32[]{:S(2)}) copy-start(s32[2]{0:T(128)S(1)} %pad_add_fusion.where) | copy-start | bytes 28
  11.8 25.5 %collective-permute-start.4 = (bf16[256,1024]{1,0:T(8,128)(2,1)}, bf16[256,1024]{1,0:T(8,128)(2,1)}, u32[]{:S(2)}, u32[]{:S(2)}) collective-permute-start(bf16[256,1024]{1,0:T(8,128)(2,1)} %get-tuple-element.180), channel_id=1, source_target_pairs={{0,4},{1,5},{2,6},{3,7},{4,0},{5,1},{6,2},{7,3},{8,12},{9,13},{10,... | collective-permute-start | bytes 1572872 | tf_op jit(solution)/shard_map/ppermute | solution.py:30
  16.6 22.9 %collective-permute-start.5 = (bf16[128,2048]{1,0:T(8,128)(2,1)}, bf16[128,2048]{1,0:T(8,128)(2,1)S(1)}, u32[]{:S(2)}, u32[]{:S(2)}) collective-permute-start(bf16[128,2048]{1,0:T(8,128)(2,1)} %get-tuple-element.83), channel_id=1, source_target_pairs={{0,2},{1,3},{2,0},{3,1},{4,6},{5,7},{6,4},{7,5},{8,10},{9,11},{10,... | collective-permute-start | bytes 1572872 | tf_op jit(solution)/shard_map/ppermute | solution.py:30
  21.1 22.7 %collective-permute-start.10 = (bf16[128,2048]{1,0:T(8,128)(2,1)}, bf16[128,2048]{1,0:T(8,128)(2,1)}, u32[]{:S(2)}, u32[]{:S(2)}) collective-permute-start(bf16[128,2048]{1,0:T(8,128)(2,1)} %pad_maximum_fusion.7), channel_id=1, source_target_pairs={{0,8},{8,0},{16,24},{24,16},{1,9},{9,1},{17,25},{25,17},{2,10},{10... | collective-permute-start | bytes 1572872 | tf_op jit(solution)/shard_map/ppermute | solution.py:30
  21.1 6.3 %copy-start.35 = (s32[1024]{0:T(1024)}, s32[1024]{0:T(1024)S(1)}, u32[]{:S(2)}) copy-start(s32[1024]{0:T(1024)S(1)} %pad_clamp_fusion) | copy-start | bytes 12292
  21.1 16.2 %collective-permute-start.6 = (f32[4,8,128]{2,1,0:T(8,128)S(1)}, f32[4,8,128]{2,1,0:T(8,128)S(1)}, u32[]{:S(2)}, u32[]{:S(2)}) collective-permute-start(f32[4,8,128]{2,1,0:T(8,128)S(1)} %pad_maximum_fusion.10.tables), channel_id=1, source_target_pairs={{0,4},{1,5},{2,6},{3,7},{4,0},{5,1},{6,2},{7,3},{8,12},{9,13},{10,... | collective-permute-start | bytes 49160 | tf_op jit(solution)/shard_map/ppermute | solution.py:30
  39.5 23.3 %collective-permute-start.7 = (bf16[256,1024]{1,0:T(8,128)(2,1)}, bf16[256,1024]{1,0:T(8,128)(2,1)}, u32[]{:S(2)}, u32[]{:S(2)}) collective-permute-start(bf16[256,1024]{1,0:T(8,128)(2,1)} %get-tuple-element.84), channel_id=1, source_target_pairs={{0,4},{1,5},{2,6},{3,7},{4,0},{5,1},{6,2},{7,3},{8,12},{9,13},{10,... | collective-permute-start | bytes 1572872 | tf_op jit(solution)/shard_map/ppermute | solution.py:30
  40.1 22.7 %collective-permute-start.9 = (bf16[256,1024]{1,0:T(8,128)(2,1)}, bf16[256,1024]{1,0:T(8,128)(2,1)S(1)}, u32[]{:S(2)}, u32[]{:S(2)}) collective-permute-start(bf16[256,1024]{1,0:T(8,128)(2,1)} %collective-permute-done.4.refs_2_), channel_id=1, source_target_pairs={{0,1},{1,0},{2,3},{3,2},{4,5},{5,4},{6,7},{7,6},{8,9},{9,8},{10,11... | collective-permute-start | bytes 1572872 | tf_op jit(solution)/shard_map/ppermute | solution.py:30
  41.3 22.3 %collective-permute-start.8 = (bf16[128,2048]{1,0:T(8,128)(2,1)S(1)}, bf16[128,2048]{1,0:T(8,128)(2,1)S(1)}, u32[]{:S(2)}, u32[]{:S(2)}) collective-permute-start(bf16[128,2048]{1,0:T(8,128)(2,1)S(1)} %get-tuple-element.87), channel_id=1, source_target_pairs={{0,2},{1,3},{2,0},{3,1},{4,6},{5,7},{6,4},{7,5},{8,10},{9,11},{10,... | collective-permute-start | bytes 1572872 | tf_op jit(solution)/shard_map/ppermute | solution.py:30
  63.6 15.0 %collective-permute-start.15 = (bf16[2,8,64,768]{3,2,0,1:T(8,128)(2,1)}, bf16[2,8,64,768]{3,2,0,1:T(8,128)(2,1)}, u32[]{:S(2)}, u32[]{:S(2)}) collective-permute-start(bf16[2,8,64,768]{3,2,0,1:T(8,128)(2,1)} %bitcast.9), channel_id=1, source_target_pairs={{0,8},{8,0},{16,24},{24,16},{1,9},{9,1},{17,25},{25,17},{2,10},{10... | collective-permute-start | bytes 4718600 | tf_op jit(solution)/shard_map/ppermute | solution.py:30
  63.6 15.0 %collective-permute-start.13 = (bf16[256,1024]{1,0:T(8,128)(2,1)}, bf16[256,1024]{1,0:T(8,128)(2,1)}, u32[]{:S(2)}, u32[]{:S(2)}) collective-permute-start(bf16[256,1024]{1,0:T(8,128)(2,1)} %collective-permute-done.7.refs_2_), channel_id=1, source_target_pairs={{0,1},{1,0},{2,3},{3,2},{4,5},{5,4},{6,7},{7,6},{8,9},{9,8},{10,11... | collective-permute-start | bytes 1572872 | tf_op jit(solution)/shard_map/ppermute | solution.py:30
  65.0 30.2 %collective-permute-start.14 = (bf16[256,1024]{1,0:T(8,128)(2,1)}, bf16[256,1024]{1,0:T(8,128)(2,1)}, u32[]{:S(2)}, u32[]{:S(2)}) collective-permute-start(bf16[256,1024]{1,0:T(8,128)(2,1)} %get-tuple-element.117.refs_4_), channel_id=1, source_target_pairs={{0,1},{1,0},{2,3},{3,2},{4,5},{5,4},{6,7},{7,6},{8,9},{9,8},{10,11... | collective-permute-start | bytes 1572872 | tf_op jit(solution)/shard_map/ppermute | solution.py:30
  65.7 29.6 %collective-permute-start.11 = (bf16[256,1024]{1,0:T(8,128)(2,1)}, bf16[256,1024]{1,0:T(8,128)(2,1)}, u32[]{:S(2)}, u32[]{:S(2)}) collective-permute-start(bf16[256,1024]{1,0:T(8,128)(2,1)} %get-tuple-element.117.refs_4_), channel_id=1, source_target_pairs={{0,4},{1,5},{2,6},{3,7},{4,0},{5,1},{6,2},{7,3},{8,12},{9,13},{10,... | collective-permute-start | bytes 1572872 | tf_op jit(solution)/shard_map/ppermute | solution.py:30
  70.7 26.4 %copy-start.4 = (bf16[256,1024]{1,0:T(8,128)(2,1)}, bf16[256,1024]{1,0:T(8,128)(2,1)S(1)}, u32[]{:S(2)}) copy-start(bf16[256,1024]{1,0:T(8,128)(2,1)S(1)} %get-tuple-element.111.refs_4_) | copy-start | bytes 1572868
  70.7 24.6 %collective-permute-start.12 = (bf16[256,1024]{1,0:T(8,128)(2,1)}, bf16[256,1024]{1,0:T(8,128)(2,1)S(1)}, u32[]{:S(2)}, u32[]{:S(2)}) collective-permute-start(bf16[256,1024]{1,0:T(8,128)(2,1)} %get-tuple-element.98), channel_id=1, source_target_pairs={{0,2},{1,3},{2,0},{3,1},{4,6},{5,7},{6,4},{7,5},{8,10},{9,11},{10,... | collective-permute-start | bytes 1572872 | tf_op jit(solution)/shard_map/ppermute | solution.py:30
  81.0 4.6 %copy-start.20 = (f32[2,8,2,64,768]{4,3,0,1,2:T(8,128)}, f32[2,8,2,64,768]{4,3,0,1,2:T(8,128)S(1)}, u32[]{:S(2)}) copy-start(f32[2,8,2,64,768]{4,3,0,1,2:T(8,128)S(1)} %maximum_convert_fusion) | copy-start | bytes 18874372
  94.0 7.9 %copy-start.8 = (bf16[256,1024]{1,0:T(8,128)(2,1)S(1)}, bf16[256,1024]{1,0:T(8,128)(2,1)}, u32[]{:S(2)}) copy-start(bf16[256,1024]{1,0:T(8,128)(2,1)} %get-tuple-element.120.refs_4_) | copy-start | bytes 1572868
  95.2 33.3 %copy-start.6 = (bf16[256,1024]{1,0:T(8,128)(2,1)}, bf16[256,1024]{1,0:T(8,128)(2,1)S(1)}, u32[]{:S(2)}) copy-start(bf16[256,1024]{1,0:T(8,128)(2,1)S(1)} %collective-permute-done.12.refs_5_) | copy-start | bytes 1572868
  97.1 41.7 %slice-start = ((s8[6291456]{0:T(1024)(128)(4,1)}), s8[4194304]{0:T(1024)(128)(4,1)S(1)}, s32[]{:S(2)}) async-start(s8[6291456]{0:T(1024)(128)(4,1)} %bitcast.131), calls=%async_computation | async-start | bytes 8388608
  98.9 32.1 %collective-permute-start.16 = (bf16[1,384,1024]{2,1,0:T(8,128)(2,1)S(1)}, bf16[1,384,1024]{2,1,0:T(8,128)(2,1)S(1)}, u32[]{:S(2)}, u32[]{:S(2)}) collective-permute-start(bf16[1,384,1024]{2,1,0:T(8,128)(2,1)S(1)} %bitcast.137), channel_id=1, source_target_pairs={{0,16},{8,24},{16,0},{24,8},{1,17},{9,25},{17,1},{25,9},{2,18},{10... | collective-permute-start | bytes 2359304 | tf_op jit(solution)/shard_map/ppermute | solution.py:30
  100.5 22.2 %collective-permute-start.18 = (bf16[256,1024]{1,0:T(8,128)(2,1)S(1)}, bf16[256,1024]{1,0:T(8,128)(2,1)S(1)}, u32[]{:S(2)}, u32[]{:S(2)}) collective-permute-start(bf16[256,1024]{1,0:T(8,128)(2,1)S(1)} %get-tuple-element.121), channel_id=1, source_target_pairs={{0,2},{1,3},{2,0},{3,1},{4,6},{5,7},{6,4},{7,5},{8,10},{9,11},{10,... | collective-permute-start | bytes 1572872 | tf_op jit(solution)/shard_map/ppermute | solution.py:30
  100.5 22.2 %collective-permute-start.19 = (bf16[256,1024]{1,0:T(8,128)(2,1)}, bf16[256,1024]{1,0:T(8,128)(2,1)S(1)}, u32[]{:S(2)}, u32[]{:S(2)}) collective-permute-start(bf16[256,1024]{1,0:T(8,128)(2,1)} %collective-permute-done.11.refs_6_), channel_id=1, source_target_pairs={{0,1},{1,0},{2,3},{3,2},{4,5},{5,4},{6,7},{7,6},{8,9},{9,8},{10,11... | collective-permute-start | bytes 1572872 | tf_op jit(solution)/shard_map/ppermute | solution.py:30
  102.0 22.6 %collective-permute-start.20 = (bf16[256,1024]{1,0:T(8,128)(2,1)S(1)}, bf16[256,1024]{1,0:T(8,128)(2,1)S(1)}, u32[]{:S(2)}, u32[]{:S(2)}) collective-permute-start(bf16[256,1024]{1,0:T(8,128)(2,1)S(1)} %copy-done.8), channel_id=1, source_target_pairs={{0,1},{1,0},{2,3},{3,2},{4,5},{5,4},{6,7},{7,6},{8,9},{9,8},{10,11... | collective-permute-start | bytes 1572872 | tf_op jit(solution)/shard_map/ppermute | solution.py:30
  102.5 24.6 %collective-permute-start.17 = (bf16[256,1024]{1,0:T(8,128)(2,1)S(1)}, bf16[256,1024]{1,0:T(8,128)(2,1)S(1)}, u32[]{:S(2)}, u32[]{:S(2)}) collective-permute-start(bf16[256,1024]{1,0:T(8,128)(2,1)S(1)} %copy-done.8), channel_id=1, source_target_pairs={{0,4},{1,5},{2,6},{3,7},{4,0},{5,1},{6,2},{7,3},{8,12},{9,13},{10,... | collective-permute-start | bytes 1572872 | tf_op jit(solution)/shard_map/ppermute | solution.py:30
  127.2 9.2 %collective-permute-start.21 = (bf16[256,1024]{1,0:T(8,128)(2,1)S(1)}, bf16[256,1024]{1,0:T(8,128)(2,1)S(1)}, u32[]{:S(2)}, u32[]{:S(2)}) collective-permute-start(bf16[256,1024]{1,0:T(8,128)(2,1)S(1)} %collective-permute-done.17.refs_6_), channel_id=1, source_target_pairs={{0,1},{1,0},{2,3},{3,2},{4,5},{5,4},{6,7},{7,6},{8,9},{9,8},{10,11... | collective-permute-start | bytes 1572872 | tf_op jit(solution)/shard_map/ppermute | solution.py:30
  130.9 7.9 %slice-start.1 = ((s8[6291456]{0:T(1024)(128)(4,1)}), s8[2097152]{0:T(1024)(128)(4,1)S(1)}, s32[]{:S(2)}) async-start(s8[6291456]{0:T(1024)(128)(4,1)} %bitcast.131), calls=%async_computation.1 | async-start | bytes 4194304
  130.9 20.3 %collective-permute-start.23 = (bf16[512,1024]{1,0:T(8,128)(2,1)S(1)}, bf16[512,1024]{1,0:T(8,128)(2,1)S(1)}, u32[]{:S(2)}, u32[]{:S(2)}) collective-permute-start(bf16[512,1024]{1,0:T(8,128)(2,1)S(1)} %get-tuple-element.131), channel_id=1, source_target_pairs={{0,2},{1,3},{2,0},{3,1},{4,6},{5,7},{6,4},{7,5},{8,10},{9,11},{10,... | collective-permute-start | bytes 3145736 | tf_op jit(solution)/shard_map/ppermute | solution.py:30
  132.5 6.3 %copy-start.5 = (bf16[256,1024]{1,0:T(8,128)(2,1)S(1)}, bf16[256,1024]{1,0:T(8,128)(2,1)}, u32[]{:S(2)}) copy-start(bf16[256,1024]{1,0:T(8,128)(2,1)} %copy-done.4) | copy-start | bytes 1572868
  132.5 6.3 %copy-start.7 = (bf16[256,1024]{1,0:T(8,128)(2,1)S(1)}, bf16[256,1024]{1,0:T(8,128)(2,1)}, u32[]{:S(2)}) copy-start(bf16[256,1024]{1,0:T(8,128)(2,1)} %copy-done.6) | copy-start | bytes 1572868
  132.5 6.3 %copy-start.19 = (s32[2]{0:T(128)S(1)}, s32[2]{0:T(128)}, u32[]{:S(2)}) copy-start(s32[2]{0:T(128)} %copy-done.17) | copy-start | bytes 28
  138.2 3.0 %copy-start.9 = (f32[384,1024]{1,0:T(8,128)}, f32[384,1024]{1,0:T(8,128)S(1)}, u32[]{:S(2)}) copy-start(f32[384,1024]{1,0:T(8,128)S(1)} %get-tuple-element.128) | copy-start | bytes 4718596
  138.2 16.7 %collective-permute-start.24 = (bf16[1,384,1024]{2,1,0:T(8,128)(2,1)S(1)}, bf16[1,384,1024]{2,1,0:T(8,128)(2,1)S(1)}, u32[]{:S(2)}, u32[]{:S(2)}) collective-permute-start(bf16[1,384,1024]{2,1,0:T(8,128)(2,1)S(1)} %bitcast.138), channel_id=1, source_target_pairs={{0,16},{8,24},{16,0},{24,8},{1,17},{9,25},{17,1},{25,9},{2,18},{10... | collective-permute-start | bytes 2359304 | tf_op jit(solution)/shard_map/ppermute | solution.py:30
  138.8 5.5 %slice-start.2 = ((s8[6291456]{0:T(1024)(128)(4,1)}), s8[4194304]{0:T(1024)(128)(4,1)S(1)}, s32[]{:S(2)}) async-start(s8[6291456]{0:T(1024)(128)(4,1)} %bitcast.142), calls=%async_computation.2 | async-start | bytes 8388608
  141.2 3.2 %slice-start.3 = ((s8[6291456]{0:T(1024)(128)(4,1)}), s8[2097152]{0:T(1024)(128)(4,1)S(1)}, s32[]{:S(2)}) async-start(s8[6291456]{0:T(1024)(128)(4,1)} %bitcast.142), calls=%async_computation.3 | async-start | bytes 4194304
  143.7 11.2 %collective-permute-start.22 = (bf16[8,64,768]{2,1,0:T(8,128)(2,1)S(1)}, bf16[8,64,768]{2,1,0:T(8,128)(2,1)S(1)}, u32[]{:S(2)}, u32[]{:S(2)}) collective-permute-start(bf16[8,64,768]{2,1,0:T(8,128)(2,1)S(1)} %get-tuple-element.161), channel_id=1, source_target_pairs={{0,8},{8,0},{16,24},{24,16},{1,9},{9,1},{17,25},{25,17},{2,10},{10... | collective-permute-start | bytes 2359304 | tf_op jit(solution)/shard_map/ppermute | solution.py:30
  143.8 11.1 %collective-permute-start.25 = (bf16[8,64,768]{2,1,0:T(8,128)(2,1)S(1)}, bf16[8,64,768]{2,1,0:T(8,128)(2,1)S(1)}, u32[]{:S(2)}, u32[]{:S(2)}) collective-permute-start(bf16[8,64,768]{2,1,0:T(8,128)(2,1)S(1)} %get-tuple-element.162), channel_id=1, source_target_pairs={{0,8},{8,0},{16,24},{24,16},{1,9},{9,1},{17,25},{25,17},{2,10},{10... | collective-permute-start | bytes 2359304 | tf_op jit(solution)/shard_map/ppermute | solution.py:30
  151.2 10.6 %copy-start = (bf16[512,1024]{1,0:T(8,128)(2,1)}, bf16[512,1024]{1,0:T(8,128)(2,1)S(1)}, u32[]{:S(2)}) copy-start(bf16[512,1024]{1,0:T(8,128)(2,1)S(1)} %collective-permute-done.23.refs_1_.refs_3_.refs_5_.refs_7_) | copy-start | bytes 3145732
  153.1 33.5 %collective-permute-start.30 = (bf16[512,1024]{1,0:T(8,128)(2,1)}, bf16[512,1024]{1,0:T(8,128)(2,1)S(1)}, u32[]{:S(2)}, u32[]{:S(2)}) collective-permute-start(bf16[512,1024]{1,0:T(8,128)(2,1)} %get-tuple-element.146), channel_id=1, source_target_pairs={{0,2},{1,3},{2,0},{3,1},{4,6},{5,7},{6,4},{7,5},{8,10},{9,11},{10,... | collective-permute-start | bytes 3145736 | tf_op jit(solution)/shard_map/ppermute | solution.py:30
  157.9 3.4 %copy-start.24 = (f32[8,2,64,768]{3,2,0,1:T(8,128)S(1)}, f32[8,2,64,768]{3,2,0,1:T(8,128)}, u32[]{:S(2)}) copy-start(f32[8,2,64,768]{3,2,0,1:T(8,128)} %get-tuple-element.156) | copy-start | bytes 9437188
  158.8 3.0 %copy-start.2 = (bf16[1024,768]{1,0:T(8,128)(2,1)}, bf16[1024,768]{1,0:T(8,128)(2,1)S(1)}, u32[]{:S(2)}) copy-start(bf16[1024,768]{1,0:T(8,128)(2,1)S(1)} %fusion.grad_pre) | copy-start | bytes 4718596
  163.8 8.7 %collective-permute-start.33 = (f32[4,1,64]{2,0,1:T(4,128)S(1)}, f32[4,1,64]{2,0,1:T(4,128)}, u32[]{:S(2)}, u32[]{:S(2)}) collective-permute-start(f32[4,1,64]{2,0,1:T(4,128)S(1)} %bitcast.163), channel_id=1, source_target_pairs={{0,1},{1,0},{2,3},{3,2},{4,5},{5,4},{6,7},{7,6},{8,9},{9,8},{10,11... | collective-permute-start | bytes 3080 | tf_op jit(solution)/shard_map/ppermute | solution.py:30
  169.3 7.3 %copy-start.10 = (f32[384,1024]{1,0:T(8,128)S(1)}, f32[384,1024]{1,0:T(8,128)}, u32[]{:S(2)}) copy-start(f32[384,1024]{1,0:T(8,128)} %copy-done.9) | copy-start | bytes 4718596
  169.3 7.3 %copy-start.30 = (bf16[1,384,1024]{2,1,0:T(8,128)(2,1)S(1)}, bf16[1,384,1024]{2,1,0:T(8,128)(2,1)}, u32[]{:S(2)}) copy-start(bf16[1,384,1024]{2,1,0:T(8,128)(2,1)} %copy-done.29) | copy-start | bytes 2359300
  170.3 20.4 %collective-permute-start.29 = (bf16[1,256,768]{2,1,0:T(8,128)(2,1)S(1)}, bf16[1,256,768]{2,1,0:T(8,128)(2,1)S(1)}, u32[]{:S(2)}, u32[]{:S(2)}) collective-permute-start(bf16[1,256,768]{2,1,0:T(8,128)(2,1)S(1)} %bitcast.139), channel_id=1, source_target_pairs={{0,16},{8,24},{16,0},{24,8},{1,17},{9,25},{17,1},{25,9},{2,18},{10... | collective-permute-start | bytes 1179656 | tf_op jit(solution)/shard_map/ppermute | solution.py:30
  170.9 14.4 %collective-permute-start.26 = (bf16[1,256,768]{2,1,0:T(8,128)(2,1)S(1)}, bf16[1,256,768]{2,1,0:T(8,128)(2,1)S(1)}, u32[]{:S(2)}, u32[]{:S(2)}) collective-permute-start(bf16[1,256,768]{2,1,0:T(8,128)(2,1)S(1)} %bitcast.141), channel_id=1, source_target_pairs={{0,16},{8,24},{16,0},{24,8},{1,17},{9,25},{17,1},{25,9},{2,18},{10... | collective-permute-start | bytes 1179656 | tf_op jit(solution)/shard_map/ppermute | solution.py:30
  173.1 5.0 %collective-permute-start.34 = (f32[1,4,64]{2,1,0:T(4,128)S(1)}, f32[1,4,64]{2,1,0:T(4,128)S(1)}, u32[]{:S(2)}, u32[]{:S(2)}) collective-permute-start(f32[1,4,64]{2,1,0:T(4,128)S(1)} %get-tuple-element.188), channel_id=1, source_target_pairs={{0,4},{1,5},{2,6},{3,7},{4,0},{5,1},{6,2},{7,3},{8,12},{9,13},{10,... | collective-permute-start | bytes 3080 | tf_op jit(solution)/shard_map/ppermute | solution.py:30
  176.8 9.8 %copy-start.25 = (f32[384,1024]{1,0:T(8,128)}, f32[384,1024]{1,0:T(8,128)S(1)}, u32[]{:S(2)}) copy-start(f32[384,1024]{1,0:T(8,128)S(1)} %convert_add_fusion) | copy-start | bytes 4718596
  186.1 4.6 %copy-start.12 = (f32[256,768]{1,0:T(8,128)S(1)}, f32[256,768]{1,0:T(8,128)}, u32[]{:S(2)}) copy-start(f32[256,768]{1,0:T(8,128)} %copy-done.11) | copy-start | bytes 2359300
  186.1 10.9 %collective-permute-start.27 = (f32[192,1024]{1,0:T(8,128)}, f32[192,1024]{1,0:T(8,128)}, u32[]{:S(2)}, u32[]{:S(2)}) collective-permute-start(f32[192,1024]{1,0:T(8,128)} %slice.101), channel_id=1, source_target_pairs={{0,8},{8,0},{16,24},{24,16},{1,9},{9,1},{17,25},{25,17},{2,10},{10... | collective-permute-start | bytes 2359304 | tf_op jit(solution)/shard_map/ppermute | solution.py:30
  186.1 12.4 %collective-permute-start.28 = (f32[192,1024]{1,0:T(8,128)}, f32[192,1024]{1,0:T(8,128)}, u32[]{:S(2)}, u32[]{:S(2)}) collective-permute-start(f32[192,1024]{1,0:T(8,128)} %slice.105), channel_id=1, source_target_pairs={{0,8},{8,0},{16,24},{24,16},{1,9},{9,1},{17,25},{25,17},{2,10},{10... | collective-permute-start | bytes 2359304 | tf_op jit(solution)/shard_map/ppermute | solution.py:30
  188.4 7.0 %collective-permute-start.35 = (f32[2,2,64]{2,1,0:T(2,128)S(1)}, f32[2,2,64]{2,1,0:T(2,128)S(1)}, u32[]{:S(2)}, u32[]{:S(2)}) collective-permute-start(f32[2,2,64]{2,1,0:T(2,128)S(1)} %get-tuple-element.186), channel_id=1, source_target_pairs={{0,2},{1,3},{2,0},{3,1},{4,6},{5,7},{6,4},{7,5},{8,10},{9,11},{10,... | collective-permute-start | bytes 3080 | tf_op jit(solution)/shard_map/ppermute | solution.py:30
  191.5 4.8 %copy-start.34 = (s32[128,8]{0,1:T(8,128)S(1)}, s32[128,8]{0,1:T(8,128)}, u32[]{:S(2)}) copy-start(s32[128,8]{0,1:T(8,128)} %param.10) | copy-start | bytes 12292
  191.5 4.8 %copy-start.38 = (s32[8]{0:T(128)S(1)}, s32[8]{0:T(128)}, u32[]{:S(2)}) copy-start(s32[8]{0:T(128)} %copy-done.37) | copy-start | bytes 100
  191.5 19.5 %collective-permute-start.31 = (bf16[1,256,768]{2,1,0:T(8,128)(2,1)}, bf16[1,256,768]{2,1,0:T(8,128)(2,1)}, u32[]{:S(2)}, u32[]{:S(2)}) collective-permute-start(bf16[1,256,768]{2,1,0:T(8,128)(2,1)} %bitcast.38), channel_id=1, source_target_pairs={{0,16},{8,24},{16,0},{24,8},{1,17},{9,25},{17,1},{25,9},{2,18},{10... | collective-permute-start | bytes 1179656 | tf_op jit(solution)/shard_map/ppermute | solution.py:30
  193.9 4.6 %copy-start.26 = (f32[384,1024]{1,0:T(8,128)S(1)}, f32[384,1024]{1,0:T(8,128)}, u32[]{:S(2)}) copy-start(f32[384,1024]{1,0:T(8,128)} %copy-done.25) | copy-start | bytes 4718596
  193.9 17.0 %collective-permute-start.32 = (bf16[1,256,768]{2,1,0:T(8,128)(2,1)S(1)}, bf16[1,256,768]{2,1,0:T(8,128)(2,1)S(1)}, u32[]{:S(2)}, u32[]{:S(2)}) collective-permute-start(bf16[1,256,768]{2,1,0:T(8,128)(2,1)S(1)} %bitcast.140), channel_id=1, source_target_pairs={{0,16},{8,24},{16,0},{24,8},{1,17},{9,25},{17,1},{25,9},{2,18},{10... | collective-permute-start | bytes 1179656 | tf_op jit(solution)/shard_map/ppermute | solution.py:30
  199.8 11.1 %copy-start.14 = (f32[256,768]{1,0:T(8,128)S(1)}, f32[256,768]{1,0:T(8,128)}, u32[]{:S(2)}) copy-start(f32[256,768]{1,0:T(8,128)} %copy-done.13) | copy-start | bytes 2359300
  201.8 10.3 %copy-start.27 = (bf16[256,768]{1,0:T(8,128)(2,1)S(1)}, bf16[256,768]{1,0:T(8,128)(2,1)}, u32[]{:S(2)}) copy-start(bf16[256,768]{1,0:T(8,128)(2,1)} %convert_add_fusion.5) | copy-start | bytes 1179652
  201.8 10.3 %copy-start.28 = (bf16[256,768]{1,0:T(8,128)(2,1)S(1)}, bf16[256,768]{1,0:T(8,128)(2,1)}, u32[]{:S(2)}) copy-start(bf16[256,768]{1,0:T(8,128)(2,1)} %convert_add_fusion.4) | copy-start | bytes 1179652
  (15 other events, 23.2 us)
